TPU v7x, 32 devices: a whole 2x2x4 slice. The times are simulated.
32 devices in a mesh: tensor: 4 (over y, core), context: 8 (over z, x).
Axes of the slice: x: 2, y: 2, z: 4, core: 2. Of those that a mesh axis runs over, the one named last changes fastest.
Arguments:
- queries: bfloat16 [1024, 1024], P('tensor', 'context'), parts along dimension 0, may hold values from -6 to 6
- keys: bfloat16 [1024, 1024], P('tensor', 'context'), parts along dimension 0, may hold values from -6 to 6
- values: bfloat16 [1024, 1024], P('tensor', 'context'), parts along dimension 0, may hold values from -6 to 6
- filters: float32 [1024, 1024], P(('tensor', 'context')), parts along dimension 0, may hold values from -1 to 1
- skip: float32 [1024], P('tensor'), parts along dimension 0, may hold values from -3 to 3
Outputs:
- output: bfloat16 [1024, 1024], P('tensor', 'context'), parts along dimension 0
There are 4 independent parts, one for each index of `tensor`. A program takes and returns all parts, laid end to end along the dimension named above; each array names one. Nothing has to cross between parts.
All inputs are finite; a program needn't handle non-finite values.
Results may differ from a plain program's by a relative error of at most 0.008.
Values may be sent and summed in bfloat16 or wider, within the bound.
No kernel may reach another device: no remote copies, remote signals or barrier semaphores. Data moves between devices by JAX's collectives and lax.ppermute only.
A program may use at most 64 MiB of HBM per device.

v0:
```python
import math

import jax
import jax.numpy as jnp
from jax import lax
from jax.sharding import PartitionSpec as P

RADIX = 128


def tables(row_count, col_count, period):
    row_ids = lax.broadcasted_iota(jnp.int32, (row_count, col_count), 0)
    col_ids = lax.broadcasted_iota(jnp.int32, (row_count, col_count), 1)
    phases = (row_ids * col_ids % period).astype(jnp.float32) * (2.0 * math.pi / period)
    return (jnp.cos(phases), jnp.sin(phases))


def matmul(form, left, right):
    return jnp.einsum(
        form, left, right, precision=lax.Precision.HIGHEST, preferred_element_type=jnp.float32
    )


def forward(signal, radix_size):
    chan_count, seq_len = signal.shape
    full_len = 2 * seq_len
    section_two = full_len // radix_size
    half_radix = radix_size // 2
    blocked = signal.reshape(chan_count, half_radix, section_two)
    cos_first, sin_first = tables(radix_size, half_radix, radix_size)
    turn_cos, turn_sin = tables(radix_size, section_two, full_len)
    cos_second, sin_second = tables(section_two, section_two, section_two)
    real_part = matmul("ab,cbd->cad", cos_first, blocked)
    imag_part = -matmul("ab,cbd->cad", sin_first, blocked)
    real_part, imag_part = (
        real_part * turn_cos + imag_part * turn_sin,
        imag_part * turn_cos - real_part * turn_sin,
    )
    spec_real = matmul("cad,de->cae", real_part, cos_second) + matmul(
        "cad,de->cae", imag_part, sin_second
    )
    spec_imag = matmul("cad,de->cae", imag_part, cos_second) - matmul(
        "cad,de->cae", real_part, sin_second
    )
    return (spec_real, spec_imag)


def inverse(spec_real, spec_imag, radix_size):
    chan_count, _, section_two = spec_real.shape
    full_len = radix_size * section_two
    half_radix = radix_size // 2
    cos_second, sin_second = tables(section_two, section_two, section_two)
    turn_cos, turn_sin = tables(radix_size, section_two, full_len)
    dual_real = matmul("cad,de->cae", spec_real, cos_second) - matmul(
        "cad,de->cae", spec_imag, sin_second
    )
    dual_imag = matmul("cad,de->cae", spec_imag, cos_second) + matmul(
        "cad,de->cae", spec_real, sin_second
    )
    dual_real, dual_imag = (
        dual_real * turn_cos - dual_imag * turn_sin,
        dual_imag * turn_cos + dual_real * turn_sin,
    )
    cos_last, sin_last = tables(half_radix, radix_size, radix_size)
    result = matmul("ab,cbd->cad", cos_last, dual_real) - matmul("ab,cbd->cad", sin_last, dual_imag)
    return result.reshape(chan_count, half_radix * section_two) / full_len


def convolve(signal, filter_rows, radix_size):
    sig_real, sig_imag = forward(signal.astype(jnp.float32), radix_size)
    filt_real, filt_imag = forward(filter_rows, radix_size)
    prod_real = sig_real * filt_real - sig_imag * filt_imag
    prod_imag = sig_real * filt_imag + sig_imag * filt_real
    return inverse(prod_real, prod_imag, radix_size).astype(jnp.bfloat16)


def per_device(queries, keys, values, filters, skip):
    channels, tok_dev = keys.shape
    shards = lax.axis_size("context")
    local_ch = channels // shards
    gated_input = (keys.astype(jnp.float32) * values.astype(jnp.float32)).astype(jnp.bfloat16)
    stacked = gated_input.reshape(shards, local_ch, tok_dev)
    arrived = lax.all_to_all(stacked, "context", split_axis=0, concat_axis=2, tiled=True)
    convolved = convolve(arrived.reshape(local_ch, -1), filters, RADIX)
    returned = lax.all_to_all(
        convolved.reshape(1, local_ch, -1), "context", split_axis=2, concat_axis=0, tiled=True
    )
    conv_tokens = returned.reshape(channels, tok_dev)
    result = queries.astype(jnp.float32) * (
        conv_tokens.astype(jnp.float32) + skip[:, None] * gated_input.astype(jnp.float32)
    )
    return result.astype(jnp.bfloat16)


def solution(mesh):
    placed = (
        P("tensor", "context"),
        P("tensor", "context"),
        P("tensor", "context"),
        P(("tensor", "context"), None),
        P("tensor"),
    )
    return jax.shard_map(
        per_device, mesh=mesh, in_specs=placed, out_specs=P("tensor", "context"), check_vma=False
    )
```

profile of v0, /device:TPU:0, one launch (start us, length us, event | category | flops | bytes accessed | tf_op | source)
XLA Modules:
  0.0 37.8 jit_solution(6013519005858818282)
XLA Ops:
  0.0 0.0 copy-start
  0.0 1.6 %multiply_convert_fusion = bf16[256,128]{1,0:T(8,128)(2,1)} fusion(bf16[256,128]{1,0:T(8,128)(2,1)} %param.7, bf16[256,128]{1,0:T(8,128)(2,1)} %param.6), kind=kLoop, calls=%fused_computation.41 | loop fusion | flops 131072 | bytes 196608 | tf_op jit(solution)/shard_map/convert_element_type | solution.py:81
  1.6 7.3 %all-to-all-start = ((bf16[8,32,128]{2,1,0:T(8,128)(2,1)}), bf16[8,32,128]{2,1,0:T(8,128)(2,1)S(1)}, u32[]{:S(2)}, u32[]{:S(2)}) async-start(bf16[8,32,128]{2,1,0:T(8,128)(2,1)} %bitcast), calls=%async_computation | async-start | bytes 131072 | tf_op jit(solution)/shard_map/all_to_all | solution.py:83
  8.8 0.1 fusion.94
  8.9 0.0 copy-done
  8.9 0.2 copy.54
  9.1 0.2 copy.55
  9.3 0.5 %convolution_negate_fusion = f32[128,32,16]{0,1,2:T(8,128)S(1)} fusion(f32[32,64,16]{1,0,2:T(8,128)S(1)} %copy.55), kind=kOutput, calls=%fused_computation.8 | convolution fusion | flops 50511872 | bytes 393216 | tf_op jit(solution)/shard_map/ab,cbd->cad/dot_general | solution.py:19
  9.8 0.5 %subtract_bitcast_fusion = (f32[32,128,16]{1,0,2:T(8,128)S(1)}, f32[32,128,16]{1,0,2:T(8,128)S(1)}) fusion(f32[128,32,16]{0,1,2:T(8,128)S(1)} %convolution_negate_fusion, f32[128,16]{0,1:T(8,128)S(1)} %get-tuple-element.9, f32[128,16]{0,1:T(8,128)S(1)} %get-tuple-element.10, f32[32,64,16]{1,0,2:T(8,128)S(1)} %copy.55), kind=kOutput, calls=%fused_computation.23 | convolution fusion | flops 50839552 | bytes 933888 | tf_op jit(solution)/shard_map/ab,cbd->cad/dot_general | solution.py:19
  10.4 0.5 %fusion.15 = f32[32,128,16]{1,2,0:T(8,128)S(1)} fusion(f32[32,128,16]{1,0,2:T(8,128)S(1)} %get-tuple-element.8), kind=kOutput, calls=%fused_computation.31 | convolution fusion | flops 12586496 | bytes 524288 | tf_op jit(solution)/shard_map/cad,de->cae/dot_general | solution.py:19
  10.9 0.5 %fusion.11 = f32[32,128,16]{1,2,0:T(8,128)S(1)} fusion(f32[32,128,16]{1,0,2:T(8,128)S(1)} %get-tuple-element.7), kind=kOutput, calls=%fused_computation.27 | convolution fusion | flops 12586496 | bytes 524288 | tf_op jit(solution)/shard_map/cad,de->cae/dot_general | solution.py:19
  11.4 0.5 %convolution_add_fusion.1 = f32[32,128,16]{1,2,0:T(8,128)S(1)} fusion(f32[32,128,16]{1,2,0:T(8,128)S(1)} %fusion.15, f32[32,128,16]{1,0,2:T(8,128)S(1)} %get-tuple-element.7), kind=kOutput, calls=%fused_computation.6 | convolution fusion | flops 12652032 | bytes 786432 | tf_op jit(solution)/shard_map/cad,de->cae/dot_general | solution.py:19
  12.0 0.5 %convolution_subtract_fusion.2 = f32[32,128,16]{1,2,0:T(8,128)S(1)} fusion(f32[32,128,16]{1,2,0:T(8,128)S(1)} %fusion.11, f32[32,128,16]{1,0,2:T(8,128)S(1)} %get-tuple-element.8), kind=kOutput, calls=%fused_computation.4 | convolution fusion | flops 12652032 | bytes 786432 | tf_op jit(solution)/shard_map/cad,de->cae/dot_general | solution.py:19
  12.5 3.2 %all-to-all-done = bf16[8,32,128]{2,1,0:T(8,128)(2,1)S(1)} async-done(((bf16[8,32,128]{2,1,0:T(8,128)(2,1)}), bf16[8,32,128]{2,1,0:T(8,128)(2,1)S(1)}, u32[]{:S(2)}, u32[]{:S(2)}) %all-to-all-start) | async-done | bytes 65568 | tf_op jit(solution)/shard_map/all_to_all | solution.py:83
  15.7 0.2 copy.51
  15.9 0.3 copy.52
  16.2 0.4 %convolution_bitcast_fusion = f32[32,128,16]{1,2,0:T(8,128)S(1)} fusion(bf16[32,64,16]{1,2,0:T(8,128)(2,1)S(1)} %copy.52), kind=kOutput, calls=%fused_computation.11 | convolution fusion | flops 50446336 | bytes 327680 | tf_op jit(solution)/shard_map/ab,cbd->cad/dot_general | solution.py:19
  16.6 0.4 %fusion.1 = f32[32,128,16]{1,2,0:T(8,128)S(1)} fusion(bf16[32,64,16]{1,2,0:T(8,128)(2,1)S(1)} %copy.52), kind=kOutput, calls=%fused_computation.10 | convolution fusion | flops 50511872 | bytes 327680 | tf_op jit(solution)/shard_map/ab,cbd->cad/dot_general | solution.py:19
  17.0 0.4 %fusion.23 = f32[32,128,16]{1,2,0:T(8,128)S(1)} fusion(f32[32,128,16]{1,2,0:T(8,128)S(1)} %fusion.1, f32[32,128,16]{1,2,0:T(8,128)S(1)} %convolution_bitcast_fusion, f32[128,16]{0,1:T(8,128)S(1)} %get-tuple-element.9, f32[128,16]{0,1:T(8,128)S(1)} %get-tuple-element.10), kind=kOutput, calls=%fused_computation.42 | convolution fusion | flops 12783104 | bytes 802816 | tf_op jit(solution)/shard_map/cad,de->cae/dot_general | solution.py:19
  17.4 0.4 %fusion.24 = f32[32,128,16]{1,2,0:T(8,128)S(1)} fusion(f32[32,128,16]{1,2,0:T(8,128)S(1)} %convolution_bitcast_fusion, f32[32,128,16]{1,2,0:T(8,128)S(1)} %fusion.1, f32[128,16]{0,1:T(8,128)S(1)} %get-tuple-element.9, f32[128,16]{0,1:T(8,128)S(1)} %get-tuple-element.10), kind=kOutput, calls=%fused_computation.43 | convolution fusion | flops 12783104 | bytes 802816 | tf_op jit(solution)/shard_map/cad,de->cae/dot_general | solution.py:19
  17.9 0.4 %convolution_add_fusion.2 = f32[32,128,16]{1,2,0:T(8,128)S(1)} fusion(f32[32,128,16]{1,2,0:T(8,128)S(1)} %fusion.23, f32[32,128,16]{1,2,0:T(8,128)S(1)} %convolution_bitcast_fusion, f32[32,128,16]{1,2,0:T(8,128)S(1)} %fusion.1, f32[128,16]{0,1:T(8,128)S(1)} %get-tuple-element.9, f32[128,16]{0,1:T(8,128)S(1)} %get-tuple-element.10), kind=kOutput, calls=%fused_computation.7 | convolution fusion | flops 12848640 | bytes 1064960 | tf_op jit(solution)/shard_map/cad,de->cae/dot_general | solution.py:19
  18.3 0.5 %multiply_subtract_fusion = (f32[32,128,16]{1,2,0:T(8,128)S(1)}, f32[32,128,16]{1,2,0:T(8,128)S(1)}) fusion(f32[32,128,16]{1,2,0:T(8,128)S(1)} %convolution_subtract_fusion.2, f32[32,128,16]{1,2,0:T(8,128)S(1)} %convolution_add_fusion.2, f32[32,128,16]{1,2,0:T(8,128)S(1)} %convolution_add_fusion.1, f32[32,128,16]{1,2,0:T(8,128)S(1)} %fusion.24, ...), kind=kOutput, calls=%fused_computation.22 | convolution fusion | flops 13241856 | bytes 2113536 | tf_op jit(solution)/shard_map/cad,de->cae/dot_general | solution.py:19
  18.8 0.4 %fusion.68 = f32[32,128,16]{1,2,0:T(8,128)S(1)} fusion(f32[32,128,16]{1,2,0:T(8,128)S(1)} %get-tuple-element.5), kind=kOutput, calls=%fused_computation.93 | convolution fusion | flops 12586496 | bytes 524288 | tf_op jit(solution)/shard_map/cad,de->cae/dot_general | solution.py:19
  19.2 0.4 %fusion.66 = f32[32,128,16]{1,2,0:T(8,128)S(1)} fusion(f32[32,128,16]{1,2,0:T(8,128)S(1)} %get-tuple-element.6), kind=kOutput, calls=%fused_computation.91 | convolution fusion | flops 12586496 | bytes 524288 | tf_op jit(solution)/shard_map/cad,de->cae/dot_general | solution.py:19
  19.6 0.4 %convolution_subtract_fusion.1 = f32[32,128,16]{1,2,0:T(8,128)S(1)} fusion(f32[32,128,16]{1,2,0:T(8,128)S(1)} %fusion.68, f32[32,128,16]{1,2,0:T(8,128)S(1)} %get-tuple-element.6), kind=kOutput, calls=%fused_computation.3 | convolution fusion | flops 12652032 | bytes 786432 | tf_op jit(solution)/shard_map/cad,de->cae/dot_general | solution.py:19
  20.0 0.4 %convolution_add_fusion = f32[32,128,16]{1,2,0:T(8,128)S(1)} fusion(f32[32,128,16]{1,2,0:T(8,128)S(1)} %fusion.66, f32[32,128,16]{1,2,0:T(8,128)S(1)} %get-tuple-element.5), kind=kOutput, calls=%fused_computation.2 | convolution fusion | flops 12652032 | bytes 786432 | tf_op jit(solution)/shard_map/cad,de->cae/dot_general | solution.py:19
  20.4 0.5 %fusion.7 = f32[32,16,64]{2,1,0:T(8,128)S(1)} fusion(f32[32,128,16]{1,2,0:T(8,128)S(1)} %convolution_add_fusion, f32[32,128,16]{1,2,0:T(8,128)S(1)} %convolution_subtract_fusion.1, f32[128,16]{0,1:T(8,128)S(1)} %get-tuple-element.9, f32[128,16]{0,1:T(8,128)S(1)} %get-tuple-element.10), kind=kOutput, calls=%fused_computation.17 | convolution fusion | flops 50642944 | bytes 671744 | tf_op jit(solution)/shard_map/ab,cbd->cad/dot_general | solution.py:19
  20.9 0.5 %fusion.3 = bf16[32,64,16]{1,2,0:T(8,128)(2,1)S(1)} fusion(f32[32,16,64]{2,1,0:T(8,128)S(1)} %fusion.7, f32[32,128,16]{1,2,0:T(8,128)S(1)} %convolution_subtract_fusion.1, f32[32,128,16]{1,2,0:T(8,128)S(1)} %convolution_add_fusion, f32[128,16]{0,1:T(8,128)S(1)} %get-tuple-element.9, f32[128,16]{0,1:T(8,128)S(1)} %get-tuple-element.10), kind=kOutput, calls=%fused_computation.13 | convolution fusion | flops 50741248 | bytes 737280 | tf_op jit(solution)/shard_map/ab,cbd->cad/dot_general | solution.py:19
  21.4 0.3 copy.61
  21.7 0.4 %copy.75 = bf16[1,32,1024]{1,0,2:T(2,128)(2,1)S(1)} copy(bf16[1,32,1024]{1,2,0:T(8,128)(2,1)S(1)} %bitcast.93) | data formatting | bytes 131072 | tf_op jit(solution)/shard_map/convert_element_type | solution.py:74
  22.2 0.5 %broadcast.243 = bf16[]{:T(256)} broadcast(bf16[]{:T(256)} %constant.229), dimensions={} | broadcast | bytes 4
  22.7 2.2 %reduce = bf16[1024,32]{1,0:T(8,128)(2,1)S(1)} reduce(bf16[1024,1,32]{2,1,0:T(2,128)(2,1)S(1)} %bitcast.91, bf16[]{:T(256)} %broadcast.243), dimensions={1}, to_apply=%bitcast.88.reduce_sub_computation | reduce | bytes 131074
  24.9 0.3 reshape.74
  25.1 9.5 %all_to_all.24 = bf16[8,2,2048]{2,1,0:T(2,128)(2,1)S(1)} all-to-all(bf16[8,2,2048]{2,1,0:T(2,128)(2,1)S(1)} %reshape.74), channel_id=1, replica_groups=mesh['tensor'=4,'context'=8] {'context'}, dimensions={0} | all-to-all | bytes 131072 | tf_op jit(solution)/shard_map/all_to_all | solution.py:85
  34.6 0.3 reshape.75
  35.0 0.3 copy.63
  35.3 0.0 copy-start.1
  35.4 0.0 copy-start.2
  35.4 0.8 %copy-done.1 = bf16[256,128]{1,0:T(8,128)(2,1)S(1)} copy-done((bf16[256,128]{1,0:T(8,128)(2,1)S(1)}, bf16[256,128]{1,0:T(8,128)(2,1)}, u32[]{:S(2)}) %copy-start.1) | copy-done | bytes 65560
  36.2 0.0 copy-done.2
  36.2 1.6 %fusion.18 = bf16[256,128]{1,0:T(8,128)(2,1)} fusion(f32[8,1,32,128]{3,2,0,1:T(8,128)S(1)} %copy.64, bf16[256,128]{1,0:T(8,128)(2,1)} %multiply_convert_fusion, bf16[256,128]{1,0:T(8,128)(2,1)S(1)} %copy-done.1, f32[256]{0:T(256)S(1)} %copy-done.2), kind=kLoop, calls=%fused_computation.35 | loop fusion | flops 196608 | bytes 328704 | tf_op jit(solution)/shard_map/convert_element_type | solution.py:92
  (3 shorter events, 0.1 us)
Async XLA Ops:
  0.0 8.9 %copy-start = (f32[32,1024]{1,0:T(8,128)S(1)}, f32[32,1024]{1,0:T(8,128)}, u32[]{:S(2)}) copy-start(f32[32,1024]{1,0:T(8,128)} %param.8) | copy-start | bytes 393220
  1.6 14.2 %all-to-all-start = ((bf16[8,32,128]{2,1,0:T(8,128)(2,1)}), bf16[8,32,128]{2,1,0:T(8,128)(2,1)S(1)}, u32[]{:S(2)}, u32[]{:S(2)}) async-start(bf16[8,32,128]{2,1,0:T(8,128)(2,1)} %bitcast), calls=%async_computation | async-start | bytes 131072 | tf_op jit(solution)/shard_map/all_to_all | solution.py:83
  35.3 0.8 %copy-start.1 = (bf16[256,128]{1,0:T(8,128)(2,1)S(1)}, bf16[256,128]{1,0:T(8,128)(2,1)}, u32[]{:S(2)}) copy-start(bf16[256,128]{1,0:T(8,128)(2,1)} %param.5) | copy-start | bytes 196612
  35.4 0.8 %copy-start.2 = (f32[256]{0:T(256)S(1)}, f32[256]{0:T(256)}, u32[]{:S(2)}) copy-start(f32[256]{0:T(256)} %param.9) | copy-start | bytes 3076
where the time goes:
time: 38.1 us; the launch traced here: 37.8 us
  blocking collectives  9.51 us (25%)
  matrix products  8.27 us (22%)
  starting transfers between devices  7.25 us (19%)
  other arithmetic  5.39 us (14%)
  local copies, waits for them, and re-layouts  3.89 us (10%)
  waiting for transfers between devices  3.2 us (8%)
    all_to_all x1, blocking collectives, per_device(): lax.all_to_all(convolved.reshape(1, local_ch, -1), 'context', split_axis=...  9.51 us
    dot_general x18, matrix products, matmul(): jnp.einsum(form, left, right, precision=lax.Precision.HIGHEST, preferred_...  8.27 us
    all_to_all x1, starting transfers between devices, per_device(): lax.all_to_all(stacked, 'context', split_axis=0, concat_axis=2, tiled=True)  7.25 us
    all_to_all x1, waiting for transfers between devices, per_device(): lax.all_to_all(stacked, 'context', split_axis=0, concat_axis=2, tiled=True)  3.2 us
    unnamed x2, other arithmetic  2.2 us
    unnamed x11, local copies, waits for them, and re-layouts  2.15 us
    convert_element_type x1, other arithmetic, per_device(): return result.astype(jnp.bfloat16)  1.58 us
    convert_element_type x1, other arithmetic, per_device(): (keys.astype(jnp.float32) * values.astype(jnp.float32)).astype(jnp.bfloat16)  1.56 us
  transfers between devices with their start and end apart: 1, of which 1 were waited for; matrix products, arithmetic and copies ran while one was open for 10% of the time, Pallas kernels for 0%

commit v1 on v0

v1 whole, which is shorter than its diff:
```python
import functools
import math

import jax
import jax.numpy as jnp
import ml_dtypes
import numpy as np
from jax import lax
from jax.experimental import pallas as pl
from jax.experimental.pallas import tpu as pltpu
from jax.sharding import PartitionSpec as P

AXIS = "context"
HALVES = 2


def split_table(table):
    high = table.astype(ml_dtypes.bfloat16)
    low = (table - high.astype(np.float64)).astype(ml_dtypes.bfloat16)
    return high, low


def tables(block):
    full = 2 * block
    angles = np.pi * (2 * np.arange(block) + 1) / full
    signal = np.outer(np.arange(block), angles)
    taps = np.outer(np.arange(full) - block, angles)
    wx_high, wx_low = split_table(np.concatenate([np.cos(signal), -np.sin(signal)], axis=1))
    wf_high, wf_low = split_table(np.concatenate([np.cos(taps), -np.sin(taps)], axis=1))
    wy_high, wy_low = split_table(
        np.concatenate([np.cos(signal.T), -np.sin(signal.T)], axis=0) / block
    )
    return (
        np.concatenate([wx_high, wx_low], axis=0),
        np.concatenate([wf_high, wf_high, wf_low], axis=0),
        np.concatenate([wy_high, wy_high, wy_low], axis=0),
    )


def dot(left, right):
    return lax.dot_general(
        left, right, (((1,), (0,)), ((), ())), preferred_element_type=jnp.float32
    )


def split_dot(left, right):
    high = left.astype(jnp.bfloat16)
    low = (left - high.astype(jnp.float32)).astype(jnp.bfloat16)
    return dot(jnp.concatenate([high, low, high], axis=1), right)


def gate_kernel(keys_ref, values_ref, gated_ref, send_ref):
    peers, halves, rows, _ = send_ref.shape
    groups = peers // halves
    gated = (keys_ref[...].astype(jnp.float32) * values_ref[...].astype(jnp.float32)).astype(
        jnp.bfloat16
    )
    gated_ref[...] = gated
    for half in range(halves):
        for group in range(groups):
            start = (half * groups + group) * rows
            part = gated[start : start + rows]
            for copy in range(halves):
                send_ref[copy * groups + group, half] = part


def taps_kernel(own_ref, other_ref, table_ref, gated_ref, skip_ref, taps_ref, skipped_ref):
    half = lax.axis_index(AXIS) // (lax.axis_size(AXIS) // HALVES)
    shards, _, rows, full = taps_ref.shape
    block = full // 2
    table = table_ref[...]
    for which, ref in ((half, own_ref), (1 - half, other_ref)):
        padded = jnp.concatenate([jnp.zeros((rows, block), jnp.float32), ref[...]], axis=1)
        windows = jnp.concatenate(
            [padded[:, m * block : m * block + full] for m in range(shards)], axis=0
        )
        spectra = split_dot(windows, table)
        for m in range(shards):
            taps_ref[m, which] = spectra[m * rows : (m + 1) * rows]
    skipped_ref[...] = skip_ref[...] * gated_ref[...].astype(jnp.float32)


def conv_kernel(arrived_ref, taps_ref, wx_ref, wy_ref, *refs):
    outs, signal_ref, product_ref = refs[:-2], refs[-2], refs[-1]
    shards, halves, rows, block = arrived_ref.shape
    groups = shards // halves
    index = lax.axis_index(AXIS)
    half, group = index // groups, lax.rem(index, groups)
    chans = halves * rows
    arrived = arrived_ref[...].reshape(shards * chans, block)
    signal_ref[...] = dot(jnp.concatenate([arrived, arrived], axis=1), wx_ref[...])

    for part in range(halves):

        @pl.when(half == part)
        def _():
            for piece in range(chans // 8):
                which, at = piece * 8 // rows, piece * 8 % rows
                taps_re = []
                taps_im = []
                last = (part + 1) * groups
                for m in range(last):
                    tap = taps_ref[m, which, at : at + 8, :]
                    taps_re.append(tap[:, :block])
                    taps_im.append(tap[:, block:])
                total_re = [None] * groups
                total_im = [None] * groups
                for b in range(last):
                    row = b * chans + piece * 8
                    wave = signal_ref[row : row + 8, :]
                    re, im = wave[:, :block], wave[:, block:]
                    for g in range(groups):
                        m = part * groups + g - b
                        if m < 0:
                            continue
                        new_re = re * taps_re[m] - im * taps_im[m]
                        new_im = re * taps_im[m] + im * taps_re[m]
                        total_re[g] = new_re if b == 0 else total_re[g] + new_re
                        total_im[g] = new_im if b == 0 else total_im[g] + new_im
                for g in range(groups):
                    row = g * chans + piece * 8
                    product_ref[row : row + 8, :block] = total_re[g]
                    product_ref[row : row + 8, block:] = total_im[g]

    for k, out_ref in enumerate(outs):
        start = pl.multiple_of((group ^ k) * chans, chans)
        spectrum = product_ref[pl.ds(start, chans), :]
        out_ref[...] = split_dot(spectrum, wy_ref[...]).astype(jnp.bfloat16)


def final_kernel(queries_ref, skipped_ref, *refs):
    parts, out_ref = refs[:-1], refs[-1]
    groups = len(parts)
    group = lax.rem(lax.axis_index(AXIS), groups)
    rows = parts[0].shape[0] // HALVES
    for k, part_ref in enumerate(parts):
        for half in range(HALVES):
            start = pl.multiple_of((half * groups + (group ^ k)) * rows, rows)
            place = pl.ds(start, rows)
            total = (
                part_ref[half * rows : (half + 1) * rows, :].astype(jnp.float32)
                + skipped_ref[place, :]
            )
            out_ref[place, :] = (queries_ref[place, :].astype(jnp.float32) * total).astype(
                jnp.bfloat16
            )


def call(kernel, outs, args, scratch=()):
    vmem = pl.BlockSpec(memory_space=pltpu.VMEM)
    return pl.pallas_call(
        kernel,
        out_shape=[jax.ShapeDtypeStruct(shape, dtype) for shape, dtype in outs],
        in_specs=[vmem] * len(args),
        out_specs=[vmem] * len(outs),
        scratch_shapes=list(scratch),
        compiler_params=pltpu.CompilerParams(vmem_limit_bytes=48 * 1024 * 1024),
    )(*args)


def per_device(queries, keys, values, filters, skip):
    channels, block = keys.shape
    shards = lax.axis_size(AXIS)
    groups = shards // HALVES
    rows = channels // shards
    chans = HALVES * rows
    wx, wf, wy = (jnp.asarray(table) for table in tables(block))
    f32, bf16 = jnp.float32, jnp.bfloat16

    other = lax.ppermute(filters, AXIS, [(i, i ^ groups) for i in range(shards)])
    gated, send = call(
        gate_kernel,
        [((channels, block), bf16), ((shards, HALVES, rows, block), bf16)],
        (keys, values),
    )
    arrived = lax.all_to_all(send, AXIS, split_axis=0, concat_axis=0, tiled=True)
    spread = jnp.broadcast_to(skip[:, None], (channels, block))
    taps, skipped = call(
        taps_kernel,
        [((shards, HALVES, rows, 2 * block), f32), ((channels, block), f32)],
        (filters, other, wf, gated, spread),
    )
    parts = call(
        conv_kernel,
        [((chans, block), bf16)] * groups,
        (arrived, taps, wx, wy),
        [
            pltpu.VMEM((shards * chans, 2 * block), f32),
            pltpu.VMEM((groups * chans, 2 * block), f32),
        ],
    )
    returned = list(parts)
    for k in range(groups - 1, 0, -1):
        returned[k] = lax.ppermute(parts[k], AXIS, [(i, i ^ k) for i in range(shards)])
    return call(final_kernel, [((channels, block), bf16)], (queries, skipped, *returned))[0]


def solution(mesh):
    placed = (
        P("tensor", AXIS),
        P("tensor", AXIS),
        P("tensor", AXIS),
        P(("tensor", AXIS), None),
        P("tensor"),
    )
    return jax.shard_map(
        per_device, mesh=mesh, in_specs=placed, out_specs=P("tensor", AXIS), check_vma=False
    )
```

time: 38.1 us -> 30.4 us (0.80)
  blocking collectives: 9.51 us -> 0 us
  matrix products: 8.27 us -> 0 us
  waiting for transfers between devices: 3.2 us -> 11.4 us
  starting transfers between devices: 7.25 us -> 13.9 us
  other arithmetic: 5.39 us -> 0 us
  Pallas kernels: 0 us -> 2.39 us
  local copies, waits for them, and re-layouts: 3.89 us -> 2.4 us
    ppermute x0 -> x4, waiting for transfers between devices: none -> 11.4 us  [the longest x1 8.75 us: per_device(): lax.ppermute(filters, AXIS, [(i, i ^ groups) for i in range(shards)])]
    all_to_all x1 -> x0, blocking collectives: 9.51 us -> none  [per_device(): lax.all_to_all(convolved.reshape(1, local_ch, -1), 'context', split_axis=...]
    dot_general x18 -> x0, matrix products: 8.27 us -> none  [matmul(): jnp.einsum(form, left, right, precision=lax.Precision.HIGHEST, preferred_...]
    ppermute x0 -> x4, starting transfers between devices: none -> 6.47 us  [the longest x3 3.55 us: per_device(): lax.ppermute(parts[k], AXIS, [(i, i ^ k) for i in range(shards)])]
    all_to_all x1, waiting for transfers between devices: 3.2 us -> 0.01 us  [per_device(): lax.all_to_all(send, AXIS, split_axis=0, concat_axis=0, tiled=True)]
    convert_element_type x2 -> x0, other arithmetic: 3.13 us -> none  [the longest x1 1.58 us: per_device(): return result.astype(jnp.bfloat16)]
    pallas_call x0 -> x4, Pallas kernels: none -> 2.39 us  [call(): pl.pallas_call(kernel, out_shape=[jax.ShapeDtypeStruct(shape, dtype) for...]
    unnamed x2 -> x0, other arithmetic: 2.2 us -> none
  transfers between devices with their start and end apart: 1 -> 5, of which waited for: 1 -> 4; matrix products, arithmetic and copies ran while one was open for 10% -> 0% of each run, Pallas kernels for 0% -> 1%
where the time goes in v1:
time: 30.4 us; the launch traced here: 30.1 us
  starting transfers between devices  13.9 us (46%)
  waiting for transfers between devices  11.4 us (38%)
  local copies, waits for them, and re-layouts  2.4 us (8%)
  Pallas kernels  2.39 us (8%)
    ppermute x1, waiting for transfers between devices, per_device(): lax.ppermute(filters, AXIS, [(i, i ^ groups) for i in range(shards)])  8.75 us
    all_to_all x1, starting transfers between devices, per_device(): lax.all_to_all(send, AXIS, split_axis=0, concat_axis=0, tiled=True)  7.38 us
    ppermute x3, starting transfers between devices, per_device(): lax.ppermute(parts[k], AXIS, [(i, i ^ k) for i in range(shards)])  3.55 us
    ppermute x1, starting transfers between devices, per_device(): lax.ppermute(filters, AXIS, [(i, i ^ groups) for i in range(shards)])  2.92 us
    ppermute x3, waiting for transfers between devices, per_device(): lax.ppermute(parts[k], AXIS, [(i, i ^ k) for i in range(shards)])  2.61 us
    pallas_call x4, Pallas kernels, call(): pl.pallas_call(kernel, out_shape=[jax.ShapeDtypeStruct(shape, dtype) for...  2.39 us
    unnamed x16, local copies, waits for them, and re-layouts  2.32 us
  transfers between devices with their start and end apart: 5, of which 4 were waited for; matrix products, arithmetic and copies ran while one was open for 0% of the time, Pallas kernels for 1%

profile of v1, /device:TPU:0, one launch (start us, length us, event | category | flops | bytes accessed | tf_op | source)
XLA Modules:
  0.0 30.1 jit_solution(10344235554093139125)
XLA Ops:
  0.0 0.0 copy-start
  0.0 0.0 copy-start.5
  0.0 0.9 %copy-done.5 = bf16[256,128]{1,0:T(8,128)(2,1)S(1)} copy-done((bf16[256,128]{1,0:T(8,128)(2,1)S(1)}, bf16[256,128]{1,0:T(8,128)(2,1)}, u32[]{:S(2)}) %copy-start.5) | copy-done | bytes 65560
  0.9 0.0 copy-start.6
  0.9 0.8 %copy-done.6 = bf16[256,128]{1,0:T(8,128)(2,1)S(1)} copy-done((bf16[256,128]{1,0:T(8,128)(2,1)S(1)}, bf16[256,128]{1,0:T(8,128)(2,1)}, u32[]{:S(2)}) %copy-start.6) | copy-done | bytes 65560
  1.7 0.7 %shard_map.82 = (bf16[256,128]{1,0:T(8,128)(2,1)S(1)}, bf16[8,2,32,128]{3,2,1,0:T(8,128)(2,1)}) custom-call(bf16[256,128]{1,0:T(8,128)(2,1)S(1)} %copy-done.5, bf16[256,128]{1,0:T(8,128)(2,1)S(1)} %copy-done.6), custom_call_target="tpu_custom_call" | custom-call | tf_op jit(solution)/shard_map/pallas_call | solution.py:151
  2.4 0.0 copy-start.7
  2.4 7.4 %all-to-all-start = ((bf16[8,2,32,128]{3,2,1,0:T(8,128)(2,1)}), bf16[8,2,32,128]{3,2,1,0:T(8,128)(2,1)S(1)}, u32[]{:S(2)}, u32[]{:S(2)}) async-start(bf16[8,2,32,128]{3,2,1,0:T(8,128)(2,1)} %get-tuple-element.15), calls=%async_computation | async-start | bytes 262144 | tf_op jit(solution)/shard_map/all_to_all | solution.py:176
  9.8 0.0 copy-start.3
  9.8 2.9 %collective-permute-start = (f32[32,1024]{1,0:T(8,128)}, f32[32,1024]{1,0:T(8,128)S(1)}, u32[]{:S(2)}, u32[]{:S(2)}) collective-permute-start(f32[32,1024]{1,0:T(8,128)} %own_ref.1), channel_id=1, source_target_pairs={{0,4},{1,5},{2,6},{3,7},{4,0},{5,1},{6,2},{7,3},{8,12},{9,13},{10,... | collective-permute-start | bytes 393224 | tf_op jit(solution)/shard_map/ppermute | solution.py:170
  12.7 8.8 %collective-permute-done.other_ref = f32[32,1024]{1,0:T(8,128)S(1)} collective-permute-done((f32[32,1024]{1,0:T(8,128)}, f32[32,1024]{1,0:T(8,128)S(1)}, u32[]{:S(2)}, u32[]{:S(2)}) %collective-permute-start) | collective-permute-done | bytes 131104 | tf_op jit(solution)/shard_map/ppermute | solution.py:170
  21.5 0.0 copy-done.7
  21.5 0.1 broadcast_in_dim.2.skip_ref
  21.6 0.0 copy-done
  21.6 0.0 copy-done.3
  21.6 0.0 copy-start.1
  21.6 0.0 copy-start.2
  21.6 0.4 %shard_map.83 = (f32[8,2,32,256]{3,2,1,0:T(8,128)S(1)}, f32[256,128]{1,0:T(8,128)S(1)}) custom-call(f32[32,1024]{1,0:T(8,128)S(1)} %copy-done.3, f32[32,1024]{1,0:T(8,128)S(1)} %collective-permute-done.other_ref, bf16[768,256]{1,0:T(8,128)(2,1)S(1)} %copy-done, bf16[256,128]{1,0:T(8,128)(2,1)S(1)} %get-tuple-element.13.gated_ref, ...), custom_call_target="tpu_custom_call" | custom-call | tf_op jit(solution)/shard_map/pallas_call | solution.py:151
  22.0 0.0 all-to-all-done.arrived_ref
  22.0 0.5 %copy-done.1 = bf16[768,128]{1,0:T(8,128)(2,1)S(1)} copy-done((bf16[768,128]{1,0:T(8,128)(2,1)S(1)}, bf16[768,128]{1,0:T(8,128)(2,1)}, u32[]{:S(2)}) %copy-start.1) | copy-done | bytes 196632
  22.5 0.1 copy-done.2
  22.6 0.0 copy-start.4
  22.6 0.7 %shard_map.84 = (bf16[64,128]{1,0:T(8,128)(2,1)S(1)}, bf16[64,128]{1,0:T(8,128)(2,1)S(1)}, bf16[64,128]{1,0:T(8,128)(2,1)S(1)}, bf16[64,128]{1,0:T(8,128)(2,1)S(1)}) custom-call(bf16[8,2,32,128]{3,2,1,0:T(8,128)(2,1)S(1)} %all-to-all-done.arrived_ref, f32[8,2,32,256]{3,2,1,0:T(8,128)S(1)} %get-tuple-element.16.taps_ref, bf16[256,256]{1,0:T(8,128)(2,1)S(1)} %copy-done.2, ...), custom_call_target="tpu_custom_call" | custom-call | tf_op jit(solution)/shard_map/pallas_call | solution.py:151
  23.3 1.5 %collective-permute-start.1 = (bf16[64,128]{1,0:T(8,128)(2,1)S(1)}, bf16[64,128]{1,0:T(8,128)(2,1)S(1)}, u32[]{:S(2)}, u32[]{:S(2)}) collective-permute-start(bf16[64,128]{1,0:T(8,128)(2,1)S(1)} %get-tuple-element.18), channel_id=1, source_target_pairs={{0,1},{1,0},{2,3},{3,2},{4,5},{5,4},{6,7},{7,6},{8,9},{9,8},{10,11... | collective-permute-start | bytes 49160 | tf_op jit(solution)/shard_map/ppermute | solution.py:194
  24.8 0.0 collective-permute-start.2
  24.8 2.0 %collective-permute-start.3 = (bf16[64,128]{1,0:T(8,128)(2,1)S(1)}, bf16[64,128]{1,0:T(8,128)(2,1)S(1)}, u32[]{:S(2)}, u32[]{:S(2)}) collective-permute-start(bf16[64,128]{1,0:T(8,128)(2,1)S(1)} %get-tuple-element.20), channel_id=1, source_target_pairs={{0,3},{1,2},{2,1},{3,0},{4,7},{5,6},{6,5},{7,4},{8,11},{9,10},{10,... | collective-permute-start | bytes 49160 | tf_op jit(solution)/shard_map/ppermute | solution.py:194
  26.8 0.3 collective-permute-done.1.refs_1_
  27.1 1.5 %collective-permute-done.2.refs_2_ = bf16[64,128]{1,0:T(8,128)(2,1)S(1)} collective-permute-done((bf16[64,128]{1,0:T(8,128)(2,1)S(1)}, bf16[64,128]{1,0:T(8,128)(2,1)S(1)}, u32[]{:S(2)}, u32[]{:S(2)}) %collective-permute-start.2) | collective-permute-done | bytes 16416 | tf_op jit(solution)/shard_map/ppermute | solution.py:194
  28.5 0.9 %collective-permute-done.3.refs_3_ = bf16[64,128]{1,0:T(8,128)(2,1)S(1)} collective-permute-done((bf16[64,128]{1,0:T(8,128)(2,1)S(1)}, bf16[64,128]{1,0:T(8,128)(2,1)S(1)}, u32[]{:S(2)}, u32[]{:S(2)}) %collective-permute-start.3) | collective-permute-done | bytes 16416 | tf_op jit(solution)/shard_map/ppermute | solution.py:194
  29.4 0.0 copy-done.4
  29.4 0.7 %shard_map.85 = bf16[256,128]{1,0:T(8,128)(2,1)} custom-call(bf16[256,128]{1,0:T(8,128)(2,1)S(1)} %copy-done.4, f32[256,128]{1,0:T(8,128)S(1)} %get-tuple-element.14.skipped_ref, bf16[64,128]{1,0:T(8,128)(2,1)S(1)} %get-tuple-element.17.refs_0_, bf16[64,128]{1,0:T(8,128)(2,1)S(1)} %collective-permute-done.1.refs_1_, ...), custom_call_target="tpu_custom_call" | custom-call | tf_op jit(solution)/shard_map/pallas_call | solution.py:151
Async XLA Ops:
  0.0 21.6 %copy-start = (bf16[768,256]{1,0:T(8,128)(2,1)S(1)}, bf16[768,256]{1,0:T(8,128)(2,1)}, u32[]{:S(2)}) copy-start(bf16[768,256]{1,0:T(8,128)(2,1)} %constant.7.clone.table_ref) | copy-start | bytes 1179652
  0.0 0.9 %copy-start.5 = (bf16[256,128]{1,0:T(8,128)(2,1)S(1)}, bf16[256,128]{1,0:T(8,128)(2,1)}, u32[]{:S(2)}) copy-start(bf16[256,128]{1,0:T(8,128)(2,1)} %keys_ref.1) | copy-start | bytes 196612
  0.9 0.8 %copy-start.6 = (bf16[256,128]{1,0:T(8,128)(2,1)S(1)}, bf16[256,128]{1,0:T(8,128)(2,1)}, u32[]{:S(2)}) copy-start(bf16[256,128]{1,0:T(8,128)(2,1)} %values_ref.1) | copy-start | bytes 196612
  2.4 19.1 %copy-start.7 = (f32[256]{0:T(256)S(1)}, f32[256]{0:T(256)}, u32[]{:S(2)}) copy-start(f32[256]{0:T(256)} %param.12) | copy-start | bytes 3076
  2.4 19.6 %all-to-all-start = ((bf16[8,2,32,128]{3,2,1,0:T(8,128)(2,1)}), bf16[8,2,32,128]{3,2,1,0:T(8,128)(2,1)S(1)}, u32[]{:S(2)}, u32[]{:S(2)}) async-start(bf16[8,2,32,128]{3,2,1,0:T(8,128)(2,1)} %get-tuple-element.15), calls=%async_computation | async-start | bytes 262144 | tf_op jit(solution)/shard_map/all_to_all | solution.py:176
  9.8 11.8 %copy-start.3 = (f32[32,1024]{1,0:T(8,128)S(1)}, f32[32,1024]{1,0:T(8,128)}, u32[]{:S(2)}) copy-start(f32[32,1024]{1,0:T(8,128)} %own_ref.1) | copy-start | bytes 393220
  9.8 11.7 %collective-permute-start = (f32[32,1024]{1,0:T(8,128)}, f32[32,1024]{1,0:T(8,128)S(1)}, u32[]{:S(2)}, u32[]{:S(2)}) collective-permute-start(f32[32,1024]{1,0:T(8,128)} %own_ref.1), channel_id=1, source_target_pairs={{0,4},{1,5},{2,6},{3,7},{4,0},{5,1},{6,2},{7,3},{8,12},{9,13},{10,... | collective-permute-start | bytes 393224 | tf_op jit(solution)/shard_map/ppermute | solution.py:170
  21.6 0.9 %copy-start.1 = (bf16[768,128]{1,0:T(8,128)(2,1)S(1)}, bf16[768,128]{1,0:T(8,128)(2,1)}, u32[]{:S(2)}) copy-start(bf16[768,128]{1,0:T(8,128)(2,1)} %constant.8.clone.wy_ref) | copy-start | bytes 589828
  21.6 1.0 %copy-start.2 = (bf16[256,256]{1,0:T(8,128)(2,1)S(1)}, bf16[256,256]{1,0:T(8,128)(2,1)}, u32[]{:S(2)}) copy-start(bf16[256,256]{1,0:T(8,128)(2,1)} %constant.6.clone.wx_ref) | copy-start | bytes 393220
  22.6 6.8 %copy-start.4 = (bf16[256,128]{1,0:T(8,128)(2,1)S(1)}, bf16[256,128]{1,0:T(8,128)(2,1)}, u32[]{:S(2)}) copy-start(bf16[256,128]{1,0:T(8,128)(2,1)} %queries_ref.1) | copy-start | bytes 196612
  23.3 3.8 %collective-permute-start.1 = (bf16[64,128]{1,0:T(8,128)(2,1)S(1)}, bf16[64,128]{1,0:T(8,128)(2,1)S(1)}, u32[]{:S(2)}, u32[]{:S(2)}) collective-permute-start(bf16[64,128]{1,0:T(8,128)(2,1)S(1)} %get-tuple-element.18), channel_id=1, source_target_pairs={{0,1},{1,0},{2,3},{3,2},{4,5},{5,4},{6,7},{7,6},{8,9},{9,8},{10,11... | collective-permute-start | bytes 49160 | tf_op jit(solution)/shard_map/ppermute | solution.py:194
  24.8 3.7 %collective-permute-start.2 = (bf16[64,128]{1,0:T(8,128)(2,1)S(1)}, bf16[64,128]{1,0:T(8,128)(2,1)S(1)}, u32[]{:S(2)}, u32[]{:S(2)}) collective-permute-start(bf16[64,128]{1,0:T(8,128)(2,1)S(1)} %get-tuple-element.19), channel_id=1, source_target_pairs={{0,2},{1,3},{2,0},{3,1},{4,6},{5,7},{6,4},{7,5},{8,10},{9,11},{10,... | collective-permute-start | bytes 49160 | tf_op jit(solution)/shard_map/ppermute | solution.py:194
  24.8 4.6 %collective-permute-start.3 = (bf16[64,128]{1,0:T(8,128)(2,1)S(1)}, bf16[64,128]{1,0:T(8,128)(2,1)S(1)}, u32[]{:S(2)}, u32[]{:S(2)}) collective-permute-start(bf16[64,128]{1,0:T(8,128)(2,1)S(1)} %get-tuple-element.20), channel_id=1, source_target_pairs={{0,3},{1,2},{2,1},{3,0},{4,7},{5,6},{6,5},{7,4},{8,11},{9,10},{10,... | collective-permute-start | bytes 49160 | tf_op jit(solution)/shard_map/ppermute | solution.py:194

commit v2 on v1

v2 whole, which is shorter than its diff:
```python
import jax
import jax.numpy as jnp
import ml_dtypes
import numpy as np
from jax import lax
from jax.experimental import pallas as pl
from jax.experimental.pallas import tpu as pltpu
from jax.sharding import PartitionSpec as P

AXIS = "context"
HALVES = 2


def split_table(table):
    high = table.astype(ml_dtypes.bfloat16)
    low = (table - high.astype(np.float64)).astype(ml_dtypes.bfloat16)
    return high, low


def transform_table(block):
    full = 2 * block
    angles = np.pi * (2 * np.arange(block) + 1) / full
    signal = np.outer(np.arange(block), angles)
    taps = np.outer(np.arange(full) - block, angles)
    forward = split_table(np.concatenate([np.cos(signal), -np.sin(signal)], axis=1))
    window = split_table(np.concatenate([np.cos(taps), -np.sin(taps)], axis=1))
    back = split_table(np.concatenate([np.cos(signal.T), -np.sin(signal.T)], axis=0) / block)
    return np.concatenate([*forward, *window, np.concatenate(back, axis=1)], axis=0)


def dot(left, right):
    return lax.dot_general(
        left, right, (((1,), (0,)), ((), ())), preferred_element_type=jnp.float32
    )


def split_dot(left, high_table, low_table):
    high = left.astype(jnp.bfloat16)
    low = (left - high.astype(jnp.float32)).astype(jnp.bfloat16)
    return dot(high, high_table) + dot(low, high_table) + dot(high, low_table)


def place():
    index = lax.axis_index(AXIS)
    groups = lax.axis_size(AXIS) // HALVES
    return index // groups, lax.rem(index, groups)


def prepare_kernel(gated_ref, filters_ref, coarse_ref, *sends):
    coarse_ref[...] = filters_ref[...].astype(jnp.bfloat16)
    groups = len(sends)
    _, group = place()
    rows = sends[0].shape[0] // HALVES
    for k, send_ref in enumerate(sends):
        for half in range(HALVES):
            start = pl.multiple_of((half * groups + (group ^ k)) * rows, rows)
            send_ref[half * rows : (half + 1) * rows, :] = gated_ref[pl.ds(start, rows), :]


def taps_of(own_ref, other_ref, table_ref, taps_ref):
    half, _ = place()
    shards, _, rows, full = taps_ref.shape
    block = full // 2
    for which, ref in ((half, own_ref), (1 - half, other_ref)):
        padded = jnp.concatenate(
            [jnp.zeros((rows, block), jnp.float32), ref[...].astype(jnp.float32)], axis=1
        )
        windows = jnp.concatenate(
            [padded[:, m * block : m * block + full] for m in range(shards)], axis=0
        )
        spectra = split_dot(windows, table_ref[full : 2 * full, :], table_ref[2 * full : 3 * full, :])
        for m in range(shards):
            taps_ref[m, which] = spectra[m * rows : (m + 1) * rows]


def signal_of(blocks_ref, table_ref):
    block = blocks_ref.shape[-1]
    stacked = blocks_ref[...].reshape(-1, block)
    return dot(jnp.concatenate([stacked, stacked], axis=1), table_ref[: 2 * block, :])


def products(signal_ref, taps_ref, shift, shape, store):
    groups, chans, block = shape
    rows = chans // HALVES
    for piece in range(chans // 8):
        which, at = piece * 8 // rows, piece * 8 % rows
        waves = [signal_ref[b * chans + piece * 8 : b * chans + piece * 8 + 8, :] for b in range(groups)]
        for j in range(groups):
            total_re = total_im = None
            for b in range(groups):
                if shift + j < b:
                    continue
                tap = taps_ref[shift + j - b, which, at : at + 8, :]
                re, im = waves[b][:, :block], waves[b][:, block:]
                tap_re, tap_im = tap[:, :block], tap[:, block:]
                new_re = re * tap_re - im * tap_im
                new_im = re * tap_im + im * tap_re
                total_re = new_re if total_re is None else total_re + new_re
                total_im = new_im if total_im is None else total_im + new_im
            store(slice(j * chans + piece * 8, j * chans + piece * 8 + 8), total_re, total_im)


def stack_kernel(*refs):
    arrived, blocks_ref = refs[:-1][::-1], refs[-1]
    _, group = place()
    for k, ref in enumerate(arrived):
        blocks_ref[group ^ k] = ref[...]


def near_kernel(own_ref, other_ref, blocks_ref, table_ref, gated_ref, skip_ref, taps_ref, product_ref, skipped_ref, signal_ref):
    skipped_ref[...] = skip_ref[...] * gated_ref[...].astype(jnp.float32)
    block = blocks_ref.shape[-1]
    taps_of(own_ref, other_ref, table_ref, taps_ref)
    signal_ref[...] = signal_of(blocks_ref, table_ref)

    def store(at, re, im):
        product_ref[at, :block] = re
        product_ref[at, block:] = im

    products(signal_ref, taps_ref, 0, blocks_ref.shape, store)


def far_kernel(taps_ref, blocks_ref, near_ref, table_ref, *refs):
    outs, signal_ref, product_ref = refs[:-2], refs[-2], refs[-1]
    half, group = place()
    groups, chans, block = blocks_ref.shape
    full = 2 * block

    @pl.when(half == 0)
    def _():
        product_ref[...] = near_ref[...]

    @pl.when(half > 0)
    def _():
        signal_ref[...] = signal_of(blocks_ref, table_ref)

        def store(at, re, im):
            product_ref[at, :block] = near_ref[at, :block] + re
            product_ref[at, block:] = near_ref[at, block:] + im

        products(signal_ref, taps_ref, groups, blocks_ref.shape, store)

    back = table_ref[3 * full : 4 * full, :]
    for k, out_ref in enumerate(outs):
        start = pl.multiple_of((group ^ k) * chans, chans)
        spectrum = product_ref[pl.ds(start, chans), :]
        out_ref[...] = split_dot(spectrum, back[:, :block], back[:, block:]).astype(jnp.bfloat16)


def final_kernel(queries_ref, skipped_ref, *refs):
    parts, out_ref = refs[:-1][::-1], refs[-1]
    groups = len(parts)
    _, group = place()
    rows = parts[0].shape[0] // HALVES
    for k, part_ref in enumerate(parts):
        for half in range(HALVES):
            start = pl.multiple_of((half * groups + (group ^ k)) * rows, rows)
            where = pl.ds(start, rows)
            total = (
                part_ref[half * rows : (half + 1) * rows, :].astype(jnp.float32)
                + skipped_ref[where, :]
            )
            out_ref[where, :] = (queries_ref[where, :].astype(jnp.float32) * total).astype(
                jnp.bfloat16
            )


def call(kernel, outs, args, scratch=()):
    vmem = pl.BlockSpec(memory_space=pltpu.VMEM)
    return pl.pallas_call(
        kernel,
        out_shape=[jax.ShapeDtypeStruct(shape, dtype) for shape, dtype in outs],
        in_specs=[vmem] * len(args),
        out_specs=[vmem] * len(outs),
        scratch_shapes=list(scratch),
        compiler_params=pltpu.CompilerParams(vmem_limit_bytes=16 * 1024 * 1024),
    )(*args)


def per_device(queries, keys, values, filters, skip):
    channels, block = keys.shape
    shards = lax.axis_size(AXIS)
    groups = shards // HALVES
    rows = channels // shards
    chans = HALVES * rows
    f32, bf16 = jnp.float32, jnp.bfloat16
    table = jnp.asarray(transform_table(block))
    swap = lambda x, k: lax.ppermute(x, AXIS, [(i, i ^ k) for i in range(shards)])

    gated = (keys.astype(f32) * values.astype(f32)).astype(bf16)
    coarse, *sends = call(
        prepare_kernel,
        [(filters.shape, bf16)] + [((chans, block), bf16)] * groups,
        (gated, filters),
    )
    other = swap(coarse, groups)
    arrived = [swap(sends[k], k) if k else sends[k] for k in range(groups - 1, -1, -1)]
    (own,) = call(stack_kernel, [((groups, chans, block), bf16)], arrived)
    across = swap(own, groups)
    spread = jnp.broadcast_to(skip[:, None], (channels, block))
    taps, product, skipped = call(
        near_kernel,
        [((shards, HALVES, rows, 2 * block), f32), ((groups * chans, 2 * block), f32), ((channels, block), f32)],
        (filters, other, own, table, gated, spread),
        [pltpu.VMEM((groups * chans, 2 * block), f32)],
    )
    parts = call(
        far_kernel,
        [((chans, block), bf16)] * groups,
        (taps, across, product, table),
        [pltpu.VMEM((groups * chans, 2 * block), f32)] * 2,
    )
    returned = [swap(parts[k], k) if k else parts[k] for k in range(groups - 1, -1, -1)]
    return call(final_kernel, [((channels, block), bf16)], (queries, skipped, *returned))[0]


def solution(mesh):
    placed = (
        P("tensor", AXIS),
        P("tensor", AXIS),
        P("tensor", AXIS),
        P(("tensor", AXIS), None),
        P("tensor"),
    )
    return jax.shard_map(
        per_device, mesh=mesh, in_specs=placed, out_specs=P("tensor", AXIS), check_vma=False
    )
```

time: 30.4 us -> 22.7 us (0.75)
  waiting for transfers between devices: 11.4 us -> 5.4 us
  local copies, waits for them, and re-layouts: 2.4 us -> 1 us
  other arithmetic: 0 us -> 0.95 us
  Pallas kernels: 2.39 us -> 1.46 us
    all_to_all x1 -> x0, starting transfers between devices: 7.38 us -> none  [per_device(): lax.all_to_all(send, AXIS, split_axis=0, concat_axis=0, tiled=True)]
    ppermute x4 -> x8, starting transfers between devices: 6.47 us -> 13.7 us  [per_device(): lax.ppermute(x, AXIS, [(i, i ^ k) for i in range(shards)])]
    ppermute x4 -> x8, waiting for transfers between devices: 11.4 us -> 5.4 us  [per_device(): lax.ppermute(x, AXIS, [(i, i ^ k) for i in range(shards)])]
    unnamed x16 -> x10, local copies, waits for them, and re-layouts: 2.32 us -> 0.91 us
    convert_element_type x0 -> x1, other arithmetic: none -> 0.95 us  [per_device(): gated = (keys.astype(f32) * values.astype(f32)).astype(bf16)]
    pallas_call x4 -> x5, Pallas kernels: 2.39 us -> 1.46 us  [call(): pl.pallas_call(kernel, out_shape=[jax.ShapeDtypeStruct(shape, dtype) for...]
  transfers between devices with their start and end apart: 5 -> 8, of which waited for: 4 -> 5; matrix products, arithmetic and copies ran while one was open for 0% -> 0% of each run, Pallas kernels for 1% -> 2%
where the time goes in v2:
time: 22.7 us; the launch traced here: 22.6 us
  starting transfers between devices  13.7 us (60%)
  waiting for transfers between devices  5.4 us (24%)
  Pallas kernels  1.46 us (6%)
  local copies, waits for them, and re-layouts  1 us (4%)
  other arithmetic  0.95 us (4%)
    ppermute x8, starting transfers between devices, per_device(): lax.ppermute(x, AXIS, [(i, i ^ k) for i in range(shards)])  13.7 us
    ppermute x8, waiting for transfers between devices, per_device(): lax.ppermute(x, AXIS, [(i, i ^ k) for i in range(shards)])  5.4 us
    pallas_call x5, Pallas kernels, call(): pl.pallas_call(kernel, out_shape=[jax.ShapeDtypeStruct(shape, dtype) for...  1.46 us
    convert_element_type x1, other arithmetic, per_device(): gated = (keys.astype(f32) * values.astype(f32)).astype(bf16)  0.95 us
    unnamed x10, local copies, waits for them, and re-layouts  0.91 us
  transfers between devices with their start and end apart: 8, of which 5 were waited for; matrix products, arithmetic and copies ran while one was open for 0% of the time, Pallas kernels for 2%

profile of v2, /device:TPU:0, one launch (start us, length us, event | category | flops | bytes accessed | tf_op | source)
XLA Modules:
  0.0 22.6 jit_solution(11214380940939132027)
XLA Ops:
  0.0 0.0 copy-start
  0.0 0.9 %multiply_convert_fusion.gated_ref = bf16[256,128]{1,0:T(8,128)(2,1)S(1)} fusion(bf16[256,128]{1,0:T(8,128)(2,1)} %param.8, bf16[256,128]{1,0:T(8,128)(2,1)} %param.7), kind=kLoop, calls=%fused_computation | loop fusion | flops 131072 | bytes 196608 | tf_op jit(solution)/shard_map/convert_element_type | solution.py:190
  1.0 0.0 copy-start.1
  1.0 0.9 %copy-done.1 = f32[32,1024]{1,0:T(8,128)S(1)} copy-done((f32[32,1024]{1,0:T(8,128)S(1)}, f32[32,1024]{1,0:T(8,128)}, u32[]{:S(2)}) %copy-start.1) | copy-done | bytes 131096
  1.9 4.0 %collective-permute-start.1 = (bf16[64,128]{1,0:T(8,128)(2,1)S(1)}, bf16[64,128]{1,0:T(8,128)(2,1)S(1)}, u32[]{:S(2)}, u32[]{:S(2)}) collective-permute-start(bf16[64,128]{1,0:T(8,128)(2,1)S(1)} %get-tuple-element.18), channel_id=1, source_target_pairs={{0,3},{1,2},{2,1},{3,0},{4,7},{5,6},{6,5},{7,4},{8,11},{9,10},{10,... | collective-permute-start | bytes 49160 | tf_op jit(solution)/shard_map/ppermute | solution.py:188
  5.9 0.4 %collective-permute-start.2 = (bf16[64,128]{1,0:T(8,128)(2,1)S(1)}, bf16[64,128]{1,0:T(8,128)(2,1)S(1)}, u32[]{:S(2)}, u32[]{:S(2)}) collective-permute-start(bf16[64,128]{1,0:T(8,128)(2,1)S(1)} %get-tuple-element.19), channel_id=1, source_target_pairs={{0,2},{1,3},{2,0},{3,1},{4,6},{5,7},{6,4},{7,5},{8,10},{9,11},{10,... | collective-permute-start | bytes 49160 | tf_op jit(solution)/shard_map/ppermute | solution.py:188
  6.4 0.0 copy-start.4
  6.4 0.2 collective-permute-start.3
  6.5 2.9 %collective-permute-start = (bf16[32,1024]{1,0:T(8,128)(2,1)S(1)}, bf16[32,1024]{1,0:T(8,128)(2,1)S(1)}, u32[]{:S(2)}, u32[]{:S(2)}) collective-permute-start(bf16[32,1024]{1,0:T(8,128)(2,1)S(1)} %get-tuple-element.17), channel_id=1, source_target_pairs={{0,4},{1,5},{2,6},{3,7},{4,0},{5,1},{6,2},{7,3},{8,12},{9,13},{10,... | collective-permute-start | bytes 196616 | tf_op jit(solution)/shard_map/ppermute | solution.py:188
  9.5 0.0 collective-permute-done.1.refs_0_
  9.5 0.7 %collective-permute-done.2.refs_1_ = bf16[64,128]{1,0:T(8,128)(2,1)S(1)} collective-permute-done((bf16[64,128]{1,0:T(8,128)(2,1)S(1)}, bf16[64,128]{1,0:T(8,128)(2,1)S(1)}, u32[]{:S(2)}, u32[]{:S(2)}) %collective-permute-start.2) | collective-permute-done | bytes 16416 | tf_op jit(solution)/shard_map/ppermute | solution.py:188
  10.2 0.0 collective-permute-done.3.refs_2_
  10.2 0.0 copy-start.2
  10.2 2.5 %collective-permute-start.4 = (bf16[4,64,128]{2,1,0:T(8,128)(2,1)S(1)}, bf16[4,64,128]{2,1,0:T(8,128)(2,1)S(1)}, u32[]{:S(2)}, u32[]{:S(2)}) collective-permute-start(bf16[4,64,128]{2,1,0:T(8,128)(2,1)S(1)} %shard_map.65.blocks_ref), channel_id=1, source_target_pairs={{0,4},{1,5},{2,6},{3,7},{4,0},{5,1},{6,2},{7,3},{8,12},{9,13},{10,... | collective-permute-start | bytes 196616 | tf_op jit(solution)/shard_map/ppermute | solution.py:188
  12.8 0.0 collective-permute-done.other_ref
  12.8 0.0 copy-done.4
  12.8 0.1 broadcast_in_dim.2.skip_ref
  12.9 0.0 copy-done
  12.9 0.0 copy-done.2
  12.9 0.5 %shard_map.66 = (f32[8,2,32,256]{3,2,1,0:T(8,128)S(1)}, f32[256,256]{1,0:T(8,128)S(1)}, f32[256,128]{1,0:T(8,128)S(1)}) custom-call(f32[32,1024]{1,0:T(8,128)S(1)} %copy-done.2, bf16[32,1024]{1,0:T(8,128)(2,1)S(1)} %collective-permute-done.other_ref, bf16[4,64,128]{2,1,0:T(8,128)(2,1)S(1)} %shard_map.65.blocks_ref, bf16[1024,256]{1,0:T(8,128)(2,1)S(1)} %copy-done, ...), custom_call_target="tpu_custom_call" | custom-call | tf_op jit(solution)/shard_map/pallas_call | solution.py:170
  13.4 2.1 %collective-permute-done.4.blocks_ref = bf16[4,64,128]{2,1,0:T(8,128)(2,1)S(1)} collective-permute-done((bf16[4,64,128]{2,1,0:T(8,128)(2,1)S(1)}, bf16[4,64,128]{2,1,0:T(8,128)(2,1)S(1)}, u32[]{:S(2)}, u32[]{:S(2)}) %collective-permute-start.4) | collective-permute-done | bytes 65568 | tf_op jit(solution)/shard_map/ppermute | solution.py:188
  15.5 0.0 copy-start.3
  15.5 0.3 %shard_map.67 = (bf16[64,128]{1,0:T(8,128)(2,1)S(1)}, bf16[64,128]{1,0:T(8,128)(2,1)S(1)}, bf16[64,128]{1,0:T(8,128)(2,1)S(1)}, bf16[64,128]{1,0:T(8,128)(2,1)S(1)}) custom-call(f32[8,2,32,256]{3,2,1,0:T(8,128)S(1)} %get-tuple-element.23.taps_ref, bf16[4,64,128]{2,1,0:T(8,128)(2,1)S(1)} %collective-permute-done.4.blocks_ref, ...), custom_call_target="tpu_custom_call" | custom-call | tf_op jit(solution)/shard_map/pallas_call | solution.py:170
  15.7 1.9 %collective-permute-start.5 = (bf16[64,128]{1,0:T(8,128)(2,1)S(1)}, bf16[64,128]{1,0:T(8,128)(2,1)S(1)}, u32[]{:S(2)}, u32[]{:S(2)}) collective-permute-start(bf16[64,128]{1,0:T(8,128)(2,1)S(1)} %get-tuple-element.25), channel_id=1, source_target_pairs={{0,3},{1,2},{2,1},{3,0},{4,7},{5,6},{6,5},{7,4},{8,11},{9,10},{10,... | collective-permute-start | bytes 49160 | tf_op jit(solution)/shard_map/ppermute | solution.py:188
  17.6 0.6 %collective-permute-start.6 = (bf16[64,128]{1,0:T(8,128)(2,1)S(1)}, bf16[64,128]{1,0:T(8,128)(2,1)S(1)}, u32[]{:S(2)}, u32[]{:S(2)}) collective-permute-start(bf16[64,128]{1,0:T(8,128)(2,1)S(1)} %get-tuple-element.26), channel_id=1, source_target_pairs={{0,2},{1,3},{2,0},{3,1},{4,6},{5,7},{6,4},{7,5},{8,10},{9,11},{10,... | collective-permute-start | bytes 49160 | tf_op jit(solution)/shard_map/ppermute | solution.py:188
  18.2 1.1 %collective-permute-start.7 = (bf16[64,128]{1,0:T(8,128)(2,1)S(1)}, bf16[64,128]{1,0:T(8,128)(2,1)S(1)}, u32[]{:S(2)}, u32[]{:S(2)}) collective-permute-start(bf16[64,128]{1,0:T(8,128)(2,1)S(1)} %get-tuple-element.27), channel_id=1, source_target_pairs={{0,1},{1,0},{2,3},{3,2},{4,5},{5,4},{6,7},{7,6},{8,9},{9,8},{10,11... | collective-permute-start | bytes 49160 | tf_op jit(solution)/shard_map/ppermute | solution.py:188
  19.3 1.1 %collective-permute-done.5.refs_0_ = bf16[64,128]{1,0:T(8,128)(2,1)S(1)} collective-permute-done((bf16[64,128]{1,0:T(8,128)(2,1)S(1)}, bf16[64,128]{1,0:T(8,128)(2,1)S(1)}, u32[]{:S(2)}, u32[]{:S(2)}) %collective-permute-start.5) | collective-permute-done | bytes 16416 | tf_op jit(solution)/shard_map/ppermute | solution.py:188
  20.4 0.9 %collective-permute-done.6.refs_1_ = bf16[64,128]{1,0:T(8,128)(2,1)S(1)} collective-permute-done((bf16[64,128]{1,0:T(8,128)(2,1)S(1)}, bf16[64,128]{1,0:T(8,128)(2,1)S(1)}, u32[]{:S(2)}, u32[]{:S(2)}) %collective-permute-start.6) | collective-permute-done | bytes 16416 | tf_op jit(solution)/shard_map/ppermute | solution.py:188
  21.4 0.6 %collective-permute-done.7.refs_2_ = bf16[64,128]{1,0:T(8,128)(2,1)S(1)} collective-permute-done((bf16[64,128]{1,0:T(8,128)(2,1)S(1)}, bf16[64,128]{1,0:T(8,128)(2,1)S(1)}, u32[]{:S(2)}, u32[]{:S(2)}) %collective-permute-start.7) | collective-permute-done | bytes 16416 | tf_op jit(solution)/shard_map/ppermute | solution.py:188
  21.9 0.0 copy-done.3
  21.9 0.7 %shard_map.68 = bf16[256,128]{1,0:T(8,128)(2,1)} custom-call(bf16[256,128]{1,0:T(8,128)(2,1)S(1)} %copy-done.3, f32[256,128]{1,0:T(8,128)S(1)} %get-tuple-element.22.skipped_ref, bf16[64,128]{1,0:T(8,128)(2,1)S(1)} %collective-permute-done.5.refs_0_, bf16[64,128]{1,0:T(8,128)(2,1)S(1)} %collective-permute-done.6.refs_1_, ...), custom_call_target="tpu_custom_call" | custom-call | tf_op jit(solution)/shard_map/pallas_call | solution.py:170
  (2 shorter events, 0.0 us)
Async XLA Ops:
  0.0 12.9 %copy-start = (bf16[1024,256]{1,0:T(8,128)(2,1)S(1)}, bf16[1024,256]{1,0:T(8,128)(2,1)}, u32[]{:S(2)}) copy-start(bf16[1024,256]{1,0:T(8,128)(2,1)} %constant.2.clone.table_ref) | copy-start | bytes 1572868
  1.0 0.9 %copy-start.1 = (f32[32,1024]{1,0:T(8,128)S(1)}, f32[32,1024]{1,0:T(8,128)}, u32[]{:S(2)}) copy-start(f32[32,1024]{1,0:T(8,128)} %own_ref.1) | copy-start | bytes 393220
  1.9 7.6 %collective-permute-start.1 = (bf16[64,128]{1,0:T(8,128)(2,1)S(1)}, bf16[64,128]{1,0:T(8,128)(2,1)S(1)}, u32[]{:S(2)}, u32[]{:S(2)}) collective-permute-start(bf16[64,128]{1,0:T(8,128)(2,1)S(1)} %get-tuple-element.18), channel_id=1, source_target_pairs={{0,3},{1,2},{2,1},{3,0},{4,7},{5,6},{6,5},{7,4},{8,11},{9,10},{10,... | collective-permute-start | bytes 49160 | tf_op jit(solution)/shard_map/ppermute | solution.py:188
  5.9 4.3 %collective-permute-start.2 = (bf16[64,128]{1,0:T(8,128)(2,1)S(1)}, bf16[64,128]{1,0:T(8,128)(2,1)S(1)}, u32[]{:S(2)}, u32[]{:S(2)}) collective-permute-start(bf16[64,128]{1,0:T(8,128)(2,1)S(1)} %get-tuple-element.19), channel_id=1, source_target_pairs={{0,2},{1,3},{2,0},{3,1},{4,6},{5,7},{6,4},{7,5},{8,10},{9,11},{10,... | collective-permute-start | bytes 49160 | tf_op jit(solution)/shard_map/ppermute | solution.py:188
  6.4 6.4 %copy-start.4 = (f32[256]{0:T(256)S(1)}, f32[256]{0:T(256)}, u32[]{:S(2)}) copy-start(f32[256]{0:T(256)} %param.10) | copy-start | bytes 3076
  6.4 3.9 %collective-permute-start.3 = (bf16[64,128]{1,0:T(8,128)(2,1)S(1)}, bf16[64,128]{1,0:T(8,128)(2,1)S(1)}, u32[]{:S(2)}, u32[]{:S(2)}) collective-permute-start(bf16[64,128]{1,0:T(8,128)(2,1)S(1)} %get-tuple-element.20), channel_id=1, source_target_pairs={{0,1},{1,0},{2,3},{3,2},{4,5},{5,4},{6,7},{7,6},{8,9},{9,8},{10,11... | collective-permute-start | bytes 49160 | tf_op jit(solution)/shard_map/ppermute | solution.py:188
  6.5 6.2 %collective-permute-start = (bf16[32,1024]{1,0:T(8,128)(2,1)S(1)}, bf16[32,1024]{1,0:T(8,128)(2,1)S(1)}, u32[]{:S(2)}, u32[]{:S(2)}) collective-permute-start(bf16[32,1024]{1,0:T(8,128)(2,1)S(1)} %get-tuple-element.17), channel_id=1, source_target_pairs={{0,4},{1,5},{2,6},{3,7},{4,0},{5,1},{6,2},{7,3},{8,12},{9,13},{10,... | collective-permute-start | bytes 196616 | tf_op jit(solution)/shard_map/ppermute | solution.py:188
  10.2 2.7 %copy-start.2 = (f32[32,1024]{1,0:T(8,128)S(1)}, f32[32,1024]{1,0:T(8,128)}, u32[]{:S(2)}) copy-start(f32[32,1024]{1,0:T(8,128)} %own_ref.1) | copy-start | bytes 393220
  10.2 5.2 %collective-permute-start.4 = (bf16[4,64,128]{2,1,0:T(8,128)(2,1)S(1)}, bf16[4,64,128]{2,1,0:T(8,128)(2,1)S(1)}, u32[]{:S(2)}, u32[]{:S(2)}) collective-permute-start(bf16[4,64,128]{2,1,0:T(8,128)(2,1)S(1)} %shard_map.65.blocks_ref), channel_id=1, source_target_pairs={{0,4},{1,5},{2,6},{3,7},{4,0},{5,1},{6,2},{7,3},{8,12},{9,13},{10,... | collective-permute-start | bytes 196616 | tf_op jit(solution)/shard_map/ppermute | solution.py:188
  15.5 6.5 %copy-start.3 = (bf16[256,128]{1,0:T(8,128)(2,1)S(1)}, bf16[256,128]{1,0:T(8,128)(2,1)}, u32[]{:S(2)}) copy-start(bf16[256,128]{1,0:T(8,128)(2,1)} %queries_ref.1) | copy-start | bytes 196612
  15.7 4.7 %collective-permute-start.5 = (bf16[64,128]{1,0:T(8,128)(2,1)S(1)}, bf16[64,128]{1,0:T(8,128)(2,1)S(1)}, u32[]{:S(2)}, u32[]{:S(2)}) collective-permute-start(bf16[64,128]{1,0:T(8,128)(2,1)S(1)} %get-tuple-element.25), channel_id=1, source_target_pairs={{0,3},{1,2},{2,1},{3,0},{4,7},{5,6},{6,5},{7,4},{8,11},{9,10},{10,... | collective-permute-start | bytes 49160 | tf_op jit(solution)/shard_map/ppermute | solution.py:188
  17.6 3.7 %collective-permute-start.6 = (bf16[64,128]{1,0:T(8,128)(2,1)S(1)}, bf16[64,128]{1,0:T(8,128)(2,1)S(1)}, u32[]{:S(2)}, u32[]{:S(2)}) collective-permute-start(bf16[64,128]{1,0:T(8,128)(2,1)S(1)} %get-tuple-element.26), channel_id=1, source_target_pairs={{0,2},{1,3},{2,0},{3,1},{4,6},{5,7},{6,4},{7,5},{8,10},{9,11},{10,... | collective-permute-start | bytes 49160 | tf_op jit(solution)/shard_map/ppermute | solution.py:188
  18.2 3.7 %collective-permute-start.7 = (bf16[64,128]{1,0:T(8,128)(2,1)S(1)}, bf16[64,128]{1,0:T(8,128)(2,1)S(1)}, u32[]{:S(2)}, u32[]{:S(2)}) collective-permute-start(bf16[64,128]{1,0:T(8,128)(2,1)S(1)} %get-tuple-element.27), channel_id=1, source_target_pairs={{0,1},{1,0},{2,3},{3,2},{4,5},{5,4},{6,7},{7,6},{8,9},{9,8},{10,11... | collective-permute-start | bytes 49160 | tf_op jit(solution)/shard_map/ppermute | solution.py:188

commit v3 on v0

v3 whole, which is shorter than its diff:
```python
import jax
import jax.numpy as jnp
import ml_dtypes
import numpy as np
from jax import lax
from jax.experimental import pallas as pl
from jax.experimental.pallas import tpu as pltpu
from jax.sharding import PartitionSpec as P

AXIS = "context"
HALVES = 2


def transform_table(block):
    angles = np.pi * np.outer(np.arange(block), 2 * np.arange(block) + 1) / (2 * block)
    table = np.concatenate([np.cos(angles), -np.sin(angles)], axis=1)
    high = table.astype(ml_dtypes.bfloat16)
    low = (table - high.astype(np.float64)).astype(ml_dtypes.bfloat16)
    return np.concatenate([high, low], axis=0)


def dot(left, right, turned=False):
    dims = (((1,), (1 if turned else 0,)), ((), ()))
    return lax.dot_general(left, right, dims, preferred_element_type=jnp.float32)


def split(values):
    high = values.astype(jnp.bfloat16)
    return high, (values - high.astype(jnp.float32)).astype(jnp.bfloat16)


def place():
    index = lax.axis_index(AXIS)
    groups = lax.axis_size(AXIS) // HALVES
    return index // groups, lax.rem(index, groups)


def span(start, size):
    return pl.ds(pl.multiple_of(start * size, size), size)


def store_waves(blocks, table_ref, waves_refs):
    _, group = place()
    rows = waves_refs[0].shape[1]
    stacked = jnp.concatenate(blocks, axis=0)
    spectra = dot(jnp.concatenate([stacked, stacked], axis=1), table_ref[...])
    parts = len(waves_refs)
    for k in range(len(blocks) // parts):
        for i, ref in enumerate(waves_refs):
            at = (k * parts + i) * rows
            ref[group ^ k] = spectra[at : at + rows]


def store_taps(taps, table_ref, taps_ref):
    count, rows, full = taps_ref.shape
    block = full // 2
    high, low = split(jnp.concatenate(taps, axis=0))
    spectra = dot(jnp.concatenate([high, high], axis=1), table_ref[...]) + dot(
        low, table_ref[:block, :]
    )
    odd = lax.rem(lax.broadcasted_iota(jnp.int32, (rows, block), 1), 2)
    sign = 1.0 - 2.0 * odd.astype(jnp.float32)
    for m in range(count):
        now = spectra[m * rows : (m + 1) * rows]
        if m == 0:
            taps_ref[m] = now
            continue
        past = spectra[(m - 1) * rows : m * rows]
        taps_ref[m, :, :block] = now[:, :block] - sign * past[:, block:]
        taps_ref[m, :, block:] = now[:, block:] + sign * past[:, :block]


def back_from(spectra, table_ref):
    block = spectra.shape[1] // 2
    high, low = split(spectra)
    top, rest = table_ref[:block, :], table_ref[block:, :]
    total = dot(high, top, True) + dot(low, top, True) + dot(high, rest, True)
    return total * (1.0 / block)


def products(waves_ref, taps_ref, shift, out_ref, start=None):
    groups, rows, full = waves_ref.shape
    block = full // 2
    for at in range(0, rows, 8):
        part = slice(at, at + 8)
        waves = [waves_ref[b, part, :] for b in range(groups)]
        for j in range(groups):
            total = [None, None]
            if start is not None:
                total = [start[j, part, :block], start[j, part, block:]]
            for b in range(groups):
                if shift + j < b:
                    continue
                tap = taps_ref[shift + j - b, part, :]
                re, im = waves[b][:, :block], waves[b][:, block:]
                tap_re, tap_im = tap[:, :block], tap[:, block:]
                new = [re * tap_re - im * tap_im, re * tap_im + im * tap_re]
                total = [n if t is None else t + n for t, n in zip(total, new)]
            out_ref[j, part, :block] = total[0]
            out_ref[j, part, block:] = total[1]


def prepare_kernel(*refs):
    sources, targets, (gated_ref, coarse_ref) = refs[:6], refs[6:10], refs[10:12]
    sends, (keys_ref, values_ref, sem) = refs[12:-3], refs[-3:]
    near_ref, block = targets[0], gated_ref.shape[1]
    copies = [
        pltpu.make_async_copy(source, target, sem.at[i])
        for i, (source, target) in enumerate(zip(sources, (keys_ref, values_ref, *targets)))
    ]
    for copy in copies:
        copy.start()
    copies[0].wait()
    copies[1].wait()
    gated_ref[...] = (
        keys_ref[...].astype(jnp.float32) * values_ref[...].astype(jnp.float32)
    ).astype(jnp.bfloat16)
    groups = len(sends)
    _, group = place()
    rows = sends[0].shape[0] // HALVES
    for k, send_ref in enumerate(sends):
        for half in range(HALVES):
            send_ref[half * rows : (half + 1) * rows, :] = gated_ref[
                span(half * groups + (group ^ k), rows), :
            ]
    copies[2].wait()
    for m in range(near_ref.shape[1] // block):
        coarse_ref[m * rows : (m + 1) * rows, :] = near_ref[
            :, m * block : (m + 1) * block
        ].astype(jnp.bfloat16)
    for copy in copies[3:]:
        copy.wait()


def stack_kernel(*refs):
    arrived, out_ref = refs[:-1][::-1], refs[-1]
    chans = arrived[0].shape[0]
    for k, ref in enumerate(arrived):
        out_ref[k * chans : (k + 1) * chans, :] = ref[...]


def halves_of(blocks):
    half, _ = place()
    rows = blocks[0].shape[0] // HALVES
    parts = []
    for ref in blocks:
        parts += [ref[span(half, rows), :], ref[span(1 - half, rows), :]]
    return parts


def own_kernel(table_ref, own_ref, gated_ref, skip_ref, *refs):
    arrived, (taps_ref, waves_ref, sums_ref, skipped_ref, own_waves_ref) = refs[:-5][::-1], refs[-5:]
    block = gated_ref.shape[1]
    store_taps(
        [own_ref[:, m * block : (m + 1) * block] for m in range(taps_ref.shape[0])],
        table_ref,
        taps_ref,
    )
    store_waves(halves_of(arrived), table_ref, [own_waves_ref, waves_ref])
    products(own_waves_ref, taps_ref, 0, sums_ref)
    spread = jnp.broadcast_to(skip_ref[...][None, :], (block, gated_ref.shape[0])).T
    skipped_ref[...] = spread * gated_ref[...].astype(jnp.float32)


def other_kernel(table_ref, other_ref, waves_ref, taps_ref, sums_ref):
    rows = waves_ref.shape[1]
    store_taps(
        [
            other_ref[m * rows : (m + 1) * rows, :].astype(jnp.float32)
            for m in range(taps_ref.shape[0])
        ],
        table_ref,
        taps_ref,
    )
    products(waves_ref, taps_ref, 0, sums_ref)


def store_back(own_ref, other_ref, table_ref, back_ref, outs):
    half, group = place()
    groups, rows, full = own_ref.shape
    spectra = [ref[...].reshape(groups * rows, full) for ref in (own_ref, other_ref)]
    back = back_from(jnp.concatenate(spectra, axis=0), table_ref)
    back_ref[...] = back.astype(jnp.bfloat16).reshape(back_ref.shape)
    for k, out_ref in enumerate(outs):
        out_ref[span(half, rows), :] = back_ref[group ^ k]
        out_ref[span(1 - half, rows), :] = back_ref[groups + (group ^ k)]


def near_kernel(table_ref, own_ref, other_ref, *refs):
    store_back(own_ref, other_ref, table_ref, refs[-1], refs[:-1])


def far_kernel(table_ref, own_taps_ref, taps_ref, own_ref, other_ref, across_ref, *refs):
    outs, (own_waves_ref, waves_ref, own_sums_ref, sums_ref, back_ref) = refs[:-5], refs[-5:]
    groups, rows, _ = own_ref.shape
    chans = HALVES * rows
    blocks = [across_ref.at[k * chans : (k + 1) * chans, :] for k in range(groups)]
    store_waves(halves_of(blocks), table_ref, [own_waves_ref, waves_ref])
    products(own_waves_ref, own_taps_ref, groups, own_sums_ref, own_ref)
    products(waves_ref, taps_ref, groups, sums_ref, other_ref)
    store_back(own_sums_ref, sums_ref, table_ref, back_ref, outs)


def join_kernel(*refs):
    parts, out_ref = refs[:-1][::-1], refs[-1]
    groups = len(parts)
    _, group = place()
    rows = parts[0].shape[0] // HALVES
    for k, part_ref in enumerate(parts):
        for half in range(HALVES):
            out_ref[span(half * groups + (group ^ k), rows), :] = part_ref[
                half * rows : (half + 1) * rows, :
            ]


def copy_kernel(in_ref, out_ref):
    out_ref[...] = in_ref[...]


def final_kernel(queries_ref, skipped_ref, convolved_ref, out_ref):
    total = convolved_ref[...].astype(jnp.float32) + skipped_ref[...]
    out_ref[...] = (queries_ref[...].astype(jnp.float32) * total).astype(jnp.bfloat16)


VMEM = pl.BlockSpec(memory_space=pltpu.VMEM)
HBM = pl.BlockSpec(memory_space=pltpu.HBM)


def call(kernel, outs, args, scratch=(), far=0):
    args = [
        pltpu.with_memory_space_constraint(arg, pltpu.HBM) if i < far else arg
        for i, arg in enumerate(args)
    ]
    return pl.pallas_call(
        kernel,
        out_shape=[jax.ShapeDtypeStruct(shape, dtype) for shape, dtype in outs],
        in_specs=[HBM if i < far else VMEM for i in range(len(args))],
        out_specs=[VMEM] * len(outs),
        scratch_shapes=list(scratch),
        compiler_params=pltpu.CompilerParams(vmem_limit_bytes=16 * 1024 * 1024),
    )(*args)


def per_device(queries, keys, values, filters, skip):
    channels, block = keys.shape
    shards = lax.axis_size(AXIS)
    groups = shards // HALVES
    rows = channels // shards
    chans = HALVES * rows
    full = 2 * block
    f32, bf16 = jnp.float32, jnp.bfloat16
    table = jnp.asarray(transform_table(block))
    swap = lambda x, k: lax.ppermute(x, AXIS, [(i, i ^ k) for i in range(shards)])
    whole = ((channels, block), bf16)
    group_part = ((chans, block), bf16)
    spectra = ((groups, rows, full), f32)
    outputs = ((shards, rows, block), bf16)
    all_taps = ((shards, rows, full), f32)
    scratch = lambda *shapes: [pltpu.VMEM(*shape) for shape in shapes]

    near = (filters, skip, table, queries)
    own, skip, table, queries, gated, coarse, *sends = call(
        prepare_kernel,
        [(x.shape, x.dtype) for x in near] + [whole, whole] + [group_part] * groups,
        (keys, values, *near),
        scratch(whole, whole) + [pltpu.SemaphoreType.DMA((6,))],
        6,
    )
    other = swap(coarse, groups)
    arrived = [swap(sends[k], k) if k else sends[k] for k in range(groups - 1, -1, -1)]
    (stacked,) = call(stack_kernel, [whole], arrived)
    across = swap(stacked, groups)
    taps, waves, own_sums, skipped = call(
        own_kernel,
        [all_taps, spectra, spectra, ((channels, block), f32)],
        (table, own, gated, skip, *arrived),
        scratch(spectra),
    )
    other_taps, other_sums = call(other_kernel, [all_taps, spectra], (table, other, waves))

    def give_back(parts):
        returned = [swap(parts[k], k) if k else parts[k] for k in range(groups - 1, -1, -1)]
        return call(join_kernel, [whole], returned)[0]

    def early():
        return give_back(
            call(
                near_kernel, [group_part] * groups, (table, own_sums, other_sums), scratch(outputs)
            ),
        )

    def late(across):
        return give_back(
            call(
                far_kernel,
                [group_part] * groups,
                (table, taps, other_taps, own_sums, other_sums, across),
                scratch(spectra, spectra, spectra, spectra, outputs)
            )
        )

    copy = lambda x: call(copy_kernel, [whole], (x,))[0]
    first = lax.axis_index(AXIS) < groups
    convolved = lax.cond(first, early, lambda: copy(gated))
    convolved = lax.cond(
        first, lambda done, _: copy(done), lambda _, across: late(across), convolved, across
    )
    return call(final_kernel, [whole], (queries, skipped, convolved))[0]


def solution(mesh):
    placed = (
        P("tensor", AXIS),
        P("tensor", AXIS),
        P("tensor", AXIS),
        P(("tensor", AXIS), None),
        P("tensor"),
    )
    return jax.shard_map(
        per_device, mesh=mesh, in_specs=placed, out_specs=P("tensor", AXIS), check_vma=False
    )
```

time: 38.1 us -> 20.9 us (0.55)
  the two profiles are of different devices: /device:TPU:0 before, /device:TPU:24 now
where the time goes in v3:
time: 20.9 us; the launch traced here: 20.7 us
  waiting for transfers between devices  9.95 us (48%)
  starting transfers between devices  7.77 us (37%)
  Pallas kernels  2.9 us (14%)
    ppermute x8, waiting for transfers between devices, per_device(): lax.ppermute(x, AXIS, [(i, i ^ k) for i in range(shards)])  9.95 us
    ppermute x8, starting transfers between devices, per_device(): lax.ppermute(x, AXIS, [(i, i ^ k) for i in range(shards)])  7.77 us
    pallas_call x8, Pallas kernels, call(): pl.pallas_call(kernel, out_shape=[jax.ShapeDtypeStruct(shape, dtype) for...  2.9 us
  transfers between devices with their start and end apart: 8, of which 7 were waited for; matrix products, arithmetic and copies ran while one was open for 0% of the time, Pallas kernels for 3%

profile of v3, /device:TPU:24, one launch (start us, length us, event | category | flops | bytes accessed | tf_op | source)
XLA Modules:
  0.0 20.7 jit_solution(1002773489979129498)
XLA Ops:
  0.0 1.1 %shard_map.64 = (f32[32,1024]{1,0:T(8,128)S(1)}, f32[256]{0:T(256)S(1)}, bf16[256,256]{1,0:T(8,128)(2,1)S(1)}, bf16[256,128]{1,0:T(8,128)(2,1)S(1)}, bf16[256,12...) custom-call(bf16[256,128]{1,0:T(8,128)(2,1)} %refs_0_.1, ...), custom_call_target="tpu_custom_call" | custom-call | tf_op jit(solution)/shard_map/pallas_call | solution.py:234
  1.1 1.4 %collective-permute-start.6 = (bf16[64,128]{1,0:T(8,128)(2,1)S(1)}, bf16[64,128]{1,0:T(8,128)(2,1)S(1)}, u32[]{:S(2)}, u32[]{:S(2)}) collective-permute-start(bf16[64,128]{1,0:T(8,128)(2,1)S(1)} %get-tuple-element.69), channel_id=1, source_target_pairs={{0,3},{1,2},{2,1},{3,0},{4,7},{5,6},{6,5},{7,4},{8,11},{9,10},{10,... | collective-permute-start | bytes 49160 | tf_op jit(solution)/shard_map/ppermute | solution.py:253
  2.6 1.6 %collective-permute-start.7 = (bf16[64,128]{1,0:T(8,128)(2,1)S(1)}, bf16[64,128]{1,0:T(8,128)(2,1)S(1)}, u32[]{:S(2)}, u32[]{:S(2)}) collective-permute-start(bf16[64,128]{1,0:T(8,128)(2,1)S(1)} %get-tuple-element.70), channel_id=1, source_target_pairs={{0,2},{1,3},{2,0},{3,1},{4,6},{5,7},{6,4},{7,5},{8,10},{9,11},{10,... | collective-permute-start | bytes 49160 | tf_op jit(solution)/shard_map/ppermute | solution.py:253
  4.1 0.5 %collective-permute-start.8 = (bf16[64,128]{1,0:T(8,128)(2,1)S(1)}, bf16[64,128]{1,0:T(8,128)(2,1)S(1)}, u32[]{:S(2)}, u32[]{:S(2)}) collective-permute-start(bf16[64,128]{1,0:T(8,128)(2,1)S(1)} %get-tuple-element.71), channel_id=1, source_target_pairs={{0,1},{1,0},{2,3},{3,2},{4,5},{5,4},{6,7},{7,6},{8,9},{9,8},{10,11... | collective-permute-start | bytes 49160 | tf_op jit(solution)/shard_map/ppermute | solution.py:253
  4.7 0.3 %collective-permute-start.9 = (bf16[256,128]{1,0:T(8,128)(2,1)S(1)}, bf16[256,128]{1,0:T(8,128)(2,1)S(1)}, u32[]{:S(2)}, u32[]{:S(2)}) collective-permute-start(bf16[256,128]{1,0:T(8,128)(2,1)S(1)} %get-tuple-element.75), channel_id=1, source_target_pairs={{0,4},{1,5},{2,6},{3,7},{4,0},{5,1},{6,2},{7,3},{8,12},{9,13},{10,... | collective-permute-start | bytes 196616 | tf_op jit(solution)/shard_map/ppermute | solution.py:253
  5.0 0.8 %collective-permute-done.6.refs_0_ = bf16[64,128]{1,0:T(8,128)(2,1)S(1)} collective-permute-done((bf16[64,128]{1,0:T(8,128)(2,1)S(1)}, bf16[64,128]{1,0:T(8,128)(2,1)S(1)}, u32[]{:S(2)}, u32[]{:S(2)}) %collective-permute-start.6) | collective-permute-done | bytes 16416 | tf_op jit(solution)/shard_map/ppermute | solution.py:253
  5.8 0.5 %collective-permute-done.7.refs_1_ = bf16[64,128]{1,0:T(8,128)(2,1)S(1)} collective-permute-done((bf16[64,128]{1,0:T(8,128)(2,1)S(1)}, bf16[64,128]{1,0:T(8,128)(2,1)S(1)}, u32[]{:S(2)}, u32[]{:S(2)}) %collective-permute-start.7) | collective-permute-done | bytes 16416 | tf_op jit(solution)/shard_map/ppermute | solution.py:253
  6.3 1.6 %collective-permute-done.8.refs_2_ = bf16[64,128]{1,0:T(8,128)(2,1)S(1)} collective-permute-done((bf16[64,128]{1,0:T(8,128)(2,1)S(1)}, bf16[64,128]{1,0:T(8,128)(2,1)S(1)}, u32[]{:S(2)}, u32[]{:S(2)}) %collective-permute-start.8) | collective-permute-done | bytes 16416 | tf_op jit(solution)/shard_map/ppermute | solution.py:253
  7.9 0.3 %collective-permute-start.10 = (bf16[256,128]{1,0:T(8,128)(2,1)S(1)}, bf16[256,128]{1,0:T(8,128)(2,1)S(1)}, u32[]{:S(2)}, u32[]{:S(2)}) collective-permute-start(bf16[256,128]{1,0:T(8,128)(2,1)S(1)} %shard_map.67), channel_id=1, source_target_pairs={{0,4},{1,5},{2,6},{3,7},{4,0},{5,1},{6,2},{7,3},{8,12},{9,13},{10,... | collective-permute-start | bytes 196616 | tf_op jit(solution)/shard_map/ppermute | solution.py:253
  8.2 0.3 %shard_map.65 = (f32[8,32,256]{2,1,0:T(8,128)S(1)}, f32[4,32,256]{2,1,0:T(8,128)S(1)}, f32[4,32,256]{2,1,0:T(8,128)S(1)}, f32[256,128]{1,0:T(8,128)S(1)}) custom-call(bf16[256,256]{1,0:T(8,128)(2,1)S(1)} %get-tuple-element.65.table_ref, f32[32,1024]{1,0:T(8,128)S(1)} %get-tuple-element.66.own_ref, bf16[256,128]{1,0:T(8,128)(2,1)S(1)} %get-tuple-element.67.gated_ref, ...), custom_call_target="tpu_custom_call" | custom-call | tf_op jit(solution)/shard_map/pallas_call | solution.py:234
  8.5 3.3 %collective-permute-done.9.other_ref = bf16[256,128]{1,0:T(8,128)(2,1)S(1)} collective-permute-done((bf16[256,128]{1,0:T(8,128)(2,1)S(1)}, bf16[256,128]{1,0:T(8,128)(2,1)S(1)}, u32[]{:S(2)}, u32[]{:S(2)}) %collective-permute-start.9) | collective-permute-done | bytes 65568 | tf_op jit(solution)/shard_map/ppermute | solution.py:253
  11.8 0.2 %shard_map.66 = (f32[8,32,256]{2,1,0:T(8,128)S(1)}, f32[4,32,256]{2,1,0:T(8,128)S(1)}) custom-call(bf16[256,256]{1,0:T(8,128)(2,1)S(1)} %get-tuple-element.65.table_ref, bf16[256,128]{1,0:T(8,128)(2,1)S(1)} %collective-permute-done.9.other_ref, f32[4,32,256]{2,1,0:T(8,128)S(1)} %get-tuple-element.76.waves_ref), custom_call_target="tpu_custom_call" | custom-call | tf_op jit(solution)/shard_map/pallas_call | solution.py:234
  12.1 1.6 %collective-permute-done.10 = bf16[256,128]{1,0:T(8,128)(2,1)S(1)} collective-permute-done((bf16[256,128]{1,0:T(8,128)(2,1)S(1)}, bf16[256,128]{1,0:T(8,128)(2,1)S(1)}, u32[]{:S(2)}, u32[]{:S(2)}) %collective-permute-start.10) | collective-permute-done | bytes 65568 | tf_op jit(solution)/shard_map/ppermute | solution.py:253
  13.6 6.4 %conditional.3 = (bf16[256,128]{1,0:T(8,128)(2,1)S(1)}) conditional(s32[]{:T(128)} %convert_element_type.4, (bf16[256,256]{1,0:T(8,128)(2,1)S(1)}, f32[8,32,256]{2,1,0:T(8,128)S(1)}, f32[8,32,256]{2,1,0:T(8,128)S(1)}, f32[4,32,256]{2,1,0:T(8,128)S(1)}, f32[4,32,256]{2,1,0:T(8,128)S(1)}, /*index=5*/bf16[256,128]{1,0:T(8,128)(2,1)S(1)}) %tuple.17, ...), branch_computations={%region_2.0_spmd, %region_3.0_spmd} | conditional | bytes 196736 | solution.py:305
  13.6 0.6 %branch_0_fun.4 = (bf16[64,128]{1,0:T(8,128)(2,1)S(1)}, bf16[64,128]{1,0:T(8,128)(2,1)S(1)}, bf16[64,128]{1,0:T(8,128)(2,1)S(1)}, bf16[64,128]{1,0:T(8,128)(2,1)S(1)}) custom-call(bf16[256,256]{1,0:T(8,128)(2,1)S(1)} %get-tuple-element.38.table_ref, f32[8,32,256]{2,1,0:T(8,128)S(1)} %get-tuple-element.39.own_taps_ref, ...), custom_call_target="tpu_custom_call" | custom-call | tf_op jit(solution)/shard_map/cond/branch_0_fun/pallas_call | solution.py:234
  14.2 0.1 collective-permute-start.3
  14.3 2.0 %collective-permute-start.4 = (bf16[64,128]{1,0:T(8,128)(2,1)S(1)}, bf16[64,128]{1,0:T(8,128)(2,1)S(1)}, u32[]{:S(2)}, u32[]{:S(2)}) collective-permute-start(bf16[64,128]{1,0:T(8,128)(2,1)S(1)} %get-tuple-element.45), channel_id=1, source_target_pairs={{0,2},{1,3},{2,0},{3,1},{4,6},{5,7},{6,4},{7,5},{8,10},{9,11},{10,... | collective-permute-start | bytes 49160 | tf_op jit(solution)/shard_map/cond/branch_0_fun/ppermute | solution.py:253
  16.3 1.5 %collective-permute-start.5 = (bf16[64,128]{1,0:T(8,128)(2,1)S(1)}, bf16[64,128]{1,0:T(8,128)(2,1)S(1)}, u32[]{:S(2)}, u32[]{:S(2)}) collective-permute-start(bf16[64,128]{1,0:T(8,128)(2,1)S(1)} %get-tuple-element.46), channel_id=1, source_target_pairs={{0,1},{1,0},{2,3},{3,2},{4,5},{5,4},{6,7},{7,6},{8,9},{9,8},{10,11... | collective-permute-start | bytes 49160 | tf_op jit(solution)/shard_map/cond/branch_0_fun/ppermute | solution.py:253
  17.8 1.1 %collective-permute-done.3.refs_0_ = bf16[64,128]{1,0:T(8,128)(2,1)S(1)} collective-permute-done((bf16[64,128]{1,0:T(8,128)(2,1)S(1)}, bf16[64,128]{1,0:T(8,128)(2,1)S(1)}, u32[]{:S(2)}, u32[]{:S(2)}) %collective-permute-start.3) | collective-permute-done | bytes 16416 | tf_op jit(solution)/shard_map/cond/branch_0_fun/ppermute | solution.py:253
  18.9 0.0 collective-permute-done.4.refs_1_
  18.9 1.1 %collective-permute-done.5.refs_2_ = bf16[64,128]{1,0:T(8,128)(2,1)S(1)} collective-permute-done((bf16[64,128]{1,0:T(8,128)(2,1)S(1)}, bf16[64,128]{1,0:T(8,128)(2,1)S(1)}, u32[]{:S(2)}, u32[]{:S(2)}) %collective-permute-start.5) | collective-permute-done | bytes 16416 | tf_op jit(solution)/shard_map/cond/branch_0_fun/ppermute | solution.py:253
  20.1 0.7 %shard_map.68 = bf16[256,128]{1,0:T(8,128)(2,1)} custom-call(bf16[256,128]{1,0:T(8,128)(2,1)S(1)} %get-tuple-element.64.queries_ref, f32[256,128]{1,0:T(8,128)S(1)} %get-tuple-element.73.skipped_ref, bf16[256,128]{1,0:T(8,128)(2,1)S(1)} %get-tuple-element.81.convolved_ref), custom_call_target="tpu_custom_call" | custom-call | tf_op jit(solution)/shard_map/pallas_call | solution.py:234
  (4 shorter events, 0.0 us)
Async XLA Ops:
  1.1 4.7 %collective-permute-start.6 = (bf16[64,128]{1,0:T(8,128)(2,1)S(1)}, bf16[64,128]{1,0:T(8,128)(2,1)S(1)}, u32[]{:S(2)}, u32[]{:S(2)}) collective-permute-start(bf16[64,128]{1,0:T(8,128)(2,1)S(1)} %get-tuple-element.69), channel_id=1, source_target_pairs={{0,3},{1,2},{2,1},{3,0},{4,7},{5,6},{6,5},{7,4},{8,11},{9,10},{10,... | collective-permute-start | bytes 49160 | tf_op jit(solution)/shard_map/ppermute | solution.py:253
  2.6 3.7 %collective-permute-start.7 = (bf16[64,128]{1,0:T(8,128)(2,1)S(1)}, bf16[64,128]{1,0:T(8,128)(2,1)S(1)}, u32[]{:S(2)}, u32[]{:S(2)}) collective-permute-start(bf16[64,128]{1,0:T(8,128)(2,1)S(1)} %get-tuple-element.70), channel_id=1, source_target_pairs={{0,2},{1,3},{2,0},{3,1},{4,6},{5,7},{6,4},{7,5},{8,10},{9,11},{10,... | collective-permute-start | bytes 49160 | tf_op jit(solution)/shard_map/ppermute | solution.py:253
  4.1 3.7 %collective-permute-start.8 = (bf16[64,128]{1,0:T(8,128)(2,1)S(1)}, bf16[64,128]{1,0:T(8,128)(2,1)S(1)}, u32[]{:S(2)}, u32[]{:S(2)}) collective-permute-start(bf16[64,128]{1,0:T(8,128)(2,1)S(1)} %get-tuple-element.71), channel_id=1, source_target_pairs={{0,1},{1,0},{2,3},{3,2},{4,5},{5,4},{6,7},{7,6},{8,9},{9,8},{10,11... | collective-permute-start | bytes 49160 | tf_op jit(solution)/shard_map/ppermute | solution.py:253
  4.7 7.1 %collective-permute-start.9 = (bf16[256,128]{1,0:T(8,128)(2,1)S(1)}, bf16[256,128]{1,0:T(8,128)(2,1)S(1)}, u32[]{:S(2)}, u32[]{:S(2)}) collective-permute-start(bf16[256,128]{1,0:T(8,128)(2,1)S(1)} %get-tuple-element.75), channel_id=1, source_target_pairs={{0,4},{1,5},{2,6},{3,7},{4,0},{5,1},{6,2},{7,3},{8,12},{9,13},{10,... | collective-permute-start | bytes 196616 | tf_op jit(solution)/shard_map/ppermute | solution.py:253
  7.9 5.8 %collective-permute-start.10 = (bf16[256,128]{1,0:T(8,128)(2,1)S(1)}, bf16[256,128]{1,0:T(8,128)(2,1)S(1)}, u32[]{:S(2)}, u32[]{:S(2)}) collective-permute-start(bf16[256,128]{1,0:T(8,128)(2,1)S(1)} %shard_map.67), channel_id=1, source_target_pairs={{0,4},{1,5},{2,6},{3,7},{4,0},{5,1},{6,2},{7,3},{8,12},{9,13},{10,... | collective-permute-start | bytes 196616 | tf_op jit(solution)/shard_map/ppermute | solution.py:253
  14.2 4.7 %collective-permute-start.3 = (bf16[64,128]{1,0:T(8,128)(2,1)S(1)}, bf16[64,128]{1,0:T(8,128)(2,1)S(1)}, u32[]{:S(2)}, u32[]{:S(2)}) collective-permute-start(bf16[64,128]{1,0:T(8,128)(2,1)S(1)} %get-tuple-element.44), channel_id=1, source_target_pairs={{0,3},{1,2},{2,1},{3,0},{4,7},{5,6},{6,5},{7,4},{8,11},{9,10},{10,... | collective-permute-start | bytes 49160 | tf_op jit(solution)/shard_map/cond/branch_0_fun/ppermute | solution.py:253
  14.3 4.6 %collective-permute-start.4 = (bf16[64,128]{1,0:T(8,128)(2,1)S(1)}, bf16[64,128]{1,0:T(8,128)(2,1)S(1)}, u32[]{:S(2)}, u32[]{:S(2)}) collective-permute-start(bf16[64,128]{1,0:T(8,128)(2,1)S(1)} %get-tuple-element.45), channel_id=1, source_target_pairs={{0,2},{1,3},{2,0},{3,1},{4,6},{5,7},{6,4},{7,5},{8,10},{9,11},{10,... | collective-permute-start | bytes 49160 | tf_op jit(solution)/shard_map/cond/branch_0_fun/ppermute | solution.py:253
  16.3 3.7 %collective-permute-start.5 = (bf16[64,128]{1,0:T(8,128)(2,1)S(1)}, bf16[64,128]{1,0:T(8,128)(2,1)S(1)}, u32[]{:S(2)}, u32[]{:S(2)}) collective-permute-start(bf16[64,128]{1,0:T(8,128)(2,1)S(1)} %get-tuple-element.46), channel_id=1, source_target_pairs={{0,1},{1,0},{2,3},{3,2},{4,5},{5,4},{6,7},{7,6},{8,9},{9,8},{10,11... | collective-permute-start | bytes 49160 | tf_op jit(solution)/shard_map/cond/branch_0_fun/ppermute | solution.py:253

commit v4 on v3

--- a/solution.py
+++ b/solution.py
@@ -104,6 +104,7 @@
     sources, targets, (gated_ref, coarse_ref) = refs[:6], refs[6:10], refs[10:12]
     sends, (keys_ref, values_ref, sem) = refs[12:-3], refs[-3:]
     near_ref, block = targets[0], gated_ref.shape[1]
+    half, group = place()
     copies = [
         pltpu.make_async_copy(source, target, sem.at[i])
         for i, (source, target) in enumerate(zip(sources, (keys_ref, values_ref, *targets)))
@@ -116,89 +117,101 @@
         keys_ref[...].astype(jnp.float32) * values_ref[...].astype(jnp.float32)
     ).astype(jnp.bfloat16)
     groups = len(sends)
-    _, group = place()
     rows = sends[0].shape[0] // HALVES
     for k, send_ref in enumerate(sends):
-        for half in range(HALVES):
-            send_ref[half * rows : (half + 1) * rows, :] = gated_ref[
-                span(half * groups + (group ^ k), rows), :
+        for part in range(HALVES):
+            send_ref[part * rows : (part + 1) * rows, :] = gated_ref[
+                span(part * groups + (group ^ k), rows), :
             ]
     copies[2].wait()
-    for m in range(near_ref.shape[1] // block):
-        coarse_ref[m * rows : (m + 1) * rows, :] = near_ref[
-            :, m * block : (m + 1) * block
-        ].astype(jnp.bfloat16)
+    coarse_ref[:rows, :] = sends[0][span(1 - half, rows), :]
+    for m in range(groups):
+        parts = split(near_ref[:, m * block : (m + 1) * block])
+        coarse_ref[(m + 1) * rows : (m + 2) * rows, :] = parts[0]
+        at = (groups + 1 + m) * rows
+        if at < coarse_ref.shape[0]:
+            coarse_ref[at : at + rows, :] = parts[1]
     for copy in copies[3:]:
         copy.wait()
 
 
-def stack_kernel(*refs):
-    arrived, out_ref = refs[:-1][::-1], refs[-1]
-    chans = arrived[0].shape[0]
-    for k, ref in enumerate(arrived):
-        out_ref[k * chans : (k + 1) * chans, :] = ref[...]
-
-
-def halves_of(blocks):
+def lead_kernel(table_ref, own_ref, *refs):
+    arrived, (out_ref, taps_ref, waves_ref, sums_ref) = refs[:-4][::-1], refs[-4:]
     half, _ = place()
-    rows = blocks[0].shape[0] // HALVES
-    parts = []
-    for ref in blocks:
-        parts += [ref[span(half, rows), :], ref[span(1 - half, rows), :]]
-    return parts
-
-
-def own_kernel(table_ref, own_ref, gated_ref, skip_ref, *refs):
-    arrived, (taps_ref, waves_ref, sums_ref, skipped_ref, own_waves_ref) = refs[:-5][::-1], refs[-5:]
-    block = gated_ref.shape[1]
+    groups, rows, full = waves_ref.shape
+    block = full // 2
+
+    @pl.when(half == 0)
+    def _():
+        for k, ref in enumerate(arrived[1:]):
+            out_ref[(groups + k) * rows : (groups + k + 1) * rows, :] = ref[rows:, :]
+        store_taps(
+            [own_ref[:, m * block : (m + 1) * block] for m in range(taps_ref.shape[0])],
+            table_ref,
+            taps_ref,
+        )
+        store_waves([ref[:rows, :] for ref in arrived], table_ref, [waves_ref])
+        products(waves_ref, taps_ref, groups, sums_ref)
+        sums = sums_ref[...].reshape(groups * rows, full)
+        out_ref[: groups * rows, :] = back_from(sums, table_ref).astype(jnp.bfloat16)
+
+
+def store_parts(own, other, outs):
+    half, group = place()
+    rows = outs[0].shape[0] // HALVES
+    for k, out_ref in enumerate(outs):
+        out_ref[span(half, rows), :] = own(group ^ k).astype(jnp.bfloat16)
+        out_ref[span(1 - half, rows), :] = other(group ^ k).astype(jnp.bfloat16)
+
+
+def near_kernel(table_ref, own_ref, other_ref, gated_ref, skip_ref, *refs):
+    groups = (len(refs) - 8) // 2
+    arrived, parts = refs[:groups][::-1], refs[groups : 2 * groups]
+    taps_ref, sums_ref, out_ref, skipped_ref = refs[2 * groups : 2 * groups + 4]
+    other_taps_ref, own_waves_ref, waves_ref, other_sums_ref = refs[2 * groups + 4 :]
+    half, _ = place()
+    _, rows, full = sums_ref.shape
+    block = full // 2
     store_taps(
         [own_ref[:, m * block : (m + 1) * block] for m in range(taps_ref.shape[0])],
         table_ref,
         taps_ref,
     )
-    store_waves(halves_of(arrived), table_ref, [own_waves_ref, waves_ref])
+    other_taps = []
+    for m in range(groups):
+        tap = other_ref[(m + 1) * rows : (m + 2) * rows, :].astype(jnp.float32)
+        at = (groups + 1 + m) * rows
+        if at < other_ref.shape[0]:
+            tap = tap + other_ref[at : at + rows, :].astype(jnp.float32)
+        other_taps.append(tap)
+    store_taps(other_taps, table_ref, other_taps_ref)
+    blocks = []
+    for ref in arrived:
+        blocks += [ref[span(half, rows), :], ref[span(1 - half, rows), :]]
+    store_waves(blocks, table_ref, [own_waves_ref, waves_ref])
     products(own_waves_ref, taps_ref, 0, sums_ref)
+    products(waves_ref, other_taps_ref, 0, other_sums_ref)
+    spectra = [ref[...].reshape(groups * rows, full) for ref in (other_sums_ref, sums_ref)]
+    out_ref[...] = back_from(jnp.concatenate(spectra, axis=0), table_ref).reshape(out_ref.shape)
+    store_parts(lambda j: out_ref[groups + j], lambda j: out_ref[j], parts)
     spread = jnp.broadcast_to(skip_ref[...][None, :], (block, gated_ref.shape[0])).T
     skipped_ref[...] = spread * gated_ref[...].astype(jnp.float32)
 
 
-def other_kernel(table_ref, other_ref, waves_ref, taps_ref, sums_ref):
-    rows = waves_ref.shape[1]
-    store_taps(
-        [
-            other_ref[m * rows : (m + 1) * rows, :].astype(jnp.float32)
-            for m in range(taps_ref.shape[0])
-        ],
-        table_ref,
-        taps_ref,
-    )
-    products(waves_ref, taps_ref, 0, sums_ref)
-
-
-def store_back(own_ref, other_ref, table_ref, back_ref, outs):
-    half, group = place()
-    groups, rows, full = own_ref.shape
-    spectra = [ref[...].reshape(groups * rows, full) for ref in (own_ref, other_ref)]
-    back = back_from(jnp.concatenate(spectra, axis=0), table_ref)
-    back_ref[...] = back.astype(jnp.bfloat16).reshape(back_ref.shape)
-    for k, out_ref in enumerate(outs):
-        out_ref[span(half, rows), :] = back_ref[group ^ k]
-        out_ref[span(1 - half, rows), :] = back_ref[groups + (group ^ k)]
-
-
-def near_kernel(table_ref, own_ref, other_ref, *refs):
-    store_back(own_ref, other_ref, table_ref, refs[-1], refs[:-1])
-
-
-def far_kernel(table_ref, own_taps_ref, taps_ref, own_ref, other_ref, across_ref, *refs):
-    outs, (own_waves_ref, waves_ref, own_sums_ref, sums_ref, back_ref) = refs[:-5], refs[-5:]
-    groups, rows, _ = own_ref.shape
-    chans = HALVES * rows
-    blocks = [across_ref.at[k * chans : (k + 1) * chans, :] for k in range(groups)]
-    store_waves(halves_of(blocks), table_ref, [own_waves_ref, waves_ref])
-    products(own_waves_ref, own_taps_ref, groups, own_sums_ref, own_ref)
-    products(waves_ref, taps_ref, groups, sums_ref, other_ref)
-    store_back(own_sums_ref, sums_ref, table_ref, back_ref, outs)
+def far_kernel(table_ref, taps_ref, sums_ref, other_ref, came_ref, across_ref, *refs):
+    outs, (waves_ref, total_ref, own_ref) = refs[:-3], refs[-3:]
+    groups, rows, full = sums_ref.shape
+    blocks = [came_ref[:rows, :]]
+    blocks += [across_ref[at * rows : (at + 1) * rows, :] for at in range(groups, 2 * groups - 1)]
+    store_waves(blocks, table_ref, [waves_ref])
+    products(waves_ref, taps_ref, groups, total_ref, sums_ref)
+    total = total_ref[...].reshape(groups * rows, full)
+    own_ref[...] = back_from(total, table_ref).reshape(own_ref.shape)
+
+    def other(j):
+        return other_ref[j] + across_ref[span(j, rows), :].astype(jnp.float32)
+
+    store_parts(lambda j: own_ref[j], other, outs)
 
 
 def join_kernel(*refs):
@@ -253,55 +266,56 @@
     swap = lambda x, k: lax.ppermute(x, AXIS, [(i, i ^ k) for i in range(shards)])
     whole = ((channels, block), bf16)
     group_part = ((chans, block), bf16)
-    spectra = ((groups, rows, full), f32)
-    outputs = ((shards, rows, block), bf16)
-    all_taps = ((shards, rows, full), f32)
+    waves_of = ((groups, rows, full), f32)
+    taps_of = lambda count: ((count, rows, full), f32)
+    across_part = (((2 * groups - 1) * rows, block), bf16)
+    outputs = ((shards, rows, block), f32)
     scratch = lambda *shapes: [pltpu.VMEM(*shape) for shape in shapes]
 
     near = (filters, skip, table, queries)
     own, skip, table, queries, gated, coarse, *sends = call(
         prepare_kernel,
-        [(x.shape, x.dtype) for x in near] + [whole, whole] + [group_part] * groups,
+        [(x.shape, x.dtype) for x in near]
+        + [whole, across_part]
+        + [group_part] * groups,
         (keys, values, *near),
         scratch(whole, whole) + [pltpu.SemaphoreType.DMA((6,))],
         6,
     )
     other = swap(coarse, groups)
     arrived = [swap(sends[k], k) if k else sends[k] for k in range(groups - 1, -1, -1)]
-    (stacked,) = call(stack_kernel, [whole], arrived)
-    across = swap(stacked, groups)
-    taps, waves, own_sums, skipped = call(
-        own_kernel,
-        [all_taps, spectra, spectra, ((channels, block), f32)],
-        (table, own, gated, skip, *arrived),
-        scratch(spectra),
-    )
-    other_taps, other_sums = call(other_kernel, [all_taps, spectra], (table, other, waves))
+    (lead,) = call(
+        lead_kernel,
+        [across_part],
+        (table, own, *arrived),
+        scratch(taps_of(shards), waves_of, waves_of),
+    )
+    across = swap(lead, groups)
+    *parts, taps, sums, other_out, skipped = call(
+        near_kernel,
+        [group_part] * groups
+        + [taps_of(shards), waves_of, outputs, ((channels, block), f32)],
+        (table, own, other, gated, skip, *arrived),
+        scratch(taps_of(groups), waves_of, waves_of, waves_of),
+    )
 
     def give_back(parts):
         returned = [swap(parts[k], k) if k else parts[k] for k in range(groups - 1, -1, -1)]
         return call(join_kernel, [whole], returned)[0]
-
-    def early():
-        return give_back(
-            call(
-                near_kernel, [group_part] * groups, (table, own_sums, other_sums), scratch(outputs)
-            ),
-        )
 
     def late(across):
         return give_back(
             call(
                 far_kernel,
                 [group_part] * groups,
-                (table, taps, other_taps, own_sums, other_sums, across),
-                scratch(spectra, spectra, spectra, spectra, outputs)
+                (table, taps, sums, other_out, other, across),
+                scratch(waves_of, waves_of, ((groups, rows, block), f32)),
             )
         )
 
     copy = lambda x: call(copy_kernel, [whole], (x,))[0]
     first = lax.axis_index(AXIS) < groups
-    convolved = lax.cond(first, early, lambda: copy(gated))
+    convolved = lax.cond(first, lambda: give_back(parts), lambda: copy(gated))
     convolved = lax.cond(
         first, lambda done, _: copy(done), lambda _, across: late(across), convolved, across
     )

time: 20.9 us -> 20.6 us (0.986)
  the two profiles are of different devices: /device:TPU:24 before, /device:TPU:30 now
where the time goes in v4:
time: 20.6 us; the launch traced here: 20.4 us
  starting transfers between devices  8.73 us (42%)
  waiting for transfers between devices  8.64 us (42%)
  Pallas kernels  3 us (15%)
    ppermute x8, starting transfers between devices, per_device(): lax.ppermute(x, AXIS, [(i, i ^ k) for i in range(shards)])  8.73 us
    ppermute x8, waiting for transfers between devices, per_device(): lax.ppermute(x, AXIS, [(i, i ^ k) for i in range(shards)])  8.64 us
    pallas_call x7, Pallas kernels, call(): pl.pallas_call(kernel, out_shape=[jax.ShapeDtypeStruct(shape, dtype) for...  3 us
  transfers between devices with their start and end apart: 8, of which 7 were waited for; matrix products, arithmetic and copies ran while one was open for 0% of the time, Pallas kernels for 4%

profile of v4, /device:TPU:30, one launch (start us, length us, event | category | flops | bytes accessed | tf_op | source)
XLA Modules:
  0.0 20.4 jit_solution(17585553023045998320)
XLA Ops:
  0.0 1.1 %shard_map.64 = (f32[32,1024]{1,0:T(8,128)S(1)}, f32[256]{0:T(256)S(1)}, bf16[256,256]{1,0:T(8,128)(2,1)S(1)}, bf16[256,128]{1,0:T(8,128)(2,1)S(1)}, bf16[256,12...) custom-call(bf16[256,128]{1,0:T(8,128)(2,1)} %refs_0_.1, ...), custom_call_target="tpu_custom_call" | custom-call | tf_op jit(solution)/shard_map/pallas_call | solution.py:247
  1.1 0.5 %collective-permute-start.7 = (bf16[64,128]{1,0:T(8,128)(2,1)S(1)}, bf16[64,128]{1,0:T(8,128)(2,1)S(1)}, u32[]{:S(2)}, u32[]{:S(2)}) collective-permute-start(bf16[64,128]{1,0:T(8,128)(2,1)S(1)} %get-tuple-element.71), channel_id=1, source_target_pairs={{0,3},{1,2},{2,1},{3,0},{4,7},{5,6},{6,5},{7,4},{8,11},{9,10},{10,... | collective-permute-start | bytes 49160 | tf_op jit(solution)/shard_map/ppermute | solution.py:266
  1.6 1.6 %collective-permute-start.8 = (bf16[64,128]{1,0:T(8,128)(2,1)S(1)}, bf16[64,128]{1,0:T(8,128)(2,1)S(1)}, u32[]{:S(2)}, u32[]{:S(2)}) collective-permute-start(bf16[64,128]{1,0:T(8,128)(2,1)S(1)} %get-tuple-element.72), channel_id=1, source_target_pairs={{0,2},{1,3},{2,0},{3,1},{4,6},{5,7},{6,4},{7,5},{8,10},{9,11},{10,... | collective-permute-start | bytes 49160 | tf_op jit(solution)/shard_map/ppermute | solution.py:266
  3.2 1.5 %collective-permute-start.9 = (bf16[64,128]{1,0:T(8,128)(2,1)S(1)}, bf16[64,128]{1,0:T(8,128)(2,1)S(1)}, u32[]{:S(2)}, u32[]{:S(2)}) collective-permute-start(bf16[64,128]{1,0:T(8,128)(2,1)S(1)} %get-tuple-element.73), channel_id=1, source_target_pairs={{0,1},{1,0},{2,3},{3,2},{4,5},{5,4},{6,7},{7,6},{8,9},{9,8},{10,11... | collective-permute-start | bytes 49160 | tf_op jit(solution)/shard_map/ppermute | solution.py:266
  4.7 0.3 %collective-permute-start.6 = (bf16[224,128]{1,0:T(8,128)(2,1)S(1)}, bf16[224,128]{1,0:T(8,128)(2,1)S(1)}, u32[]{:S(2)}, u32[]{:S(2)}) collective-permute-start(bf16[224,128]{1,0:T(8,128)(2,1)S(1)} %get-tuple-element.68), channel_id=1, source_target_pairs={{0,4},{1,5},{2,6},{3,7},{4,0},{5,1},{6,2},{7,3},{8,12},{9,13},{10,... | collective-permute-start | bytes 172040 | tf_op jit(solution)/shard_map/ppermute | solution.py:266
  5.0 0.8 %collective-permute-done.7.refs_0_ = bf16[64,128]{1,0:T(8,128)(2,1)S(1)} collective-permute-done((bf16[64,128]{1,0:T(8,128)(2,1)S(1)}, bf16[64,128]{1,0:T(8,128)(2,1)S(1)}, u32[]{:S(2)}, u32[]{:S(2)}) %collective-permute-start.7) | collective-permute-done | bytes 16416 | tf_op jit(solution)/shard_map/ppermute | solution.py:266
  5.8 0.0 collective-permute-done.8.refs_1_
  5.8 1.1 %collective-permute-done.9.refs_2_ = bf16[64,128]{1,0:T(8,128)(2,1)S(1)} collective-permute-done((bf16[64,128]{1,0:T(8,128)(2,1)S(1)}, bf16[64,128]{1,0:T(8,128)(2,1)S(1)}, u32[]{:S(2)}, u32[]{:S(2)}) %collective-permute-start.9) | collective-permute-done | bytes 16416 | tf_op jit(solution)/shard_map/ppermute | solution.py:266
  6.9 1.3 %collective-permute-start.10 = (bf16[224,128]{1,0:T(8,128)(2,1)S(1)}, bf16[224,128]{1,0:T(8,128)(2,1)S(1)}, u32[]{:S(2)}, u32[]{:S(2)}) collective-permute-start(bf16[224,128]{1,0:T(8,128)(2,1)S(1)} %shard_map.66), channel_id=1, source_target_pairs={{0,4},{1,5},{2,6},{3,7},{4,0},{5,1},{6,2},{7,3},{8,12},{9,13},{10,... | collective-permute-start | bytes 172040 | tf_op jit(solution)/shard_map/ppermute | solution.py:266
  8.2 2.7 %collective-permute-done.6.other_ref = bf16[224,128]{1,0:T(8,128)(2,1)S(1)} collective-permute-done((bf16[224,128]{1,0:T(8,128)(2,1)S(1)}, bf16[224,128]{1,0:T(8,128)(2,1)S(1)}, u32[]{:S(2)}, u32[]{:S(2)}) %collective-permute-start.6) | collective-permute-done | bytes 57376 | tf_op jit(solution)/shard_map/ppermute | solution.py:266
  10.9 0.8 %shard_map.65 = (bf16[64,128]{1,0:T(8,128)(2,1)S(1)}, bf16[64,128]{1,0:T(8,128)(2,1)S(1)}, bf16[64,128]{1,0:T(8,128)(2,1)S(1)}, bf16[64,128]{1,0:T(8,128)(2,1)S(...) custom-call(bf16[256,256]{1,0:T(8,128)(2,1)S(1)} %get-tuple-element., ...), custom_call_target="tpu_custom_call" | custom-call | tf_op jit(solution)/shard_map/pallas_call | solution.py:247
  11.7 0.8 %collective-permute-done.10 = bf16[224,128]{1,0:T(8,128)(2,1)S(1)} collective-permute-done((bf16[224,128]{1,0:T(8,128)(2,1)S(1)}, bf16[224,128]{1,0:T(8,128)(2,1)S(1)}, u32[]{:S(2)}, u32[]{:S(2)}) %collective-permute-start.10) | collective-permute-done | bytes 57376 | tf_op jit(solution)/shard_map/ppermute | solution.py:266
  12.5 7.3 %conditional.3 = (bf16[256,128]{1,0:T(8,128)(2,1)S(1)}) conditional(s32[]{:T(128)} %convert_element_type.4, (bf16[256,256]{1,0:T(8,128)(2,1)S(1)}, f32[8,32,256]{2,1,0:T(8,128)S(1)}, f32[4,32,256]{2,1,0:T(8,128)S(1)}, f32[8,32,128]{2,1,0:T(8,128)S(1)}, bf16[224,128]{1,0:T(8,128)(2,1)S(1)}, /*index=5*/bf16[224,128]{1,0:T(8,128)(2,1)S(1)}) %tuple.17, ...), branch_computations={%region_2.0_spmd, %region_3.0_spmd} | conditional | bytes 196736 | solution.py:319
  12.5 0.4 %branch_0_fun.4 = (bf16[64,128]{1,0:T(8,128)(2,1)S(1)}, bf16[64,128]{1,0:T(8,128)(2,1)S(1)}, bf16[64,128]{1,0:T(8,128)(2,1)S(1)}, bf16[64,128]{1,0:T(8,128)(2,1)S(1)}) custom-call(bf16[256,256]{1,0:T(8,128)(2,1)S(1)} %get-tuple-element.37.table_ref, f32[8,32,256]{2,1,0:T(8,128)S(1)} %get-tuple-element.38.taps_ref, ...), custom_call_target="tpu_custom_call" | custom-call | tf_op jit(solution)/shard_map/cond/branch_0_fun/pallas_call | solution.py:247
  12.9 1.1 %collective-permute-start.3 = (bf16[64,128]{1,0:T(8,128)(2,1)S(1)}, bf16[64,128]{1,0:T(8,128)(2,1)S(1)}, u32[]{:S(2)}, u32[]{:S(2)}) collective-permute-start(bf16[64,128]{1,0:T(8,128)(2,1)S(1)} %get-tuple-element.43), channel_id=1, source_target_pairs={{0,3},{1,2},{2,1},{3,0},{4,7},{5,6},{6,5},{7,4},{8,11},{9,10},{10,... | collective-permute-start | bytes 49160 | tf_op jit(solution)/shard_map/cond/branch_0_fun/ppermute | solution.py:266
  14.0 2.0 %collective-permute-start.4 = (bf16[64,128]{1,0:T(8,128)(2,1)S(1)}, bf16[64,128]{1,0:T(8,128)(2,1)S(1)}, u32[]{:S(2)}, u32[]{:S(2)}) collective-permute-start(bf16[64,128]{1,0:T(8,128)(2,1)S(1)} %get-tuple-element.44), channel_id=1, source_target_pairs={{0,2},{1,3},{2,0},{3,1},{4,6},{5,7},{6,4},{7,5},{8,10},{9,11},{10,... | collective-permute-start | bytes 49160 | tf_op jit(solution)/shard_map/cond/branch_0_fun/ppermute | solution.py:266
  16.0 0.5 %collective-permute-start.5 = (bf16[64,128]{1,0:T(8,128)(2,1)S(1)}, bf16[64,128]{1,0:T(8,128)(2,1)S(1)}, u32[]{:S(2)}, u32[]{:S(2)}) collective-permute-start(bf16[64,128]{1,0:T(8,128)(2,1)S(1)} %get-tuple-element.45), channel_id=1, source_target_pairs={{0,1},{1,0},{2,3},{3,2},{4,5},{5,4},{6,7},{7,6},{8,9},{9,8},{10,11... | collective-permute-start | bytes 49160 | tf_op jit(solution)/shard_map/cond/branch_0_fun/ppermute | solution.py:266
  16.5 1.1 %collective-permute-done.3.refs_0_ = bf16[64,128]{1,0:T(8,128)(2,1)S(1)} collective-permute-done((bf16[64,128]{1,0:T(8,128)(2,1)S(1)}, bf16[64,128]{1,0:T(8,128)(2,1)S(1)}, u32[]{:S(2)}, u32[]{:S(2)}) %collective-permute-start.3) | collective-permute-done | bytes 16416 | tf_op jit(solution)/shard_map/cond/branch_0_fun/ppermute | solution.py:266
  17.6 0.3 %collective-permute-done.4.refs_1_ = bf16[64,128]{1,0:T(8,128)(2,1)S(1)} collective-permute-done((bf16[64,128]{1,0:T(8,128)(2,1)S(1)}, bf16[64,128]{1,0:T(8,128)(2,1)S(1)}, u32[]{:S(2)}, u32[]{:S(2)}) %collective-permute-start.4) | collective-permute-done | bytes 16416 | tf_op jit(solution)/shard_map/cond/branch_0_fun/ppermute | solution.py:266
  17.9 1.9 %collective-permute-done.5.refs_2_ = bf16[64,128]{1,0:T(8,128)(2,1)S(1)} collective-permute-done((bf16[64,128]{1,0:T(8,128)(2,1)S(1)}, bf16[64,128]{1,0:T(8,128)(2,1)S(1)}, u32[]{:S(2)}, u32[]{:S(2)}) %collective-permute-start.5) | collective-permute-done | bytes 16416 | tf_op jit(solution)/shard_map/cond/branch_0_fun/ppermute | solution.py:266
  19.8 0.7 %shard_map.67 = bf16[256,128]{1,0:T(8,128)(2,1)} custom-call(bf16[256,128]{1,0:T(8,128)(2,1)S(1)} %get-tuple-element.65.queries_ref, f32[256,128]{1,0:T(8,128)S(1)} %get-tuple-element.75.skipped_ref, bf16[256,128]{1,0:T(8,128)(2,1)S(1)} %get-tuple-element.84.convolved_ref), custom_call_target="tpu_custom_call" | custom-call | tf_op jit(solution)/shard_map/pallas_call | solution.py:247
  (4 shorter events, 0.0 us)
Async XLA Ops:
  1.1 4.7 %collective-permute-start.7 = (bf16[64,128]{1,0:T(8,128)(2,1)S(1)}, bf16[64,128]{1,0:T(8,128)(2,1)S(1)}, u32[]{:S(2)}, u32[]{:S(2)}) collective-permute-start(bf16[64,128]{1,0:T(8,128)(2,1)S(1)} %get-tuple-element.71), channel_id=1, source_target_pairs={{0,3},{1,2},{2,1},{3,0},{4,7},{5,6},{6,5},{7,4},{8,11},{9,10},{10,... | collective-permute-start | bytes 49160 | tf_op jit(solution)/shard_map/ppermute | solution.py:266
  1.6 4.2 %collective-permute-start.8 = (bf16[64,128]{1,0:T(8,128)(2,1)S(1)}, bf16[64,128]{1,0:T(8,128)(2,1)S(1)}, u32[]{:S(2)}, u32[]{:S(2)}) collective-permute-start(bf16[64,128]{1,0:T(8,128)(2,1)S(1)} %get-tuple-element.72), channel_id=1, source_target_pairs={{0,2},{1,3},{2,0},{3,1},{4,6},{5,7},{6,4},{7,5},{8,10},{9,11},{10,... | collective-permute-start | bytes 49160 | tf_op jit(solution)/shard_map/ppermute | solution.py:266
  3.2 3.7 %collective-permute-start.9 = (bf16[64,128]{1,0:T(8,128)(2,1)S(1)}, bf16[64,128]{1,0:T(8,128)(2,1)S(1)}, u32[]{:S(2)}, u32[]{:S(2)}) collective-permute-start(bf16[64,128]{1,0:T(8,128)(2,1)S(1)} %get-tuple-element.73), channel_id=1, source_target_pairs={{0,1},{1,0},{2,3},{3,2},{4,5},{5,4},{6,7},{7,6},{8,9},{9,8},{10,11... | collective-permute-start | bytes 49160 | tf_op jit(solution)/shard_map/ppermute | solution.py:266
  4.7 6.2 %collective-permute-start.6 = (bf16[224,128]{1,0:T(8,128)(2,1)S(1)}, bf16[224,128]{1,0:T(8,128)(2,1)S(1)}, u32[]{:S(2)}, u32[]{:S(2)}) collective-permute-start(bf16[224,128]{1,0:T(8,128)(2,1)S(1)} %get-tuple-element.68), channel_id=1, source_target_pairs={{0,4},{1,5},{2,6},{3,7},{4,0},{5,1},{6,2},{7,3},{8,12},{9,13},{10,... | collective-permute-start | bytes 172040 | tf_op jit(solution)/shard_map/ppermute | solution.py:266
  6.9 5.6 %collective-permute-start.10 = (bf16[224,128]{1,0:T(8,128)(2,1)S(1)}, bf16[224,128]{1,0:T(8,128)(2,1)S(1)}, u32[]{:S(2)}, u32[]{:S(2)}) collective-permute-start(bf16[224,128]{1,0:T(8,128)(2,1)S(1)} %shard_map.66), channel_id=1, source_target_pairs={{0,4},{1,5},{2,6},{3,7},{4,0},{5,1},{6,2},{7,3},{8,12},{9,13},{10,... | collective-permute-start | bytes 172040 | tf_op jit(solution)/shard_map/ppermute | solution.py:266
  12.9 4.7 %collective-permute-start.3 = (bf16[64,128]{1,0:T(8,128)(2,1)S(1)}, bf16[64,128]{1,0:T(8,128)(2,1)S(1)}, u32[]{:S(2)}, u32[]{:S(2)}) collective-permute-start(bf16[64,128]{1,0:T(8,128)(2,1)S(1)} %get-tuple-element.43), channel_id=1, source_target_pairs={{0,3},{1,2},{2,1},{3,0},{4,7},{5,6},{6,5},{7,4},{8,11},{9,10},{10,... | collective-permute-start | bytes 49160 | tf_op jit(solution)/shard_map/cond/branch_0_fun/ppermute | solution.py:266
  14.0 3.9 %collective-permute-start.4 = (bf16[64,128]{1,0:T(8,128)(2,1)S(1)}, bf16[64,128]{1,0:T(8,128)(2,1)S(1)}, u32[]{:S(2)}, u32[]{:S(2)}) collective-permute-start(bf16[64,128]{1,0:T(8,128)(2,1)S(1)} %get-tuple-element.44), channel_id=1, source_target_pairs={{0,2},{1,3},{2,0},{3,1},{4,6},{5,7},{6,4},{7,5},{8,10},{9,11},{10,... | collective-permute-start | bytes 49160 | tf_op jit(solution)/shard_map/cond/branch_0_fun/ppermute | solution.py:266
  16.0 3.7 %collective-permute-start.5 = (bf16[64,128]{1,0:T(8,128)(2,1)S(1)}, bf16[64,128]{1,0:T(8,128)(2,1)S(1)}, u32[]{:S(2)}, u32[]{:S(2)}) collective-permute-start(bf16[64,128]{1,0:T(8,128)(2,1)S(1)} %get-tuple-element.45), channel_id=1, source_target_pairs={{0,1},{1,0},{2,3},{3,2},{4,5},{5,4},{6,7},{7,6},{8,9},{9,8},{10,11... | collective-permute-start | bytes 49160 | tf_op jit(solution)/shard_map/cond/branch_0_fun/ppermute | solution.py:266

commit v5 on v4

--- a/solution.py
+++ b/solution.py
@@ -27,6 +27,15 @@
 def split(values):
     high = values.astype(jnp.bfloat16)
     return high, (values - high.astype(jnp.float32)).astype(jnp.bfloat16)
+
+
+def partners(groups):
+    return (groups - 1, *range(1, groups - 1), 0)
+
+
+def in_order(refs):
+    order = partners(len(refs))
+    return [refs[order.index(k)] for k in range(len(refs))]
 
 
 def place():
@@ -136,7 +145,7 @@
 
 
 def lead_kernel(table_ref, own_ref, *refs):
-    arrived, (out_ref, taps_ref, waves_ref, sums_ref) = refs[:-4][::-1], refs[-4:]
+    arrived, (out_ref, taps_ref, waves_ref, sums_ref) = in_order(refs[:-4]), refs[-4:]
     half, _ = place()
     groups, rows, full = waves_ref.shape
     block = full // 2
@@ -166,7 +175,7 @@
 
 def near_kernel(table_ref, own_ref, other_ref, gated_ref, skip_ref, *refs):
     groups = (len(refs) - 8) // 2
-    arrived, parts = refs[:groups][::-1], refs[groups : 2 * groups]
+    arrived, parts = in_order(refs[:groups]), refs[groups : 2 * groups]
     taps_ref, sums_ref, out_ref, skipped_ref = refs[2 * groups : 2 * groups + 4]
     other_taps_ref, own_waves_ref, waves_ref, other_sums_ref = refs[2 * groups + 4 :]
     half, _ = place()
@@ -215,7 +224,7 @@
 
 
 def join_kernel(*refs):
-    parts, out_ref = refs[:-1][::-1], refs[-1]
+    parts, out_ref = in_order(refs[:-1]), refs[-1]
     groups = len(parts)
     _, group = place()
     rows = parts[0].shape[0] // HALVES
@@ -283,7 +292,7 @@
         6,
     )
     other = swap(coarse, groups)
-    arrived = [swap(sends[k], k) if k else sends[k] for k in range(groups - 1, -1, -1)]
+    arrived = [swap(sends[k], k) if k else sends[k] for k in partners(groups)]
     (lead,) = call(
         lead_kernel,
         [across_part],
@@ -300,7 +309,7 @@
     )
 
     def give_back(parts):
-        returned = [swap(parts[k], k) if k else parts[k] for k in range(groups - 1, -1, -1)]
+        returned = [swap(parts[k], k) if k else parts[k] for k in partners(groups)]
         return call(join_kernel, [whole], returned)[0]
 
     def late(across):

time: 20.6 us -> 20.1 us (0.976)
  the two profiles are of different devices: /device:TPU:30 before, /device:TPU:0 now
where the time goes in v5:
time: 20.1 us; the launch traced here: 20 us
  starting transfers between devices  13.2 us (66%)
  waiting for transfers between devices  3.59 us (18%)
  Pallas kernels  3.05 us (15%)
    ppermute x8, starting transfers between devices, per_device(): lax.ppermute(x, AXIS, [(i, i ^ k) for i in range(shards)])  13.2 us
    ppermute x8, waiting for transfers between devices, per_device(): lax.ppermute(x, AXIS, [(i, i ^ k) for i in range(shards)])  3.59 us
    pallas_call x6, Pallas kernels, call(): pl.pallas_call(kernel, out_shape=[jax.ShapeDtypeStruct(shape, dtype) for...  3.05 us
  transfers between devices with their start and end apart: 8, of which 5 were waited for; matrix products, arithmetic and copies ran while one was open for 0% of the time, Pallas kernels for 6%

profile of v5, /device:TPU:0, one launch (start us, length us, event | category | flops | bytes accessed | tf_op | source)
XLA Modules:
  0.0 20.0 jit_solution(6958777665689552087)
XLA Ops:
  0.0 1.1 %shard_map.64 = (f32[32,1024]{1,0:T(8,128)S(1)}, f32[256]{0:T(256)S(1)}, bf16[256,256]{1,0:T(8,128)(2,1)S(1)}, bf16[256,128]{1,0:T(8,128)(2,1)S(1)}, bf16[256,12...) custom-call(bf16[256,128]{1,0:T(8,128)(2,1)} %refs_0_.1, ...), custom_call_target="tpu_custom_call" | custom-call | tf_op jit(solution)/shard_map/pallas_call | solution.py:256
  1.1 4.0 %collective-permute-start.7 = (bf16[64,128]{1,0:T(8,128)(2,1)S(1)}, bf16[64,128]{1,0:T(8,128)(2,1)S(1)}, u32[]{:S(2)}, u32[]{:S(2)}) collective-permute-start(bf16[64,128]{1,0:T(8,128)(2,1)S(1)} %get-tuple-element.71), channel_id=1, source_target_pairs={{0,3},{1,2},{2,1},{3,0},{4,7},{5,6},{6,5},{7,4},{8,11},{9,10},{10,... | collective-permute-start | bytes 49160 | tf_op jit(solution)/shard_map/ppermute | solution.py:275
  5.1 0.5 %collective-permute-start.8 = (bf16[64,128]{1,0:T(8,128)(2,1)S(1)}, bf16[64,128]{1,0:T(8,128)(2,1)S(1)}, u32[]{:S(2)}, u32[]{:S(2)}) collective-permute-start(bf16[64,128]{1,0:T(8,128)(2,1)S(1)} %get-tuple-element.72), channel_id=1, source_target_pairs={{0,1},{1,0},{2,3},{3,2},{4,5},{5,4},{6,7},{7,6},{8,9},{9,8},{10,11... | collective-permute-start | bytes 49160 | tf_op jit(solution)/shard_map/ppermute | solution.py:275
  5.7 0.1 collective-permute-start.9
  5.8 2.9 %collective-permute-start.6 = (bf16[224,128]{1,0:T(8,128)(2,1)S(1)}, bf16[224,128]{1,0:T(8,128)(2,1)S(1)}, u32[]{:S(2)}, u32[]{:S(2)}) collective-permute-start(bf16[224,128]{1,0:T(8,128)(2,1)S(1)} %get-tuple-element.68), channel_id=1, source_target_pairs={{0,4},{1,5},{2,6},{3,7},{4,0},{5,1},{6,2},{7,3},{8,12},{9,13},{10,... | collective-permute-start | bytes 172040 | tf_op jit(solution)/shard_map/ppermute | solution.py:275
  8.7 0.0 collective-permute-done.7.refs_0_
  8.7 0.2 collective-permute-done.8.refs_1_
  8.9 0.5 %collective-permute-done.9.refs_2_ = bf16[64,128]{1,0:T(8,128)(2,1)S(1)} collective-permute-done((bf16[64,128]{1,0:T(8,128)(2,1)S(1)}, bf16[64,128]{1,0:T(8,128)(2,1)S(1)}, u32[]{:S(2)}, u32[]{:S(2)}) %collective-permute-start.9) | collective-permute-done | bytes 16416 | tf_op jit(solution)/shard_map/ppermute | solution.py:275
  9.4 0.5 %shard_map.66 = bf16[224,128]{1,0:T(8,128)(2,1)S(1)} custom-call(bf16[256,256]{1,0:T(8,128)(2,1)S(1)} %get-tuple-element.66.table_ref, f32[32,1024]{1,0:T(8,128)S(1)} %get-tuple-element.67.own_ref, bf16[64,128]{1,0:T(8,128)(2,1)S(1)} %collective-permute-done.7.refs_0_, bf16[64,128]{1,0:T(8,128)(2,1)S(1)} %collective-permute-done.8.refs_1_, ...), custom_call_target="tpu_custom_call" | custom-call | tf_op jit(solution)/shard_map/pallas_call | solution.py:256
  9.9 2.1 %collective-permute-start.10 = (bf16[224,128]{1,0:T(8,128)(2,1)S(1)}, bf16[224,128]{1,0:T(8,128)(2,1)S(1)}, u32[]{:S(2)}, u32[]{:S(2)}) collective-permute-start(bf16[224,128]{1,0:T(8,128)(2,1)S(1)} %shard_map.66), channel_id=1, source_target_pairs={{0,4},{1,5},{2,6},{3,7},{4,0},{5,1},{6,2},{7,3},{8,12},{9,13},{10,... | collective-permute-start | bytes 172040 | tf_op jit(solution)/shard_map/ppermute | solution.py:275
  12.0 0.0 collective-permute-done.6.other_ref
  12.0 0.8 %shard_map.65 = (bf16[64,128]{1,0:T(8,128)(2,1)S(1)}, bf16[64,128]{1,0:T(8,128)(2,1)S(1)}, bf16[64,128]{1,0:T(8,128)(2,1)S(1)}, bf16[64,128]{1,0:T(8,128)(2,1)S(...) custom-call(bf16[256,256]{1,0:T(8,128)(2,1)S(1)} %get-tuple-element., ...), custom_call_target="tpu_custom_call" | custom-call | tf_op jit(solution)/shard_map/pallas_call | solution.py:256
  12.8 6.5 %conditional.2 = (bf16[256,128]{1,0:T(8,128)(2,1)S(1)}) conditional(s32[]{:T(128)} %convert_element_type.4, bf16[256,128]{1,0:T(8,128)(2,1)S(1)} %get-tuple-element.69.gated_ref, (bf16[64,128]{1,0:T(8,128)(2,1)S(1)}, bf16[64,128]{1,0:T(8,128)(2,1)S(1)}, bf16[64,128]{1,0:T(8,128)(2,1)S(1)}, bf16[64,128]{1,0:T(8,128)(2,1)S(1)}) %tuple.18), branch_computations={%region_0.0_spmd, %region_1.0_spmd} | conditional | bytes 196736 | solution.py:327
  12.8 2.2 %collective-permute-start = (bf16[64,128]{1,0:T(8,128)(2,1)S(1)}, bf16[64,128]{1,0:T(8,128)(2,1)S(1)}, u32[]{:S(2)}, u32[]{:S(2)}) collective-permute-start(bf16[64,128]{1,0:T(8,128)(2,1)S(1)} %get-tuple-element.33), channel_id=1, source_target_pairs={{0,3},{1,2},{2,1},{3,0},{4,7},{5,6},{6,5},{7,4},{8,11},{9,10},{10,... | collective-permute-start | bytes 49160 | tf_op jit(solution)/shard_map/cond/branch_1_fun/ppermute | solution.py:275
  15.0 0.5 %collective-permute-start.1 = (bf16[64,128]{1,0:T(8,128)(2,1)S(1)}, bf16[64,128]{1,0:T(8,128)(2,1)S(1)}, u32[]{:S(2)}, u32[]{:S(2)}) collective-permute-start(bf16[64,128]{1,0:T(8,128)(2,1)S(1)} %get-tuple-element.34), channel_id=1, source_target_pairs={{0,1},{1,0},{2,3},{3,2},{4,5},{5,4},{6,7},{7,6},{8,9},{9,8},{10,11... | collective-permute-start | bytes 49160 | tf_op jit(solution)/shard_map/cond/branch_1_fun/ppermute | solution.py:275
  15.5 0.9 %collective-permute-start.2 = (bf16[64,128]{1,0:T(8,128)(2,1)S(1)}, bf16[64,128]{1,0:T(8,128)(2,1)S(1)}, u32[]{:S(2)}, u32[]{:S(2)}) collective-permute-start(bf16[64,128]{1,0:T(8,128)(2,1)S(1)} %get-tuple-element.35), channel_id=1, source_target_pairs={{0,2},{1,3},{2,0},{3,1},{4,6},{5,7},{6,4},{7,5},{8,10},{9,11},{10,... | collective-permute-start | bytes 49160 | tf_op jit(solution)/shard_map/cond/branch_1_fun/ppermute | solution.py:275
  16.4 1.1 %collective-permute-done.refs_0_ = bf16[64,128]{1,0:T(8,128)(2,1)S(1)} collective-permute-done((bf16[64,128]{1,0:T(8,128)(2,1)S(1)}, bf16[64,128]{1,0:T(8,128)(2,1)S(1)}, u32[]{:S(2)}, u32[]{:S(2)}) %collective-permute-start) | collective-permute-done | bytes 16416 | tf_op jit(solution)/shard_map/cond/branch_1_fun/ppermute | solution.py:275
  17.5 1.2 %collective-permute-done.1.refs_1_ = bf16[64,128]{1,0:T(8,128)(2,1)S(1)} collective-permute-done((bf16[64,128]{1,0:T(8,128)(2,1)S(1)}, bf16[64,128]{1,0:T(8,128)(2,1)S(1)}, u32[]{:S(2)}, u32[]{:S(2)}) %collective-permute-start.1) | collective-permute-done | bytes 16416 | tf_op jit(solution)/shard_map/cond/branch_1_fun/ppermute | solution.py:275
  18.7 0.5 %collective-permute-done.2.refs_2_ = bf16[64,128]{1,0:T(8,128)(2,1)S(1)} collective-permute-done((bf16[64,128]{1,0:T(8,128)(2,1)S(1)}, bf16[64,128]{1,0:T(8,128)(2,1)S(1)}, u32[]{:S(2)}, u32[]{:S(2)}) %collective-permute-start.2) | collective-permute-done | bytes 16416 | tf_op jit(solution)/shard_map/cond/branch_1_fun/ppermute | solution.py:275
  19.3 0.0 collective-permute-done.10
  19.3 0.7 %shard_map.67 = bf16[256,128]{1,0:T(8,128)(2,1)} custom-call(bf16[256,128]{1,0:T(8,128)(2,1)S(1)} %get-tuple-element.65.queries_ref, f32[256,128]{1,0:T(8,128)S(1)} %get-tuple-element.75.skipped_ref, bf16[256,128]{1,0:T(8,128)(2,1)S(1)} %get-tuple-element.84.convolved_ref), custom_call_target="tpu_custom_call" | custom-call | tf_op jit(solution)/shard_map/pallas_call | solution.py:256
  (3 shorter events, 0.0 us)
Async XLA Ops:
  1.1 7.6 %collective-permute-start.7 = (bf16[64,128]{1,0:T(8,128)(2,1)S(1)}, bf16[64,128]{1,0:T(8,128)(2,1)S(1)}, u32[]{:S(2)}, u32[]{:S(2)}) collective-permute-start(bf16[64,128]{1,0:T(8,128)(2,1)S(1)} %get-tuple-element.71), channel_id=1, source_target_pairs={{0,3},{1,2},{2,1},{3,0},{4,7},{5,6},{6,5},{7,4},{8,11},{9,10},{10,... | collective-permute-start | bytes 49160 | tf_op jit(solution)/shard_map/ppermute | solution.py:275
  5.1 3.7 %collective-permute-start.8 = (bf16[64,128]{1,0:T(8,128)(2,1)S(1)}, bf16[64,128]{1,0:T(8,128)(2,1)S(1)}, u32[]{:S(2)}, u32[]{:S(2)}) collective-permute-start(bf16[64,128]{1,0:T(8,128)(2,1)S(1)} %get-tuple-element.72), channel_id=1, source_target_pairs={{0,1},{1,0},{2,3},{3,2},{4,5},{5,4},{6,7},{7,6},{8,9},{9,8},{10,11... | collective-permute-start | bytes 49160 | tf_op jit(solution)/shard_map/ppermute | solution.py:275
  5.7 3.7 %collective-permute-start.9 = (bf16[64,128]{1,0:T(8,128)(2,1)S(1)}, bf16[64,128]{1,0:T(8,128)(2,1)S(1)}, u32[]{:S(2)}, u32[]{:S(2)}) collective-permute-start(bf16[64,128]{1,0:T(8,128)(2,1)S(1)} %get-tuple-element.73), channel_id=1, source_target_pairs={{0,2},{1,3},{2,0},{3,1},{4,6},{5,7},{6,4},{7,5},{8,10},{9,11},{10,... | collective-permute-start | bytes 49160 | tf_op jit(solution)/shard_map/ppermute | solution.py:275
  5.8 6.2 %collective-permute-start.6 = (bf16[224,128]{1,0:T(8,128)(2,1)S(1)}, bf16[224,128]{1,0:T(8,128)(2,1)S(1)}, u32[]{:S(2)}, u32[]{:S(2)}) collective-permute-start(bf16[224,128]{1,0:T(8,128)(2,1)S(1)} %get-tuple-element.68), channel_id=1, source_target_pairs={{0,4},{1,5},{2,6},{3,7},{4,0},{5,1},{6,2},{7,3},{8,12},{9,13},{10,... | collective-permute-start | bytes 172040 | tf_op jit(solution)/shard_map/ppermute | solution.py:275
  9.9 9.3 %collective-permute-start.10 = (bf16[224,128]{1,0:T(8,128)(2,1)S(1)}, bf16[224,128]{1,0:T(8,128)(2,1)S(1)}, u32[]{:S(2)}, u32[]{:S(2)}) collective-permute-start(bf16[224,128]{1,0:T(8,128)(2,1)S(1)} %shard_map.66), channel_id=1, source_target_pairs={{0,4},{1,5},{2,6},{3,7},{4,0},{5,1},{6,2},{7,3},{8,12},{9,13},{10,... | collective-permute-start | bytes 172040 | tf_op jit(solution)/shard_map/ppermute | solution.py:275
  12.8 4.7 %collective-permute-start = (bf16[64,128]{1,0:T(8,128)(2,1)S(1)}, bf16[64,128]{1,0:T(8,128)(2,1)S(1)}, u32[]{:S(2)}, u32[]{:S(2)}) collective-permute-start(bf16[64,128]{1,0:T(8,128)(2,1)S(1)} %get-tuple-element.33), channel_id=1, source_target_pairs={{0,3},{1,2},{2,1},{3,0},{4,7},{5,6},{6,5},{7,4},{8,11},{9,10},{10,... | collective-permute-start | bytes 49160 | tf_op jit(solution)/shard_map/cond/branch_1_fun/ppermute | solution.py:275
  15.0 3.7 %collective-permute-start.1 = (bf16[64,128]{1,0:T(8,128)(2,1)S(1)}, bf16[64,128]{1,0:T(8,128)(2,1)S(1)}, u32[]{:S(2)}, u32[]{:S(2)}) collective-permute-start(bf16[64,128]{1,0:T(8,128)(2,1)S(1)} %get-tuple-element.34), channel_id=1, source_target_pairs={{0,1},{1,0},{2,3},{3,2},{4,5},{5,4},{6,7},{7,6},{8,9},{9,8},{10,11... | collective-permute-start | bytes 49160 | tf_op jit(solution)/shard_map/cond/branch_1_fun/ppermute | solution.py:275
  15.5 3.7 %collective-permute-start.2 = (bf16[64,128]{1,0:T(8,128)(2,1)S(1)}, bf16[64,128]{1,0:T(8,128)(2,1)S(1)}, u32[]{:S(2)}, u32[]{:S(2)}) collective-permute-start(bf16[64,128]{1,0:T(8,128)(2,1)S(1)} %get-tuple-element.35), channel_id=1, source_target_pairs={{0,2},{1,3},{2,0},{3,1},{4,6},{5,7},{6,4},{7,5},{8,10},{9,11},{10,... | collective-permute-start | bytes 49160 | tf_op jit(solution)/shard_map/cond/branch_1_fun/ppermute | solution.py:275

commit v6 on v5

--- a/solution.py
+++ b/solution.py
@@ -109,11 +109,9 @@
             out_ref[j, part, block:] = total[1]
 
 
-def prepare_kernel(*refs):
-    sources, targets, (gated_ref, coarse_ref) = refs[:6], refs[6:10], refs[10:12]
-    sends, (keys_ref, values_ref, sem) = refs[12:-3], refs[-3:]
-    near_ref, block = targets[0], gated_ref.shape[1]
-    half, group = place()
+def gate_kernel(*refs):
+    sources, targets, gated_ref = refs[:4], refs[4:6], refs[6]
+    sends, (keys_ref, values_ref, sem) = refs[7:-3], refs[-3:]
     copies = [
         pltpu.make_async_copy(source, target, sem.at[i])
         for i, (source, target) in enumerate(zip(sources, (keys_ref, values_ref, *targets)))
@@ -126,22 +124,29 @@
         keys_ref[...].astype(jnp.float32) * values_ref[...].astype(jnp.float32)
     ).astype(jnp.bfloat16)
     groups = len(sends)
+    _, group = place()
     rows = sends[0].shape[0] // HALVES
     for k, send_ref in enumerate(sends):
         for part in range(HALVES):
             send_ref[part * rows : (part + 1) * rows, :] = gated_ref[
                 span(part * groups + (group ^ k), rows), :
             ]
-    copies[2].wait()
-    coarse_ref[:rows, :] = sends[0][span(1 - half, rows), :]
+    for copy in copies[2:]:
+        copy.wait()
+
+
+def coarse_kernel(near_ref, stays_ref, coarse_ref):
+    half, _ = place()
+    chans, block = stays_ref.shape
+    rows = chans // HALVES
+    groups = near_ref.shape[1] // block // HALVES
+    coarse_ref[:rows, :] = stays_ref[span(1 - half, rows), :]
     for m in range(groups):
         parts = split(near_ref[:, m * block : (m + 1) * block])
         coarse_ref[(m + 1) * rows : (m + 2) * rows, :] = parts[0]
         at = (groups + 1 + m) * rows
         if at < coarse_ref.shape[0]:
             coarse_ref[at : at + rows, :] = parts[1]
-    for copy in copies[3:]:
-        copy.wait()
 
 
 def lead_kernel(table_ref, own_ref, *refs):
@@ -281,16 +286,15 @@
     outputs = ((shards, rows, block), f32)
     scratch = lambda *shapes: [pltpu.VMEM(*shape) for shape in shapes]
 
-    near = (filters, skip, table, queries)
-    own, skip, table, queries, gated, coarse, *sends = call(
-        prepare_kernel,
-        [(x.shape, x.dtype) for x in near]
-        + [whole, across_part]
-        + [group_part] * groups,
-        (keys, values, *near),
-        scratch(whole, whole) + [pltpu.SemaphoreType.DMA((6,))],
-        6,
-    )
+    queries, skip, gated, *sends = call(
+        gate_kernel,
+        [whole, (skip.shape, f32), whole] + [group_part] * groups,
+        (keys, values, queries, skip),
+        scratch(whole, whole) + [pltpu.SemaphoreType.DMA((4,))],
+        4,
+    )
+    own = filters
+    (coarse,) = call(coarse_kernel, [across_part], (own, sends[0]))
     other = swap(coarse, groups)
     arrived = [swap(sends[k], k) if k else sends[k] for k in partners(groups)]
     (lead,) = call(

time: 20.1 us -> 20 us (level)
    pallas_call x6 -> x7, Pallas kernels: 3.05 us -> 2.94 us  [call(): pl.pallas_call(kernel, out_shape=[jax.ShapeDtypeStruct(shape, dtype) for...]
  transfers between devices with their start and end apart: 8 -> 8, of which waited for: 5 -> 5; matrix products, arithmetic and copies ran while one was open for 0% -> 0% of each run, Pallas kernels for 6% -> 7%
where the time goes in v6:
time: 20 us; the launch traced here: 19.9 us
  starting transfers between devices  13.3 us (66%)
  waiting for transfers between devices  3.56 us (18%)
  Pallas kernels  2.94 us (15%)
    ppermute x8, starting transfers between devices, per_device(): lax.ppermute(x, AXIS, [(i, i ^ k) for i in range(shards)])  13.3 us
    ppermute x8, waiting for transfers between devices, per_device(): lax.ppermute(x, AXIS, [(i, i ^ k) for i in range(shards)])  3.56 us
    pallas_call x7, Pallas kernels, call(): pl.pallas_call(kernel, out_shape=[jax.ShapeDtypeStruct(shape, dtype) for...  2.94 us
  transfers between devices with their start and end apart: 8, of which 5 were waited for; matrix products, arithmetic and copies ran while one was open for 0% of the time, Pallas kernels for 7%

profile of v6, /device:TPU:0, one launch (start us, length us, event | category | flops | bytes accessed | tf_op | source)
XLA Modules:
  0.0 19.9 jit_solution(5253269156166141954)
XLA Ops:
  0.0 0.0 copy-start
  0.0 1.0 %shard_map.64 = (bf16[256,128]{1,0:T(8,128)(2,1)S(1)}, f32[256]{0:T(256)S(1)}, bf16[256,128]{1,0:T(8,128)(2,1)S(1)}, bf16[64,128]{1,0:T(8,128)(2,1)S(1)}, bf16[6...) custom-call(bf16[256,128]{1,0:T(8,128)(2,1)} %refs_0_.1, ...), custom_call_target="tpu_custom_call" | custom-call | tf_op jit(solution)/shard_map/pallas_call | solution.py:261
  1.0 0.0 copy-start.1
  1.0 4.0 %collective-permute-start.7 = (bf16[64,128]{1,0:T(8,128)(2,1)S(1)}, bf16[64,128]{1,0:T(8,128)(2,1)S(1)}, u32[]{:S(2)}, u32[]{:S(2)}) collective-permute-start(bf16[64,128]{1,0:T(8,128)(2,1)S(1)} %get-tuple-element.66), channel_id=1, source_target_pairs={{0,3},{1,2},{2,1},{3,0},{4,7},{5,6},{6,5},{7,4},{8,11},{9,10},{10,... | collective-permute-start | bytes 49160 | tf_op jit(solution)/shard_map/ppermute | solution.py:280
  5.0 0.5 %collective-permute-start.8 = (bf16[64,128]{1,0:T(8,128)(2,1)S(1)}, bf16[64,128]{1,0:T(8,128)(2,1)S(1)}, u32[]{:S(2)}, u32[]{:S(2)}) collective-permute-start(bf16[64,128]{1,0:T(8,128)(2,1)S(1)} %get-tuple-element.67), channel_id=1, source_target_pairs={{0,1},{1,0},{2,3},{3,2},{4,5},{5,4},{6,7},{7,6},{8,9},{9,8},{10,11... | collective-permute-start | bytes 49160 | tf_op jit(solution)/shard_map/ppermute | solution.py:280
  5.5 0.1 collective-permute-start.9
  5.7 0.0 copy-done
  5.7 3.0 %collective-permute-start.6 = (bf16[224,128]{1,0:T(8,128)(2,1)S(1)}, bf16[224,128]{1,0:T(8,128)(2,1)S(1)}, u32[]{:S(2)}, u32[]{:S(2)}) collective-permute-start(bf16[224,128]{1,0:T(8,128)(2,1)S(1)} %shard_map.65), channel_id=1, source_target_pairs={{0,4},{1,5},{2,6},{3,7},{4,0},{5,1},{6,2},{7,3},{8,12},{9,13},{10,... | collective-permute-start | bytes 172040 | tf_op jit(solution)/shard_map/ppermute | solution.py:280
  8.7 0.0 collective-permute-done.7.refs_0_
  8.7 0.1 collective-permute-done.8.refs_1_
  8.8 0.6 %collective-permute-done.9.refs_2_ = bf16[64,128]{1,0:T(8,128)(2,1)S(1)} collective-permute-done((bf16[64,128]{1,0:T(8,128)(2,1)S(1)}, bf16[64,128]{1,0:T(8,128)(2,1)S(1)}, u32[]{:S(2)}, u32[]{:S(2)}) %collective-permute-start.9) | collective-permute-done | bytes 16416 | tf_op jit(solution)/shard_map/ppermute | solution.py:280
  9.3 0.0 copy-done.1
  9.3 0.5 %shard_map.67 = bf16[224,128]{1,0:T(8,128)(2,1)S(1)} custom-call(bf16[256,256]{1,0:T(8,128)(2,1)S(1)} %copy-done.1, f32[32,1024]{1,0:T(8,128)S(1)} %copy-done, bf16[64,128]{1,0:T(8,128)(2,1)S(1)} %collective-permute-done.7.refs_0_, bf16[64,128]{1,0:T(8,128)(2,1)S(1)} %collective-permute-done.8.refs_1_, bf16[64,128]{1,0:T(8,128)(2,1)S(1)} %collective-permute-done.9.refs_2_, ...), custom_call_target="tpu_custom_call" | custom-call | tf_op jit(solution)/shard_map/pallas_call | solution.py:261
  9.8 2.1 %collective-permute-start.10 = (bf16[224,128]{1,0:T(8,128)(2,1)S(1)}, bf16[224,128]{1,0:T(8,128)(2,1)S(1)}, u32[]{:S(2)}, u32[]{:S(2)}) collective-permute-start(bf16[224,128]{1,0:T(8,128)(2,1)S(1)} %shard_map.67), channel_id=1, source_target_pairs={{0,4},{1,5},{2,6},{3,7},{4,0},{5,1},{6,2},{7,3},{8,12},{9,13},{10,... | collective-permute-start | bytes 172040 | tf_op jit(solution)/shard_map/ppermute | solution.py:280
  11.9 0.0 collective-permute-done.6.other_ref
  11.9 0.8 %shard_map.66 = (bf16[64,128]{1,0:T(8,128)(2,1)S(1)}, bf16[64,128]{1,0:T(8,128)(2,1)S(1)}, bf16[64,128]{1,0:T(8,128)(2,1)S(1)}, bf16[64,128]{1,0:T(8,128)(2,1)S(...) custom-call(bf16[256,256]{1,0:T(8,128)(2,1)S(1)} %copy-done.1, ...), custom_call_target="tpu_custom_call" | custom-call | tf_op jit(solution)/shard_map/pallas_call | solution.py:261
  12.7 6.5 %conditional.2 = (bf16[256,128]{1,0:T(8,128)(2,1)S(1)}) conditional(s32[]{:T(128)} %convert_element_type.4, bf16[256,128]{1,0:T(8,128)(2,1)S(1)} %get-tuple-element.64.gated_ref, (bf16[64,128]{1,0:T(8,128)(2,1)S(1)}, bf16[64,128]{1,0:T(8,128)(2,1)S(1)}, bf16[64,128]{1,0:T(8,128)(2,1)S(1)}, bf16[64,128]{1,0:T(8,128)(2,1)S(1)}) %tuple.18), branch_computations={%region_0.0_spmd, %region_1.0_spmd} | conditional | bytes 196736 | solution.py:331
  12.7 2.2 %collective-permute-start = (bf16[64,128]{1,0:T(8,128)(2,1)S(1)}, bf16[64,128]{1,0:T(8,128)(2,1)S(1)}, u32[]{:S(2)}, u32[]{:S(2)}) collective-permute-start(bf16[64,128]{1,0:T(8,128)(2,1)S(1)} %get-tuple-element.33), channel_id=1, source_target_pairs={{0,3},{1,2},{2,1},{3,0},{4,7},{5,6},{6,5},{7,4},{8,11},{9,10},{10,... | collective-permute-start | bytes 49160 | tf_op jit(solution)/shard_map/cond/branch_1_fun/ppermute | solution.py:280
  14.9 0.5 %collective-permute-start.1 = (bf16[64,128]{1,0:T(8,128)(2,1)S(1)}, bf16[64,128]{1,0:T(8,128)(2,1)S(1)}, u32[]{:S(2)}, u32[]{:S(2)}) collective-permute-start(bf16[64,128]{1,0:T(8,128)(2,1)S(1)} %get-tuple-element.34), channel_id=1, source_target_pairs={{0,1},{1,0},{2,3},{3,2},{4,5},{5,4},{6,7},{7,6},{8,9},{9,8},{10,11... | collective-permute-start | bytes 49160 | tf_op jit(solution)/shard_map/cond/branch_1_fun/ppermute | solution.py:280
  15.4 0.8 %collective-permute-start.2 = (bf16[64,128]{1,0:T(8,128)(2,1)S(1)}, bf16[64,128]{1,0:T(8,128)(2,1)S(1)}, u32[]{:S(2)}, u32[]{:S(2)}) collective-permute-start(bf16[64,128]{1,0:T(8,128)(2,1)S(1)} %get-tuple-element.35), channel_id=1, source_target_pairs={{0,2},{1,3},{2,0},{3,1},{4,6},{5,7},{6,4},{7,5},{8,10},{9,11},{10,... | collective-permute-start | bytes 49160 | tf_op jit(solution)/shard_map/cond/branch_1_fun/ppermute | solution.py:280
  16.2 1.1 %collective-permute-done.refs_0_ = bf16[64,128]{1,0:T(8,128)(2,1)S(1)} collective-permute-done((bf16[64,128]{1,0:T(8,128)(2,1)S(1)}, bf16[64,128]{1,0:T(8,128)(2,1)S(1)}, u32[]{:S(2)}, u32[]{:S(2)}) %collective-permute-start) | collective-permute-done | bytes 16416 | tf_op jit(solution)/shard_map/cond/branch_1_fun/ppermute | solution.py:280
  17.4 1.2 %collective-permute-done.1.refs_1_ = bf16[64,128]{1,0:T(8,128)(2,1)S(1)} collective-permute-done((bf16[64,128]{1,0:T(8,128)(2,1)S(1)}, bf16[64,128]{1,0:T(8,128)(2,1)S(1)}, u32[]{:S(2)}, u32[]{:S(2)}) %collective-permute-start.1) | collective-permute-done | bytes 16416 | tf_op jit(solution)/shard_map/cond/branch_1_fun/ppermute | solution.py:280
  18.6 0.5 %collective-permute-done.2.refs_2_ = bf16[64,128]{1,0:T(8,128)(2,1)S(1)} collective-permute-done((bf16[64,128]{1,0:T(8,128)(2,1)S(1)}, bf16[64,128]{1,0:T(8,128)(2,1)S(1)}, u32[]{:S(2)}, u32[]{:S(2)}) %collective-permute-start.2) | collective-permute-done | bytes 16416 | tf_op jit(solution)/shard_map/cond/branch_1_fun/ppermute | solution.py:280
  19.2 0.0 collective-permute-done.10
  19.2 0.7 %shard_map.68 = bf16[256,128]{1,0:T(8,128)(2,1)} custom-call(bf16[256,128]{1,0:T(8,128)(2,1)S(1)} %get-tuple-element.62.queries_ref, f32[256,128]{1,0:T(8,128)S(1)} %get-tuple-element.69.skipped_ref, bf16[256,128]{1,0:T(8,128)(2,1)S(1)} %get-tuple-element.78.convolved_ref), custom_call_target="tpu_custom_call" | custom-call | tf_op jit(solution)/shard_map/pallas_call | solution.py:261
  (4 shorter events, 0.1 us)
Async XLA Ops:
  0.0 5.7 %copy-start = (f32[32,1024]{1,0:T(8,128)S(1)}, f32[32,1024]{1,0:T(8,128)}, u32[]{:S(2)}) copy-start(f32[32,1024]{1,0:T(8,128)} %own_ref.3) | copy-start | bytes 393220
  1.0 8.3 %copy-start.1 = (bf16[256,256]{1,0:T(8,128)(2,1)S(1)}, bf16[256,256]{1,0:T(8,128)(2,1)}, u32[]{:S(2)}) copy-start(bf16[256,256]{1,0:T(8,128)(2,1)} %constant.8.clone.table_ref) | copy-start | bytes 393220
  1.0 7.7 %collective-permute-start.7 = (bf16[64,128]{1,0:T(8,128)(2,1)S(1)}, bf16[64,128]{1,0:T(8,128)(2,1)S(1)}, u32[]{:S(2)}, u32[]{:S(2)}) collective-permute-start(bf16[64,128]{1,0:T(8,128)(2,1)S(1)} %get-tuple-element.66), channel_id=1, source_target_pairs={{0,3},{1,2},{2,1},{3,0},{4,7},{5,6},{6,5},{7,4},{8,11},{9,10},{10,... | collective-permute-start | bytes 49160 | tf_op jit(solution)/shard_map/ppermute | solution.py:280
  5.0 3.7 %collective-permute-start.8 = (bf16[64,128]{1,0:T(8,128)(2,1)S(1)}, bf16[64,128]{1,0:T(8,128)(2,1)S(1)}, u32[]{:S(2)}, u32[]{:S(2)}) collective-permute-start(bf16[64,128]{1,0:T(8,128)(2,1)S(1)} %get-tuple-element.67), channel_id=1, source_target_pairs={{0,1},{1,0},{2,3},{3,2},{4,5},{5,4},{6,7},{7,6},{8,9},{9,8},{10,11... | collective-permute-start | bytes 49160 | tf_op jit(solution)/shard_map/ppermute | solution.py:280
  5.5 3.8 %collective-permute-start.9 = (bf16[64,128]{1,0:T(8,128)(2,1)S(1)}, bf16[64,128]{1,0:T(8,128)(2,1)S(1)}, u32[]{:S(2)}, u32[]{:S(2)}) collective-permute-start(bf16[64,128]{1,0:T(8,128)(2,1)S(1)} %get-tuple-element.68), channel_id=1, source_target_pairs={{0,2},{1,3},{2,0},{3,1},{4,6},{5,7},{6,4},{7,5},{8,10},{9,11},{10,... | collective-permute-start | bytes 49160 | tf_op jit(solution)/shard_map/ppermute | solution.py:280
  5.7 6.2 %collective-permute-start.6 = (bf16[224,128]{1,0:T(8,128)(2,1)S(1)}, bf16[224,128]{1,0:T(8,128)(2,1)S(1)}, u32[]{:S(2)}, u32[]{:S(2)}) collective-permute-start(bf16[224,128]{1,0:T(8,128)(2,1)S(1)} %shard_map.65), channel_id=1, source_target_pairs={{0,4},{1,5},{2,6},{3,7},{4,0},{5,1},{6,2},{7,3},{8,12},{9,13},{10,... | collective-permute-start | bytes 172040 | tf_op jit(solution)/shard_map/ppermute | solution.py:280
  9.8 9.4 %collective-permute-start.10 = (bf16[224,128]{1,0:T(8,128)(2,1)S(1)}, bf16[224,128]{1,0:T(8,128)(2,1)S(1)}, u32[]{:S(2)}, u32[]{:S(2)}) collective-permute-start(bf16[224,128]{1,0:T(8,128)(2,1)S(1)} %shard_map.67), channel_id=1, source_target_pairs={{0,4},{1,5},{2,6},{3,7},{4,0},{5,1},{6,2},{7,3},{8,12},{9,13},{10,... | collective-permute-start | bytes 172040 | tf_op jit(solution)/shard_map/ppermute | solution.py:280
  12.7 4.7 %collective-permute-start = (bf16[64,128]{1,0:T(8,128)(2,1)S(1)}, bf16[64,128]{1,0:T(8,128)(2,1)S(1)}, u32[]{:S(2)}, u32[]{:S(2)}) collective-permute-start(bf16[64,128]{1,0:T(8,128)(2,1)S(1)} %get-tuple-element.33), channel_id=1, source_target_pairs={{0,3},{1,2},{2,1},{3,0},{4,7},{5,6},{6,5},{7,4},{8,11},{9,10},{10,... | collective-permute-start | bytes 49160 | tf_op jit(solution)/shard_map/cond/branch_1_fun/ppermute | solution.py:280
  14.9 3.7 %collective-permute-start.1 = (bf16[64,128]{1,0:T(8,128)(2,1)S(1)}, bf16[64,128]{1,0:T(8,128)(2,1)S(1)}, u32[]{:S(2)}, u32[]{:S(2)}) collective-permute-start(bf16[64,128]{1,0:T(8,128)(2,1)S(1)} %get-tuple-element.34), channel_id=1, source_target_pairs={{0,1},{1,0},{2,3},{3,2},{4,5},{5,4},{6,7},{7,6},{8,9},{9,8},{10,11... | collective-permute-start | bytes 49160 | tf_op jit(solution)/shard_map/cond/branch_1_fun/ppermute | solution.py:280
  15.4 3.7 %collective-permute-start.2 = (bf16[64,128]{1,0:T(8,128)(2,1)S(1)}, bf16[64,128]{1,0:T(8,128)(2,1)S(1)}, u32[]{:S(2)}, u32[]{:S(2)}) collective-permute-start(bf16[64,128]{1,0:T(8,128)(2,1)S(1)} %get-tuple-element.35), channel_id=1, source_target_pairs={{0,2},{1,3},{2,0},{3,1},{4,6},{5,7},{6,4},{7,5},{8,10},{9,11},{10,... | collective-permute-start | bytes 49160 | tf_op jit(solution)/shard_map/cond/branch_1_fun/ppermute | solution.py:280

commit v7 on v6

--- a/solution.py
+++ b/solution.py
@@ -82,8 +82,9 @@
 def back_from(spectra, table_ref):
     block = spectra.shape[1] // 2
     high, low = split(spectra)
-    top, rest = table_ref[:block, :], table_ref[block:, :]
-    total = dot(high, top, True) + dot(low, top, True) + dot(high, rest, True)
+    both = dot(jnp.concatenate([high, low], axis=0), table_ref[...], True)
+    count = len(high)
+    total = both[:count, :block] + both[count:, :block] + both[:count, block:]
     return total * (1.0 / block)
 
 

time: 20 us -> 20.1 us (level)
  the two profiles are of different devices: /device:TPU:0 before, /device:TPU:24 now
where the time goes in v7:
time: 20.1 us; the launch traced here: 19.9 us
  starting transfers between devices  8.93 us (44%)
  waiting for transfers between devices  8.25 us (41%)
  Pallas kernels  2.64 us (13%)
    ppermute x8, starting transfers between devices, per_device(): lax.ppermute(x, AXIS, [(i, i ^ k) for i in range(shards)])  8.93 us
    ppermute x8, waiting for transfers between devices, per_device(): lax.ppermute(x, AXIS, [(i, i ^ k) for i in range(shards)])  8.25 us
    pallas_call x8, Pallas kernels, call(): pl.pallas_call(kernel, out_shape=[jax.ShapeDtypeStruct(shape, dtype) for...  2.64 us
  transfers between devices with their start and end apart: 8, of which 8 were waited for; matrix products, arithmetic and copies ran while one was open for 0% of the time, Pallas kernels for 3%

profile of v7, /device:TPU:24, one launch (start us, length us, event | category | flops | bytes accessed | tf_op | source)
XLA Modules:
  0.0 19.9 jit_solution(9203217955690594734)
XLA Ops:
  0.0 0.0 copy-start
  0.0 1.0 %shard_map.64 = (bf16[256,128]{1,0:T(8,128)(2,1)S(1)}, f32[256]{0:T(256)S(1)}, bf16[256,128]{1,0:T(8,128)(2,1)S(1)}, bf16[64,128]{1,0:T(8,128)(2,1)S(1)}, bf16[6...) custom-call(bf16[256,128]{1,0:T(8,128)(2,1)} %refs_0_.1, ...), custom_call_target="tpu_custom_call" | custom-call | tf_op jit(solution)/shard_map/pallas_call | solution.py:262
  1.0 0.0 copy-start.1
  1.0 1.4 %collective-permute-start.7 = (bf16[64,128]{1,0:T(8,128)(2,1)S(1)}, bf16[64,128]{1,0:T(8,128)(2,1)S(1)}, u32[]{:S(2)}, u32[]{:S(2)}) collective-permute-start(bf16[64,128]{1,0:T(8,128)(2,1)S(1)} %get-tuple-element.66), channel_id=1, source_target_pairs={{0,3},{1,2},{2,1},{3,0},{4,7},{5,6},{6,5},{7,4},{8,11},{9,10},{10,... | collective-permute-start | bytes 49160 | tf_op jit(solution)/shard_map/ppermute | solution.py:281
  2.4 0.5 %collective-permute-start.8 = (bf16[64,128]{1,0:T(8,128)(2,1)S(1)}, bf16[64,128]{1,0:T(8,128)(2,1)S(1)}, u32[]{:S(2)}, u32[]{:S(2)}) collective-permute-start(bf16[64,128]{1,0:T(8,128)(2,1)S(1)} %get-tuple-element.67), channel_id=1, source_target_pairs={{0,1},{1,0},{2,3},{3,2},{4,5},{5,4},{6,7},{7,6},{8,9},{9,8},{10,11... | collective-permute-start | bytes 49160 | tf_op jit(solution)/shard_map/ppermute | solution.py:281
  3.0 1.6 %collective-permute-start.9 = (bf16[64,128]{1,0:T(8,128)(2,1)S(1)}, bf16[64,128]{1,0:T(8,128)(2,1)S(1)}, u32[]{:S(2)}, u32[]{:S(2)}) collective-permute-start(bf16[64,128]{1,0:T(8,128)(2,1)S(1)} %get-tuple-element.68), channel_id=1, source_target_pairs={{0,2},{1,3},{2,0},{3,1},{4,6},{5,7},{6,4},{7,5},{8,10},{9,11},{10,... | collective-permute-start | bytes 49160 | tf_op jit(solution)/shard_map/ppermute | solution.py:281
  4.6 0.0 copy-done
  4.6 0.4 %collective-permute-start.6 = (bf16[224,128]{1,0:T(8,128)(2,1)S(1)}, bf16[224,128]{1,0:T(8,128)(2,1)S(1)}, u32[]{:S(2)}, u32[]{:S(2)}) collective-permute-start(bf16[224,128]{1,0:T(8,128)(2,1)S(1)} %shard_map.65), channel_id=1, source_target_pairs={{0,4},{1,5},{2,6},{3,7},{4,0},{5,1},{6,2},{7,3},{8,12},{9,13},{10,... | collective-permute-start | bytes 172040 | tf_op jit(solution)/shard_map/ppermute | solution.py:281
  5.0 0.7 %collective-permute-done.7.refs_0_ = bf16[64,128]{1,0:T(8,128)(2,1)S(1)} collective-permute-done((bf16[64,128]{1,0:T(8,128)(2,1)S(1)}, bf16[64,128]{1,0:T(8,128)(2,1)S(1)}, u32[]{:S(2)}, u32[]{:S(2)}) %collective-permute-start.7) | collective-permute-done | bytes 16416 | tf_op jit(solution)/shard_map/ppermute | solution.py:281
  5.7 0.5 %collective-permute-done.8.refs_1_ = bf16[64,128]{1,0:T(8,128)(2,1)S(1)} collective-permute-done((bf16[64,128]{1,0:T(8,128)(2,1)S(1)}, bf16[64,128]{1,0:T(8,128)(2,1)S(1)}, u32[]{:S(2)}, u32[]{:S(2)}) %collective-permute-start.8) | collective-permute-done | bytes 16416 | tf_op jit(solution)/shard_map/ppermute | solution.py:281
  6.2 0.5 %collective-permute-done.9.refs_2_ = bf16[64,128]{1,0:T(8,128)(2,1)S(1)} collective-permute-done((bf16[64,128]{1,0:T(8,128)(2,1)S(1)}, bf16[64,128]{1,0:T(8,128)(2,1)S(1)}, u32[]{:S(2)}, u32[]{:S(2)}) %collective-permute-start.9) | collective-permute-done | bytes 16416 | tf_op jit(solution)/shard_map/ppermute | solution.py:281
  6.7 0.0 copy-done.1
  6.7 1.4 %collective-permute-start.10 = (bf16[224,128]{1,0:T(8,128)(2,1)S(1)}, bf16[224,128]{1,0:T(8,128)(2,1)S(1)}, u32[]{:S(2)}, u32[]{:S(2)}) collective-permute-start(bf16[224,128]{1,0:T(8,128)(2,1)S(1)} %shard_map.67), channel_id=1, source_target_pairs={{0,4},{1,5},{2,6},{3,7},{4,0},{5,1},{6,2},{7,3},{8,12},{9,13},{10,... | collective-permute-start | bytes 172040 | tf_op jit(solution)/shard_map/ppermute | solution.py:281
  8.1 2.7 %collective-permute-done.6.other_ref = bf16[224,128]{1,0:T(8,128)(2,1)S(1)} collective-permute-done((bf16[224,128]{1,0:T(8,128)(2,1)S(1)}, bf16[224,128]{1,0:T(8,128)(2,1)S(1)}, u32[]{:S(2)}, u32[]{:S(2)}) %collective-permute-start.6) | collective-permute-done | bytes 57376 | tf_op jit(solution)/shard_map/ppermute | solution.py:281
  10.8 0.6 %shard_map.66 = (bf16[64,128]{1,0:T(8,128)(2,1)S(1)}, bf16[64,128]{1,0:T(8,128)(2,1)S(1)}, bf16[64,128]{1,0:T(8,128)(2,1)S(1)}, bf16[64,128]{1,0:T(8,128)(2,1)S(...) custom-call(bf16[256,256]{1,0:T(8,128)(2,1)S(1)} %copy-done.1, ...), custom_call_target="tpu_custom_call" | custom-call | tf_op jit(solution)/shard_map/pallas_call | solution.py:262
  11.4 0.4 %collective-permute-done.10 = bf16[224,128]{1,0:T(8,128)(2,1)S(1)} collective-permute-done((bf16[224,128]{1,0:T(8,128)(2,1)S(1)}, bf16[224,128]{1,0:T(8,128)(2,1)S(1)}, u32[]{:S(2)}, u32[]{:S(2)}) %collective-permute-start.10) | collective-permute-done | bytes 57376 | tf_op jit(solution)/shard_map/ppermute | solution.py:281
  11.8 7.5 %conditional.3 = (bf16[256,128]{1,0:T(8,128)(2,1)S(1)}) conditional(s32[]{:T(128)} %convert_element_type.4, (bf16[256,256]{1,0:T(8,128)(2,1)S(1)}, f32[8,32,256]{2,1,0:T(8,128)S(1)}, f32[4,32,256]{2,1,0:T(8,128)S(1)}, f32[8,32,128]{2,1,0:T(8,128)S(1)}, bf16[224,128]{1,0:T(8,128)(2,1)S(1)}, /*index=5*/bf16[224,128]{1,0:T(8,128)(2,1)S(1)}) %tuple.23, ...), branch_computations={%region_2.0_spmd, %region_3.0_spmd} | conditional | bytes 196736 | solution.py:333
  11.8 0.4 %branch_0_fun.4 = (bf16[64,128]{1,0:T(8,128)(2,1)S(1)}, bf16[64,128]{1,0:T(8,128)(2,1)S(1)}, bf16[64,128]{1,0:T(8,128)(2,1)S(1)}, bf16[64,128]{1,0:T(8,128)(2,1)S(1)}) custom-call(bf16[256,256]{1,0:T(8,128)(2,1)S(1)} %get-tuple-element.37.table_ref, f32[8,32,256]{2,1,0:T(8,128)S(1)} %get-tuple-element.38.taps_ref, ...), custom_call_target="tpu_custom_call" | custom-call | tf_op jit(solution)/shard_map/cond/branch_0_fun/pallas_call | solution.py:262
  12.2 2.7 %collective-permute-start.3 = (bf16[64,128]{1,0:T(8,128)(2,1)S(1)}, bf16[64,128]{1,0:T(8,128)(2,1)S(1)}, u32[]{:S(2)}, u32[]{:S(2)}) collective-permute-start(bf16[64,128]{1,0:T(8,128)(2,1)S(1)} %get-tuple-element.43), channel_id=1, source_target_pairs={{0,3},{1,2},{2,1},{3,0},{4,7},{5,6},{6,5},{7,4},{8,11},{9,10},{10,... | collective-permute-start | bytes 49160 | tf_op jit(solution)/shard_map/cond/branch_0_fun/ppermute | solution.py:281
  15.0 0.5 %collective-permute-start.4 = (bf16[64,128]{1,0:T(8,128)(2,1)S(1)}, bf16[64,128]{1,0:T(8,128)(2,1)S(1)}, u32[]{:S(2)}, u32[]{:S(2)}) collective-permute-start(bf16[64,128]{1,0:T(8,128)(2,1)S(1)} %get-tuple-element.44), channel_id=1, source_target_pairs={{0,1},{1,0},{2,3},{3,2},{4,5},{5,4},{6,7},{7,6},{8,9},{9,8},{10,11... | collective-permute-start | bytes 49160 | tf_op jit(solution)/shard_map/cond/branch_0_fun/ppermute | solution.py:281
  15.5 0.3 %collective-permute-start.5 = (bf16[64,128]{1,0:T(8,128)(2,1)S(1)}, bf16[64,128]{1,0:T(8,128)(2,1)S(1)}, u32[]{:S(2)}, u32[]{:S(2)}) collective-permute-start(bf16[64,128]{1,0:T(8,128)(2,1)S(1)} %get-tuple-element.45), channel_id=1, source_target_pairs={{0,2},{1,3},{2,0},{3,1},{4,6},{5,7},{6,4},{7,5},{8,10},{9,11},{10,... | collective-permute-start | bytes 49160 | tf_op jit(solution)/shard_map/cond/branch_0_fun/ppermute | solution.py:281
  15.8 1.1 %collective-permute-done.3.refs_0_ = bf16[64,128]{1,0:T(8,128)(2,1)S(1)} collective-permute-done((bf16[64,128]{1,0:T(8,128)(2,1)S(1)}, bf16[64,128]{1,0:T(8,128)(2,1)S(1)}, u32[]{:S(2)}, u32[]{:S(2)}) %collective-permute-start.3) | collective-permute-done | bytes 16416 | tf_op jit(solution)/shard_map/cond/branch_0_fun/ppermute | solution.py:281
  16.9 1.8 %collective-permute-done.4.refs_1_ = bf16[64,128]{1,0:T(8,128)(2,1)S(1)} collective-permute-done((bf16[64,128]{1,0:T(8,128)(2,1)S(1)}, bf16[64,128]{1,0:T(8,128)(2,1)S(1)}, u32[]{:S(2)}, u32[]{:S(2)}) %collective-permute-start.4) | collective-permute-done | bytes 16416 | tf_op jit(solution)/shard_map/cond/branch_0_fun/ppermute | solution.py:281
  18.7 0.5 %collective-permute-done.5.refs_2_ = bf16[64,128]{1,0:T(8,128)(2,1)S(1)} collective-permute-done((bf16[64,128]{1,0:T(8,128)(2,1)S(1)}, bf16[64,128]{1,0:T(8,128)(2,1)S(1)}, u32[]{:S(2)}, u32[]{:S(2)}) %collective-permute-start.5) | collective-permute-done | bytes 16416 | tf_op jit(solution)/shard_map/cond/branch_0_fun/ppermute | solution.py:281
  19.3 0.7 %shard_map.68 = bf16[256,128]{1,0:T(8,128)(2,1)} custom-call(bf16[256,128]{1,0:T(8,128)(2,1)S(1)} %get-tuple-element.62.queries_ref, f32[256,128]{1,0:T(8,128)S(1)} %get-tuple-element.69.skipped_ref, bf16[256,128]{1,0:T(8,128)(2,1)S(1)} %get-tuple-element.78.convolved_ref), custom_call_target="tpu_custom_call" | custom-call | tf_op jit(solution)/shard_map/pallas_call | solution.py:262
  (5 shorter events, 0.1 us)
Async XLA Ops:
  0.0 4.6 %copy-start = (f32[32,1024]{1,0:T(8,128)S(1)}, f32[32,1024]{1,0:T(8,128)}, u32[]{:S(2)}) copy-start(f32[32,1024]{1,0:T(8,128)} %own_ref.3) | copy-start | bytes 393220
  1.0 5.7 %copy-start.1 = (bf16[256,256]{1,0:T(8,128)(2,1)S(1)}, bf16[256,256]{1,0:T(8,128)(2,1)}, u32[]{:S(2)}) copy-start(bf16[256,256]{1,0:T(8,128)(2,1)} %constant.8.clone.table_ref) | copy-start | bytes 393220
  1.0 4.7 %collective-permute-start.7 = (bf16[64,128]{1,0:T(8,128)(2,1)S(1)}, bf16[64,128]{1,0:T(8,128)(2,1)S(1)}, u32[]{:S(2)}, u32[]{:S(2)}) collective-permute-start(bf16[64,128]{1,0:T(8,128)(2,1)S(1)} %get-tuple-element.66), channel_id=1, source_target_pairs={{0,3},{1,2},{2,1},{3,0},{4,7},{5,6},{6,5},{7,4},{8,11},{9,10},{10,... | collective-permute-start | bytes 49160 | tf_op jit(solution)/shard_map/ppermute | solution.py:281
  2.4 3.7 %collective-permute-start.8 = (bf16[64,128]{1,0:T(8,128)(2,1)S(1)}, bf16[64,128]{1,0:T(8,128)(2,1)S(1)}, u32[]{:S(2)}, u32[]{:S(2)}) collective-permute-start(bf16[64,128]{1,0:T(8,128)(2,1)S(1)} %get-tuple-element.67), channel_id=1, source_target_pairs={{0,1},{1,0},{2,3},{3,2},{4,5},{5,4},{6,7},{7,6},{8,9},{9,8},{10,11... | collective-permute-start | bytes 49160 | tf_op jit(solution)/shard_map/ppermute | solution.py:281
  3.0 3.7 %collective-permute-start.9 = (bf16[64,128]{1,0:T(8,128)(2,1)S(1)}, bf16[64,128]{1,0:T(8,128)(2,1)S(1)}, u32[]{:S(2)}, u32[]{:S(2)}) collective-permute-start(bf16[64,128]{1,0:T(8,128)(2,1)S(1)} %get-tuple-element.68), channel_id=1, source_target_pairs={{0,2},{1,3},{2,0},{3,1},{4,6},{5,7},{6,4},{7,5},{8,10},{9,11},{10,... | collective-permute-start | bytes 49160 | tf_op jit(solution)/shard_map/ppermute | solution.py:281
  4.6 6.3 %collective-permute-start.6 = (bf16[224,128]{1,0:T(8,128)(2,1)S(1)}, bf16[224,128]{1,0:T(8,128)(2,1)S(1)}, u32[]{:S(2)}, u32[]{:S(2)}) collective-permute-start(bf16[224,128]{1,0:T(8,128)(2,1)S(1)} %shard_map.65), channel_id=1, source_target_pairs={{0,4},{1,5},{2,6},{3,7},{4,0},{5,1},{6,2},{7,3},{8,12},{9,13},{10,... | collective-permute-start | bytes 172040 | tf_op jit(solution)/shard_map/ppermute | solution.py:281
  6.7 5.1 %collective-permute-start.10 = (bf16[224,128]{1,0:T(8,128)(2,1)S(1)}, bf16[224,128]{1,0:T(8,128)(2,1)S(1)}, u32[]{:S(2)}, u32[]{:S(2)}) collective-permute-start(bf16[224,128]{1,0:T(8,128)(2,1)S(1)} %shard_map.67), channel_id=1, source_target_pairs={{0,4},{1,5},{2,6},{3,7},{4,0},{5,1},{6,2},{7,3},{8,12},{9,13},{10,... | collective-permute-start | bytes 172040 | tf_op jit(solution)/shard_map/ppermute | solution.py:281
  12.2 4.7 %collective-permute-start.3 = (bf16[64,128]{1,0:T(8,128)(2,1)S(1)}, bf16[64,128]{1,0:T(8,128)(2,1)S(1)}, u32[]{:S(2)}, u32[]{:S(2)}) collective-permute-start(bf16[64,128]{1,0:T(8,128)(2,1)S(1)} %get-tuple-element.43), channel_id=1, source_target_pairs={{0,3},{1,2},{2,1},{3,0},{4,7},{5,6},{6,5},{7,4},{8,11},{9,10},{10,... | collective-permute-start | bytes 49160 | tf_op jit(solution)/shard_map/cond/branch_0_fun/ppermute | solution.py:281
  15.0 3.7 %collective-permute-start.4 = (bf16[64,128]{1,0:T(8,128)(2,1)S(1)}, bf16[64,128]{1,0:T(8,128)(2,1)S(1)}, u32[]{:S(2)}, u32[]{:S(2)}) collective-permute-start(bf16[64,128]{1,0:T(8,128)(2,1)S(1)} %get-tuple-element.44), channel_id=1, source_target_pairs={{0,1},{1,0},{2,3},{3,2},{4,5},{5,4},{6,7},{7,6},{8,9},{9,8},{10,11... | collective-permute-start | bytes 49160 | tf_op jit(solution)/shard_map/cond/branch_0_fun/ppermute | solution.py:281
  15.5 3.7 %collective-permute-start.5 = (bf16[64,128]{1,0:T(8,128)(2,1)S(1)}, bf16[64,128]{1,0:T(8,128)(2,1)S(1)}, u32[]{:S(2)}, u32[]{:S(2)}) collective-permute-start(bf16[64,128]{1,0:T(8,128)(2,1)S(1)} %get-tuple-element.45), channel_id=1, source_target_pairs={{0,2},{1,3},{2,0},{3,1},{4,6},{5,7},{6,4},{7,5},{8,10},{9,11},{10,... | collective-permute-start | bytes 49160 | tf_op jit(solution)/shard_map/cond/branch_0_fun/ppermute | solution.py:281

commit v8 on v6

--- a/solution.py
+++ b/solution.py
@@ -142,11 +142,9 @@
     groups = near_ref.shape[1] // block // HALVES
     coarse_ref[:rows, :] = stays_ref[span(1 - half, rows), :]
     for m in range(groups):
-        parts = split(near_ref[:, m * block : (m + 1) * block])
-        coarse_ref[(m + 1) * rows : (m + 2) * rows, :] = parts[0]
-        at = (groups + 1 + m) * rows
-        if at < coarse_ref.shape[0]:
-            coarse_ref[at : at + rows, :] = parts[1]
+        coarse_ref[(m + 1) * rows : (m + 2) * rows, :] = near_ref[
+            :, m * block : (m + 1) * block
+        ].astype(jnp.bfloat16)
 
 
 def lead_kernel(table_ref, own_ref, *refs):
@@ -193,11 +191,7 @@
     )
     other_taps = []
     for m in range(groups):
-        tap = other_ref[(m + 1) * rows : (m + 2) * rows, :].astype(jnp.float32)
-        at = (groups + 1 + m) * rows
-        if at < other_ref.shape[0]:
-            tap = tap + other_ref[at : at + rows, :].astype(jnp.float32)
-        other_taps.append(tap)
+        other_taps.append(other_ref[(m + 1) * rows : (m + 2) * rows, :].astype(jnp.float32))
     store_taps(other_taps, table_ref, other_taps_ref)
     blocks = []
     for ref in arrived:
@@ -253,7 +247,7 @@
 HBM = pl.BlockSpec(memory_space=pltpu.HBM)
 
 
-def call(kernel, outs, args, scratch=(), far=0):
+def call(kernel, outs, args, scratch=(), far=0, cost=None):
     args = [
         pltpu.with_memory_space_constraint(arg, pltpu.HBM) if i < far else arg
         for i, arg in enumerate(args)
@@ -264,6 +258,7 @@
         in_specs=[HBM if i < far else VMEM for i in range(len(args))],
         out_specs=[VMEM] * len(outs),
         scratch_shapes=list(scratch),
+        cost_estimate=cost,
         compiler_params=pltpu.CompilerParams(vmem_limit_bytes=16 * 1024 * 1024),
     )(*args)
 
@@ -282,6 +277,7 @@
     group_part = ((chans, block), bf16)
     waves_of = ((groups, rows, full), f32)
     taps_of = lambda count: ((count, rows, full), f32)
+    early_part = (((groups + 1) * rows, block), bf16)
     across_part = (((2 * groups - 1) * rows, block), bf16)
     outputs = ((shards, rows, block), f32)
     scratch = lambda *shapes: [pltpu.VMEM(*shape) for shape in shapes]
@@ -294,7 +290,7 @@
         4,
     )
     own = filters
-    (coarse,) = call(coarse_kernel, [across_part], (own, sends[0]))
+    (coarse,) = call(coarse_kernel, [early_part], (own, sends[0]))
     other = swap(coarse, groups)
     arrived = [swap(sends[k], k) if k else sends[k] for k in partners(groups)]
     (lead,) = call(
@@ -310,6 +306,7 @@
         + [taps_of(shards), waves_of, outputs, ((channels, block), f32)],
         (table, own, other, gated, skip, *arrived),
         scratch(taps_of(groups), waves_of, waves_of, waves_of),
+        cost=pl.CostEstimate(flops=2 * 10**8, transcendentals=0, bytes_accessed=0),
     )
 
     def give_back(parts):

time: 20 us -> 19.9 us (level); the launches traced: 19.9 us -> 19.5 us
  waiting for transfers between devices: 3.56 us -> 3.19 us
    ppermute x8, waiting for transfers between devices: 3.56 us -> 3.19 us  [per_device(): lax.ppermute(x, AXIS, [(i, i ^ k) for i in range(shards)])]
where the time goes in v8:
time: 19.9 us; the launch traced here: 19.5 us
  starting transfers between devices  13.3 us (67%)
  waiting for transfers between devices  3.19 us (16%)
  Pallas kernels  2.94 us (15%)
    ppermute x8, starting transfers between devices, per_device(): lax.ppermute(x, AXIS, [(i, i ^ k) for i in range(shards)])  13.3 us
    ppermute x8, waiting for transfers between devices, per_device(): lax.ppermute(x, AXIS, [(i, i ^ k) for i in range(shards)])  3.19 us
    pallas_call x7, Pallas kernels, call(): pl.pallas_call(kernel, out_shape=[jax.ShapeDtypeStruct(shape, dtype) for...  2.94 us
  transfers between devices with their start and end apart: 8, of which 5 were waited for; matrix products, arithmetic and copies ran while one was open for 0% of the time, Pallas kernels for 7%

profile of v8, /device:TPU:0, one launch (start us, length us, event | category | flops | bytes accessed | tf_op | source)
XLA Modules:
  0.0 19.5 jit_solution(2899813567145370253)
XLA Ops:
  0.0 0.0 copy-start
  0.0 1.0 %shard_map.64 = (bf16[256,128]{1,0:T(8,128)(2,1)S(1)}, f32[256]{0:T(256)S(1)}, bf16[256,128]{1,0:T(8,128)(2,1)S(1)}, bf16[64,128]{1,0:T(8,128)(2,1)S(1)}, bf16[6...) custom-call(bf16[256,128]{1,0:T(8,128)(2,1)} %refs_0_.1, ...), custom_call_target="tpu_custom_call" | custom-call | tf_op jit(solution)/shard_map/pallas_call | solution.py:255
  1.0 0.0 copy-start.1
  1.0 4.0 %collective-permute-start.7 = (bf16[64,128]{1,0:T(8,128)(2,1)S(1)}, bf16[64,128]{1,0:T(8,128)(2,1)S(1)}, u32[]{:S(2)}, u32[]{:S(2)}) collective-permute-start(bf16[64,128]{1,0:T(8,128)(2,1)S(1)} %get-tuple-element.66), channel_id=1, source_target_pairs={{0,3},{1,2},{2,1},{3,0},{4,7},{5,6},{6,5},{7,4},{8,11},{9,10},{10,... | collective-permute-start | bytes 49160 | tf_op jit(solution)/shard_map/ppermute | solution.py:275
  5.0 0.5 %collective-permute-start.8 = (bf16[64,128]{1,0:T(8,128)(2,1)S(1)}, bf16[64,128]{1,0:T(8,128)(2,1)S(1)}, u32[]{:S(2)}, u32[]{:S(2)}) collective-permute-start(bf16[64,128]{1,0:T(8,128)(2,1)S(1)} %get-tuple-element.67), channel_id=1, source_target_pairs={{0,1},{1,0},{2,3},{3,2},{4,5},{5,4},{6,7},{7,6},{8,9},{9,8},{10,11... | collective-permute-start | bytes 49160 | tf_op jit(solution)/shard_map/ppermute | solution.py:275
  5.5 0.1 collective-permute-start.9
  5.7 0.0 copy-done
  5.7 3.0 %collective-permute-start.6 = (bf16[160,128]{1,0:T(8,128)(2,1)S(1)}, bf16[160,128]{1,0:T(8,128)(2,1)S(1)}, u32[]{:S(2)}, u32[]{:S(2)}) collective-permute-start(bf16[160,128]{1,0:T(8,128)(2,1)S(1)} %shard_map.65), channel_id=1, source_target_pairs={{0,4},{1,5},{2,6},{3,7},{4,0},{5,1},{6,2},{7,3},{8,12},{9,13},{10,... | collective-permute-start | bytes 122888 | tf_op jit(solution)/shard_map/ppermute | solution.py:275
  8.7 0.0 collective-permute-done.7.refs_0_
  8.7 0.1 collective-permute-done.8.refs_1_
  8.8 0.5 %collective-permute-done.9.refs_2_ = bf16[64,128]{1,0:T(8,128)(2,1)S(1)} collective-permute-done((bf16[64,128]{1,0:T(8,128)(2,1)S(1)}, bf16[64,128]{1,0:T(8,128)(2,1)S(1)}, u32[]{:S(2)}, u32[]{:S(2)}) %collective-permute-start.9) | collective-permute-done | bytes 16416 | tf_op jit(solution)/shard_map/ppermute | solution.py:275
  9.3 0.0 copy-done.1
  9.3 0.5 %shard_map.67 = bf16[224,128]{1,0:T(8,128)(2,1)S(1)} custom-call(bf16[256,256]{1,0:T(8,128)(2,1)S(1)} %copy-done.1, f32[32,1024]{1,0:T(8,128)S(1)} %copy-done, bf16[64,128]{1,0:T(8,128)(2,1)S(1)} %collective-permute-done.7.refs_0_, bf16[64,128]{1,0:T(8,128)(2,1)S(1)} %collective-permute-done.8.refs_1_, bf16[64,128]{1,0:T(8,128)(2,1)S(1)} %collective-permute-done.9.refs_2_, ...), custom_call_target="tpu_custom_call" | custom-call | tf_op jit(solution)/shard_map/pallas_call | solution.py:255
  9.8 2.1 %collective-permute-start.10 = (bf16[224,128]{1,0:T(8,128)(2,1)S(1)}, bf16[224,128]{1,0:T(8,128)(2,1)S(1)}, u32[]{:S(2)}, u32[]{:S(2)}) collective-permute-start(bf16[224,128]{1,0:T(8,128)(2,1)S(1)} %shard_map.67), channel_id=1, source_target_pairs={{0,4},{1,5},{2,6},{3,7},{4,0},{5,1},{6,2},{7,3},{8,12},{9,13},{10,... | collective-permute-start | bytes 172040 | tf_op jit(solution)/shard_map/ppermute | solution.py:275
  11.9 0.0 collective-permute-done.6.other_ref
  11.9 0.8 %shard_map.66 = (bf16[64,128]{1,0:T(8,128)(2,1)S(1)}, bf16[64,128]{1,0:T(8,128)(2,1)S(1)}, bf16[64,128]{1,0:T(8,128)(2,1)S(1)}, bf16[64,128]{1,0:T(8,128)(2,1)S(...) custom-call(bf16[256,256]{1,0:T(8,128)(2,1)S(1)} %copy-done.1, ...), custom_call_target="tpu_custom_call" | custom-call | flops 200000000 | tf_op jit(solution)/shard_map/pallas_call | solution.py:255
  12.7 6.2 %conditional.2 = (bf16[256,128]{1,0:T(8,128)(2,1)S(1)}) conditional(s32[]{:T(128)} %convert_element_type.4, bf16[256,128]{1,0:T(8,128)(2,1)S(1)} %get-tuple-element.64.gated_ref, (bf16[64,128]{1,0:T(8,128)(2,1)S(1)}, bf16[64,128]{1,0:T(8,128)(2,1)S(1)}, bf16[64,128]{1,0:T(8,128)(2,1)S(1)}, bf16[64,128]{1,0:T(8,128)(2,1)S(1)}) %tuple.18), branch_computations={%region_0.0_spmd, %region_1.0_spmd} | conditional | bytes 196736 | solution.py:328
  12.7 1.9 %collective-permute-start = (bf16[64,128]{1,0:T(8,128)(2,1)S(1)}, bf16[64,128]{1,0:T(8,128)(2,1)S(1)}, u32[]{:S(2)}, u32[]{:S(2)}) collective-permute-start(bf16[64,128]{1,0:T(8,128)(2,1)S(1)} %get-tuple-element.33), channel_id=1, source_target_pairs={{0,3},{1,2},{2,1},{3,0},{4,7},{5,6},{6,5},{7,4},{8,11},{9,10},{10,... | collective-permute-start | bytes 49160 | tf_op jit(solution)/shard_map/cond/branch_1_fun/ppermute | solution.py:275
  14.5 0.5 %collective-permute-start.1 = (bf16[64,128]{1,0:T(8,128)(2,1)S(1)}, bf16[64,128]{1,0:T(8,128)(2,1)S(1)}, u32[]{:S(2)}, u32[]{:S(2)}) collective-permute-start(bf16[64,128]{1,0:T(8,128)(2,1)S(1)} %get-tuple-element.34), channel_id=1, source_target_pairs={{0,1},{1,0},{2,3},{3,2},{4,5},{5,4},{6,7},{7,6},{8,9},{9,8},{10,11... | collective-permute-start | bytes 49160 | tf_op jit(solution)/shard_map/cond/branch_1_fun/ppermute | solution.py:275
  15.1 1.2 %collective-permute-start.2 = (bf16[64,128]{1,0:T(8,128)(2,1)S(1)}, bf16[64,128]{1,0:T(8,128)(2,1)S(1)}, u32[]{:S(2)}, u32[]{:S(2)}) collective-permute-start(bf16[64,128]{1,0:T(8,128)(2,1)S(1)} %get-tuple-element.35), channel_id=1, source_target_pairs={{0,2},{1,3},{2,0},{3,1},{4,6},{5,7},{6,4},{7,5},{8,10},{9,11},{10,... | collective-permute-start | bytes 49160 | tf_op jit(solution)/shard_map/cond/branch_1_fun/ppermute | solution.py:275
  16.2 1.1 %collective-permute-done.refs_0_ = bf16[64,128]{1,0:T(8,128)(2,1)S(1)} collective-permute-done((bf16[64,128]{1,0:T(8,128)(2,1)S(1)}, bf16[64,128]{1,0:T(8,128)(2,1)S(1)}, u32[]{:S(2)}, u32[]{:S(2)}) %collective-permute-start) | collective-permute-done | bytes 16416 | tf_op jit(solution)/shard_map/cond/branch_1_fun/ppermute | solution.py:275
  17.4 0.9 %collective-permute-done.1.refs_1_ = bf16[64,128]{1,0:T(8,128)(2,1)S(1)} collective-permute-done((bf16[64,128]{1,0:T(8,128)(2,1)S(1)}, bf16[64,128]{1,0:T(8,128)(2,1)S(1)}, u32[]{:S(2)}, u32[]{:S(2)}) %collective-permute-start.1) | collective-permute-done | bytes 16416 | tf_op jit(solution)/shard_map/cond/branch_1_fun/ppermute | solution.py:275
  18.3 0.5 %collective-permute-done.2.refs_2_ = bf16[64,128]{1,0:T(8,128)(2,1)S(1)} collective-permute-done((bf16[64,128]{1,0:T(8,128)(2,1)S(1)}, bf16[64,128]{1,0:T(8,128)(2,1)S(1)}, u32[]{:S(2)}, u32[]{:S(2)}) %collective-permute-start.2) | collective-permute-done | bytes 16416 | tf_op jit(solution)/shard_map/cond/branch_1_fun/ppermute | solution.py:275
  18.8 0.0 collective-permute-done.10
  18.9 0.7 %shard_map.68 = bf16[256,128]{1,0:T(8,128)(2,1)} custom-call(bf16[256,128]{1,0:T(8,128)(2,1)S(1)} %get-tuple-element.62.queries_ref, f32[256,128]{1,0:T(8,128)S(1)} %get-tuple-element.69.skipped_ref, bf16[256,128]{1,0:T(8,128)(2,1)S(1)} %get-tuple-element.78.convolved_ref), custom_call_target="tpu_custom_call" | custom-call | tf_op jit(solution)/shard_map/pallas_call | solution.py:255
  (4 shorter events, 0.1 us)
Async XLA Ops:
  0.0 5.7 %copy-start = (f32[32,1024]{1,0:T(8,128)S(1)}, f32[32,1024]{1,0:T(8,128)}, u32[]{:S(2)}) copy-start(f32[32,1024]{1,0:T(8,128)} %own_ref.3) | copy-start | bytes 393220
  1.0 8.3 %copy-start.1 = (bf16[256,256]{1,0:T(8,128)(2,1)S(1)}, bf16[256,256]{1,0:T(8,128)(2,1)}, u32[]{:S(2)}) copy-start(bf16[256,256]{1,0:T(8,128)(2,1)} %constant.8.clone.table_ref) | copy-start | bytes 393220
  1.0 7.7 %collective-permute-start.7 = (bf16[64,128]{1,0:T(8,128)(2,1)S(1)}, bf16[64,128]{1,0:T(8,128)(2,1)S(1)}, u32[]{:S(2)}, u32[]{:S(2)}) collective-permute-start(bf16[64,128]{1,0:T(8,128)(2,1)S(1)} %get-tuple-element.66), channel_id=1, source_target_pairs={{0,3},{1,2},{2,1},{3,0},{4,7},{5,6},{6,5},{7,4},{8,11},{9,10},{10,... | collective-permute-start | bytes 49160 | tf_op jit(solution)/shard_map/ppermute | solution.py:275
  5.0 3.7 %collective-permute-start.8 = (bf16[64,128]{1,0:T(8,128)(2,1)S(1)}, bf16[64,128]{1,0:T(8,128)(2,1)S(1)}, u32[]{:S(2)}, u32[]{:S(2)}) collective-permute-start(bf16[64,128]{1,0:T(8,128)(2,1)S(1)} %get-tuple-element.67), channel_id=1, source_target_pairs={{0,1},{1,0},{2,3},{3,2},{4,5},{5,4},{6,7},{7,6},{8,9},{9,8},{10,11... | collective-permute-start | bytes 49160 | tf_op jit(solution)/shard_map/ppermute | solution.py:275
  5.5 3.7 %collective-permute-start.9 = (bf16[64,128]{1,0:T(8,128)(2,1)S(1)}, bf16[64,128]{1,0:T(8,128)(2,1)S(1)}, u32[]{:S(2)}, u32[]{:S(2)}) collective-permute-start(bf16[64,128]{1,0:T(8,128)(2,1)S(1)} %get-tuple-element.68), channel_id=1, source_target_pairs={{0,2},{1,3},{2,0},{3,1},{4,6},{5,7},{6,4},{7,5},{8,10},{9,11},{10,... | collective-permute-start | bytes 49160 | tf_op jit(solution)/shard_map/ppermute | solution.py:275
  5.7 6.2 %collective-permute-start.6 = (bf16[160,128]{1,0:T(8,128)(2,1)S(1)}, bf16[160,128]{1,0:T(8,128)(2,1)S(1)}, u32[]{:S(2)}, u32[]{:S(2)}) collective-permute-start(bf16[160,128]{1,0:T(8,128)(2,1)S(1)} %shard_map.65), channel_id=1, source_target_pairs={{0,4},{1,5},{2,6},{3,7},{4,0},{5,1},{6,2},{7,3},{8,12},{9,13},{10,... | collective-permute-start | bytes 122888 | tf_op jit(solution)/shard_map/ppermute | solution.py:275
  9.8 9.0 %collective-permute-start.10 = (bf16[224,128]{1,0:T(8,128)(2,1)S(1)}, bf16[224,128]{1,0:T(8,128)(2,1)S(1)}, u32[]{:S(2)}, u32[]{:S(2)}) collective-permute-start(bf16[224,128]{1,0:T(8,128)(2,1)S(1)} %shard_map.67), channel_id=1, source_target_pairs={{0,4},{1,5},{2,6},{3,7},{4,0},{5,1},{6,2},{7,3},{8,12},{9,13},{10,... | collective-permute-start | bytes 172040 | tf_op jit(solution)/shard_map/ppermute | solution.py:275
  12.7 4.7 %collective-permute-start = (bf16[64,128]{1,0:T(8,128)(2,1)S(1)}, bf16[64,128]{1,0:T(8,128)(2,1)S(1)}, u32[]{:S(2)}, u32[]{:S(2)}) collective-permute-start(bf16[64,128]{1,0:T(8,128)(2,1)S(1)} %get-tuple-element.33), channel_id=1, source_target_pairs={{0,3},{1,2},{2,1},{3,0},{4,7},{5,6},{6,5},{7,4},{8,11},{9,10},{10,... | collective-permute-start | bytes 49160 | tf_op jit(solution)/shard_map/cond/branch_1_fun/ppermute | solution.py:275
  14.5 3.7 %collective-permute-start.1 = (bf16[64,128]{1,0:T(8,128)(2,1)S(1)}, bf16[64,128]{1,0:T(8,128)(2,1)S(1)}, u32[]{:S(2)}, u32[]{:S(2)}) collective-permute-start(bf16[64,128]{1,0:T(8,128)(2,1)S(1)} %get-tuple-element.34), channel_id=1, source_target_pairs={{0,1},{1,0},{2,3},{3,2},{4,5},{5,4},{6,7},{7,6},{8,9},{9,8},{10,11... | collective-permute-start | bytes 49160 | tf_op jit(solution)/shard_map/cond/branch_1_fun/ppermute | solution.py:275
  15.1 3.7 %collective-permute-start.2 = (bf16[64,128]{1,0:T(8,128)(2,1)S(1)}, bf16[64,128]{1,0:T(8,128)(2,1)S(1)}, u32[]{:S(2)}, u32[]{:S(2)}) collective-permute-start(bf16[64,128]{1,0:T(8,128)(2,1)S(1)} %get-tuple-element.35), channel_id=1, source_target_pairs={{0,2},{1,3},{2,0},{3,1},{4,6},{5,7},{6,4},{7,5},{8,10},{9,11},{10,... | collective-permute-start | bytes 49160 | tf_op jit(solution)/shard_map/cond/branch_1_fun/ppermute | solution.py:275

commit v9 on v6

--- a/solution.py
+++ b/solution.py
@@ -84,6 +84,13 @@
     high, low = split(spectra)
     top, rest = table_ref[:block, :], table_ref[block:, :]
     total = dot(high, top, True) + dot(low, top, True) + dot(high, rest, True)
+    return total * (1.0 / block)
+
+
+def stacked_back_from(spectra, table_ref):
+    count, block = spectra.shape[0], spectra.shape[1] // 2
+    both = dot(jnp.concatenate(split(spectra), axis=0), table_ref[...], True)
+    total = both[:count, :block] + both[count:, :block] + both[:count, block:]
     return total * (1.0 / block)
 
 
@@ -220,7 +227,7 @@
     store_waves(blocks, table_ref, [waves_ref])
     products(waves_ref, taps_ref, groups, total_ref, sums_ref)
     total = total_ref[...].reshape(groups * rows, full)
-    own_ref[...] = back_from(total, table_ref).reshape(own_ref.shape)
+    own_ref[...] = stacked_back_from(total, table_ref).reshape(own_ref.shape)
 
     def other(j):
         return other_ref[j] + across_ref[span(j, rows), :].astype(jnp.float32)

time: 20 us -> 20 us (level)
  no operation moved by 1% of the time
where the time goes in v9:
time: 20 us; the launch traced here: 19.9 us
  starting transfers between devices  13.3 us (66%)
  waiting for transfers between devices  3.56 us (18%)
  Pallas kernels  2.94 us (15%)
    ppermute x8, starting transfers between devices, per_device(): lax.ppermute(x, AXIS, [(i, i ^ k) for i in range(shards)])  13.3 us
    ppermute x8, waiting for transfers between devices, per_device(): lax.ppermute(x, AXIS, [(i, i ^ k) for i in range(shards)])  3.56 us
    pallas_call x7, Pallas kernels, call(): pl.pallas_call(kernel, out_shape=[jax.ShapeDtypeStruct(shape, dtype) for...  2.94 us
  transfers between devices with their start and end apart: 8, of which 5 were waited for; matrix products, arithmetic and copies ran while one was open for 0% of the time, Pallas kernels for 7%

profile of v9, /device:TPU:0, one launch (start us, length us, event | category | flops | bytes accessed | tf_op | source)
XLA Modules:
  0.0 19.9 jit_solution(16144136825072426665)
XLA Ops:
  0.0 0.0 copy-start
  0.0 1.0 %shard_map.64 = (bf16[256,128]{1,0:T(8,128)(2,1)S(1)}, f32[256]{0:T(256)S(1)}, bf16[256,128]{1,0:T(8,128)(2,1)S(1)}, bf16[64,128]{1,0:T(8,128)(2,1)S(1)}, bf16[6...) custom-call(bf16[256,128]{1,0:T(8,128)(2,1)} %refs_0_.1, ...), custom_call_target="tpu_custom_call" | custom-call | tf_op jit(solution)/shard_map/pallas_call | solution.py:268
  1.0 0.0 copy-start.1
  1.0 4.0 %collective-permute-start.7 = (bf16[64,128]{1,0:T(8,128)(2,1)S(1)}, bf16[64,128]{1,0:T(8,128)(2,1)S(1)}, u32[]{:S(2)}, u32[]{:S(2)}) collective-permute-start(bf16[64,128]{1,0:T(8,128)(2,1)S(1)} %get-tuple-element.66), channel_id=1, source_target_pairs={{0,3},{1,2},{2,1},{3,0},{4,7},{5,6},{6,5},{7,4},{8,11},{9,10},{10,... | collective-permute-start | bytes 49160 | tf_op jit(solution)/shard_map/ppermute | solution.py:287
  5.0 0.5 %collective-permute-start.8 = (bf16[64,128]{1,0:T(8,128)(2,1)S(1)}, bf16[64,128]{1,0:T(8,128)(2,1)S(1)}, u32[]{:S(2)}, u32[]{:S(2)}) collective-permute-start(bf16[64,128]{1,0:T(8,128)(2,1)S(1)} %get-tuple-element.67), channel_id=1, source_target_pairs={{0,1},{1,0},{2,3},{3,2},{4,5},{5,4},{6,7},{7,6},{8,9},{9,8},{10,11... | collective-permute-start | bytes 49160 | tf_op jit(solution)/shard_map/ppermute | solution.py:287
  5.5 0.1 collective-permute-start.9
  5.7 0.0 copy-done
  5.7 3.0 %collective-permute-start.6 = (bf16[224,128]{1,0:T(8,128)(2,1)S(1)}, bf16[224,128]{1,0:T(8,128)(2,1)S(1)}, u32[]{:S(2)}, u32[]{:S(2)}) collective-permute-start(bf16[224,128]{1,0:T(8,128)(2,1)S(1)} %shard_map.65), channel_id=1, source_target_pairs={{0,4},{1,5},{2,6},{3,7},{4,0},{5,1},{6,2},{7,3},{8,12},{9,13},{10,... | collective-permute-start | bytes 172040 | tf_op jit(solution)/shard_map/ppermute | solution.py:287
  8.7 0.0 collective-permute-done.7.refs_0_
  8.7 0.1 collective-permute-done.8.refs_1_
  8.8 0.6 %collective-permute-done.9.refs_2_ = bf16[64,128]{1,0:T(8,128)(2,1)S(1)} collective-permute-done((bf16[64,128]{1,0:T(8,128)(2,1)S(1)}, bf16[64,128]{1,0:T(8,128)(2,1)S(1)}, u32[]{:S(2)}, u32[]{:S(2)}) %collective-permute-start.9) | collective-permute-done | bytes 16416 | tf_op jit(solution)/shard_map/ppermute | solution.py:287
  9.3 0.0 copy-done.1
  9.3 0.5 %shard_map.67 = bf16[224,128]{1,0:T(8,128)(2,1)S(1)} custom-call(bf16[256,256]{1,0:T(8,128)(2,1)S(1)} %copy-done.1, f32[32,1024]{1,0:T(8,128)S(1)} %copy-done, bf16[64,128]{1,0:T(8,128)(2,1)S(1)} %collective-permute-done.7.refs_0_, bf16[64,128]{1,0:T(8,128)(2,1)S(1)} %collective-permute-done.8.refs_1_, bf16[64,128]{1,0:T(8,128)(2,1)S(1)} %collective-permute-done.9.refs_2_, ...), custom_call_target="tpu_custom_call" | custom-call | tf_op jit(solution)/shard_map/pallas_call | solution.py:268
  9.8 2.1 %collective-permute-start.10 = (bf16[224,128]{1,0:T(8,128)(2,1)S(1)}, bf16[224,128]{1,0:T(8,128)(2,1)S(1)}, u32[]{:S(2)}, u32[]{:S(2)}) collective-permute-start(bf16[224,128]{1,0:T(8,128)(2,1)S(1)} %shard_map.67), channel_id=1, source_target_pairs={{0,4},{1,5},{2,6},{3,7},{4,0},{5,1},{6,2},{7,3},{8,12},{9,13},{10,... | collective-permute-start | bytes 172040 | tf_op jit(solution)/shard_map/ppermute | solution.py:287
  11.9 0.0 collective-permute-done.6.other_ref
  11.9 0.8 %shard_map.66 = (bf16[64,128]{1,0:T(8,128)(2,1)S(1)}, bf16[64,128]{1,0:T(8,128)(2,1)S(1)}, bf16[64,128]{1,0:T(8,128)(2,1)S(1)}, bf16[64,128]{1,0:T(8,128)(2,1)S(...) custom-call(bf16[256,256]{1,0:T(8,128)(2,1)S(1)} %copy-done.1, ...), custom_call_target="tpu_custom_call" | custom-call | tf_op jit(solution)/shard_map/pallas_call | solution.py:268
  12.7 6.5 %conditional.2 = (bf16[256,128]{1,0:T(8,128)(2,1)S(1)}) conditional(s32[]{:T(128)} %convert_element_type.4, bf16[256,128]{1,0:T(8,128)(2,1)S(1)} %get-tuple-element.64.gated_ref, (bf16[64,128]{1,0:T(8,128)(2,1)S(1)}, bf16[64,128]{1,0:T(8,128)(2,1)S(1)}, bf16[64,128]{1,0:T(8,128)(2,1)S(1)}, bf16[64,128]{1,0:T(8,128)(2,1)S(1)}) %tuple.18), branch_computations={%region_0.0_spmd, %region_1.0_spmd} | conditional | bytes 196736 | solution.py:338
  12.7 2.2 %collective-permute-start = (bf16[64,128]{1,0:T(8,128)(2,1)S(1)}, bf16[64,128]{1,0:T(8,128)(2,1)S(1)}, u32[]{:S(2)}, u32[]{:S(2)}) collective-permute-start(bf16[64,128]{1,0:T(8,128)(2,1)S(1)} %get-tuple-element.33), channel_id=1, source_target_pairs={{0,3},{1,2},{2,1},{3,0},{4,7},{5,6},{6,5},{7,4},{8,11},{9,10},{10,... | collective-permute-start | bytes 49160 | tf_op jit(solution)/shard_map/cond/branch_1_fun/ppermute | solution.py:287
  14.9 0.5 %collective-permute-start.1 = (bf16[64,128]{1,0:T(8,128)(2,1)S(1)}, bf16[64,128]{1,0:T(8,128)(2,1)S(1)}, u32[]{:S(2)}, u32[]{:S(2)}) collective-permute-start(bf16[64,128]{1,0:T(8,128)(2,1)S(1)} %get-tuple-element.34), channel_id=1, source_target_pairs={{0,1},{1,0},{2,3},{3,2},{4,5},{5,4},{6,7},{7,6},{8,9},{9,8},{10,11... | collective-permute-start | bytes 49160 | tf_op jit(solution)/shard_map/cond/branch_1_fun/ppermute | solution.py:287
  15.4 0.8 %collective-permute-start.2 = (bf16[64,128]{1,0:T(8,128)(2,1)S(1)}, bf16[64,128]{1,0:T(8,128)(2,1)S(1)}, u32[]{:S(2)}, u32[]{:S(2)}) collective-permute-start(bf16[64,128]{1,0:T(8,128)(2,1)S(1)} %get-tuple-element.35), channel_id=1, source_target_pairs={{0,2},{1,3},{2,0},{3,1},{4,6},{5,7},{6,4},{7,5},{8,10},{9,11},{10,... | collective-permute-start | bytes 49160 | tf_op jit(solution)/shard_map/cond/branch_1_fun/ppermute | solution.py:287
  16.2 1.1 %collective-permute-done.refs_0_ = bf16[64,128]{1,0:T(8,128)(2,1)S(1)} collective-permute-done((bf16[64,128]{1,0:T(8,128)(2,1)S(1)}, bf16[64,128]{1,0:T(8,128)(2,1)S(1)}, u32[]{:S(2)}, u32[]{:S(2)}) %collective-permute-start) | collective-permute-done | bytes 16416 | tf_op jit(solution)/shard_map/cond/branch_1_fun/ppermute | solution.py:287
  17.4 1.2 %collective-permute-done.1.refs_1_ = bf16[64,128]{1,0:T(8,128)(2,1)S(1)} collective-permute-done((bf16[64,128]{1,0:T(8,128)(2,1)S(1)}, bf16[64,128]{1,0:T(8,128)(2,1)S(1)}, u32[]{:S(2)}, u32[]{:S(2)}) %collective-permute-start.1) | collective-permute-done | bytes 16416 | tf_op jit(solution)/shard_map/cond/branch_1_fun/ppermute | solution.py:287
  18.6 0.5 %collective-permute-done.2.refs_2_ = bf16[64,128]{1,0:T(8,128)(2,1)S(1)} collective-permute-done((bf16[64,128]{1,0:T(8,128)(2,1)S(1)}, bf16[64,128]{1,0:T(8,128)(2,1)S(1)}, u32[]{:S(2)}, u32[]{:S(2)}) %collective-permute-start.2) | collective-permute-done | bytes 16416 | tf_op jit(solution)/shard_map/cond/branch_1_fun/ppermute | solution.py:287
  19.2 0.0 collective-permute-done.10
  19.2 0.7 %shard_map.68 = bf16[256,128]{1,0:T(8,128)(2,1)} custom-call(bf16[256,128]{1,0:T(8,128)(2,1)S(1)} %get-tuple-element.62.queries_ref, f32[256,128]{1,0:T(8,128)S(1)} %get-tuple-element.69.skipped_ref, bf16[256,128]{1,0:T(8,128)(2,1)S(1)} %get-tuple-element.78.convolved_ref), custom_call_target="tpu_custom_call" | custom-call | tf_op jit(solution)/shard_map/pallas_call | solution.py:268
  (4 shorter events, 0.1 us)
Async XLA Ops:
  0.0 5.7 %copy-start = (f32[32,1024]{1,0:T(8,128)S(1)}, f32[32,1024]{1,0:T(8,128)}, u32[]{:S(2)}) copy-start(f32[32,1024]{1,0:T(8,128)} %own_ref.3) | copy-start | bytes 393220
  1.0 8.3 %copy-start.1 = (bf16[256,256]{1,0:T(8,128)(2,1)S(1)}, bf16[256,256]{1,0:T(8,128)(2,1)}, u32[]{:S(2)}) copy-start(bf16[256,256]{1,0:T(8,128)(2,1)} %constant.8.clone.table_ref) | copy-start | bytes 393220
  1.0 7.7 %collective-permute-start.7 = (bf16[64,128]{1,0:T(8,128)(2,1)S(1)}, bf16[64,128]{1,0:T(8,128)(2,1)S(1)}, u32[]{:S(2)}, u32[]{:S(2)}) collective-permute-start(bf16[64,128]{1,0:T(8,128)(2,1)S(1)} %get-tuple-element.66), channel_id=1, source_target_pairs={{0,3},{1,2},{2,1},{3,0},{4,7},{5,6},{6,5},{7,4},{8,11},{9,10},{10,... | collective-permute-start | bytes 49160 | tf_op jit(solution)/shard_map/ppermute | solution.py:287
  5.0 3.7 %collective-permute-start.8 = (bf16[64,128]{1,0:T(8,128)(2,1)S(1)}, bf16[64,128]{1,0:T(8,128)(2,1)S(1)}, u32[]{:S(2)}, u32[]{:S(2)}) collective-permute-start(bf16[64,128]{1,0:T(8,128)(2,1)S(1)} %get-tuple-element.67), channel_id=1, source_target_pairs={{0,1},{1,0},{2,3},{3,2},{4,5},{5,4},{6,7},{7,6},{8,9},{9,8},{10,11... | collective-permute-start | bytes 49160 | tf_op jit(solution)/shard_map/ppermute | solution.py:287
  5.5 3.8 %collective-permute-start.9 = (bf16[64,128]{1,0:T(8,128)(2,1)S(1)}, bf16[64,128]{1,0:T(8,128)(2,1)S(1)}, u32[]{:S(2)}, u32[]{:S(2)}) collective-permute-start(bf16[64,128]{1,0:T(8,128)(2,1)S(1)} %get-tuple-element.68), channel_id=1, source_target_pairs={{0,2},{1,3},{2,0},{3,1},{4,6},{5,7},{6,4},{7,5},{8,10},{9,11},{10,... | collective-permute-start | bytes 49160 | tf_op jit(solution)/shard_map/ppermute | solution.py:287
  5.7 6.2 %collective-permute-start.6 = (bf16[224,128]{1,0:T(8,128)(2,1)S(1)}, bf16[224,128]{1,0:T(8,128)(2,1)S(1)}, u32[]{:S(2)}, u32[]{:S(2)}) collective-permute-start(bf16[224,128]{1,0:T(8,128)(2,1)S(1)} %shard_map.65), channel_id=1, source_target_pairs={{0,4},{1,5},{2,6},{3,7},{4,0},{5,1},{6,2},{7,3},{8,12},{9,13},{10,... | collective-permute-start | bytes 172040 | tf_op jit(solution)/shard_map/ppermute | solution.py:287
  9.8 9.4 %collective-permute-start.10 = (bf16[224,128]{1,0:T(8,128)(2,1)S(1)}, bf16[224,128]{1,0:T(8,128)(2,1)S(1)}, u32[]{:S(2)}, u32[]{:S(2)}) collective-permute-start(bf16[224,128]{1,0:T(8,128)(2,1)S(1)} %shard_map.67), channel_id=1, source_target_pairs={{0,4},{1,5},{2,6},{3,7},{4,0},{5,1},{6,2},{7,3},{8,12},{9,13},{10,... | collective-permute-start | bytes 172040 | tf_op jit(solution)/shard_map/ppermute | solution.py:287
  12.7 4.7 %collective-permute-start = (bf16[64,128]{1,0:T(8,128)(2,1)S(1)}, bf16[64,128]{1,0:T(8,128)(2,1)S(1)}, u32[]{:S(2)}, u32[]{:S(2)}) collective-permute-start(bf16[64,128]{1,0:T(8,128)(2,1)S(1)} %get-tuple-element.33), channel_id=1, source_target_pairs={{0,3},{1,2},{2,1},{3,0},{4,7},{5,6},{6,5},{7,4},{8,11},{9,10},{10,... | collective-permute-start | bytes 49160 | tf_op jit(solution)/shard_map/cond/branch_1_fun/ppermute | solution.py:287
  14.9 3.7 %collective-permute-start.1 = (bf16[64,128]{1,0:T(8,128)(2,1)S(1)}, bf16[64,128]{1,0:T(8,128)(2,1)S(1)}, u32[]{:S(2)}, u32[]{:S(2)}) collective-permute-start(bf16[64,128]{1,0:T(8,128)(2,1)S(1)} %get-tuple-element.34), channel_id=1, source_target_pairs={{0,1},{1,0},{2,3},{3,2},{4,5},{5,4},{6,7},{7,6},{8,9},{9,8},{10,11... | collective-permute-start | bytes 49160 | tf_op jit(solution)/shard_map/cond/branch_1_fun/ppermute | solution.py:287
  15.4 3.7 %collective-permute-start.2 = (bf16[64,128]{1,0:T(8,128)(2,1)S(1)}, bf16[64,128]{1,0:T(8,128)(2,1)S(1)}, u32[]{:S(2)}, u32[]{:S(2)}) collective-permute-start(bf16[64,128]{1,0:T(8,128)(2,1)S(1)} %get-tuple-element.35), channel_id=1, source_target_pairs={{0,2},{1,3},{2,0},{3,1},{4,6},{5,7},{6,4},{7,5},{8,10},{9,11},{10,... | collective-permute-start | bytes 49160 | tf_op jit(solution)/shard_map/cond/branch_1_fun/ppermute | solution.py:287

commit v10 on v9

--- a/solution.py
+++ b/solution.py
@@ -319,9 +319,13 @@
         scratch(taps_of(groups), waves_of, waves_of, waves_of),
     )
 
-    def give_back(parts):
-        returned = [swap(parts[k], k) if k else parts[k] for k in partners(groups)]
-        return call(join_kernel, [whole], returned)[0]
+    def give_back(parts, order):
+        returned = [swap(parts[k], k) if k else parts[k] for k in order]
+
+        def join(*refs):
+            join_kernel(*[refs[order.index(k)] for k in partners(groups)], refs[-1])
+
+        return call(join, [whole], returned)[0]
 
     def late(across):
         return give_back(
@@ -330,12 +334,14 @@
                 [group_part] * groups,
                 (table, taps, sums, other_out, other, across),
                 scratch(waves_of, waves_of, ((groups, rows, block), f32)),
-            )
+            ),
+            partners(groups),
         )
 
     copy = lambda x: call(copy_kernel, [whole], (x,))[0]
+    near_first = (1, groups - 1, *range(2, groups - 1), 0)
     first = lax.axis_index(AXIS) < groups
-    convolved = lax.cond(first, lambda: give_back(parts), lambda: copy(gated))
+    convolved = lax.cond(first, lambda: give_back(parts, near_first), lambda: copy(gated))
     convolved = lax.cond(
         first, lambda done, _: copy(done), lambda _, across: late(across), convolved, across
     )

time: 20 us -> 20 us (level)
  no operation moved by 1% of the time
where the time goes in v10:
time: 20 us; the launch traced here: 19.9 us
  starting transfers between devices  13.3 us (66%)
  waiting for transfers between devices  3.56 us (18%)
  Pallas kernels  2.94 us (15%)
    ppermute x8, starting transfers between devices, per_device(): lax.ppermute(x, AXIS, [(i, i ^ k) for i in range(shards)])  13.3 us
    ppermute x8, waiting for transfers between devices, per_device(): lax.ppermute(x, AXIS, [(i, i ^ k) for i in range(shards)])  3.56 us
    pallas_call x7, Pallas kernels, call(): pl.pallas_call(kernel, out_shape=[jax.ShapeDtypeStruct(shape, dtype) for...  2.94 us
  transfers between devices with their start and end apart: 8, of which 5 were waited for; matrix products, arithmetic and copies ran while one was open for 0% of the time, Pallas kernels for 7%

profile of v10, /device:TPU:0, one launch (start us, length us, event | category | flops | bytes accessed | tf_op | source)
XLA Modules:
  0.0 19.9 jit_solution(9387718783157975539)
XLA Ops:
  0.0 0.0 copy-start
  0.0 1.0 %shard_map.64 = (bf16[256,128]{1,0:T(8,128)(2,1)S(1)}, f32[256]{0:T(256)S(1)}, bf16[256,128]{1,0:T(8,128)(2,1)S(1)}, bf16[64,128]{1,0:T(8,128)(2,1)S(1)}, bf16[6...) custom-call(bf16[256,128]{1,0:T(8,128)(2,1)} %refs_0_.1, ...), custom_call_target="tpu_custom_call" | custom-call | tf_op jit(solution)/shard_map/pallas_call | solution.py:268
  1.0 0.0 copy-start.1
  1.0 4.0 %collective-permute-start.7 = (bf16[64,128]{1,0:T(8,128)(2,1)S(1)}, bf16[64,128]{1,0:T(8,128)(2,1)S(1)}, u32[]{:S(2)}, u32[]{:S(2)}) collective-permute-start(bf16[64,128]{1,0:T(8,128)(2,1)S(1)} %get-tuple-element.66), channel_id=1, source_target_pairs={{0,3},{1,2},{2,1},{3,0},{4,7},{5,6},{6,5},{7,4},{8,11},{9,10},{10,... | collective-permute-start | bytes 49160 | tf_op jit(solution)/shard_map/ppermute | solution.py:287
  5.0 0.5 %collective-permute-start.8 = (bf16[64,128]{1,0:T(8,128)(2,1)S(1)}, bf16[64,128]{1,0:T(8,128)(2,1)S(1)}, u32[]{:S(2)}, u32[]{:S(2)}) collective-permute-start(bf16[64,128]{1,0:T(8,128)(2,1)S(1)} %get-tuple-element.67), channel_id=1, source_target_pairs={{0,1},{1,0},{2,3},{3,2},{4,5},{5,4},{6,7},{7,6},{8,9},{9,8},{10,11... | collective-permute-start | bytes 49160 | tf_op jit(solution)/shard_map/ppermute | solution.py:287
  5.5 0.1 collective-permute-start.9
  5.7 0.0 copy-done
  5.7 3.0 %collective-permute-start.6 = (bf16[224,128]{1,0:T(8,128)(2,1)S(1)}, bf16[224,128]{1,0:T(8,128)(2,1)S(1)}, u32[]{:S(2)}, u32[]{:S(2)}) collective-permute-start(bf16[224,128]{1,0:T(8,128)(2,1)S(1)} %shard_map.65), channel_id=1, source_target_pairs={{0,4},{1,5},{2,6},{3,7},{4,0},{5,1},{6,2},{7,3},{8,12},{9,13},{10,... | collective-permute-start | bytes 172040 | tf_op jit(solution)/shard_map/ppermute | solution.py:287
  8.7 0.0 collective-permute-done.7.refs_0_
  8.7 0.1 collective-permute-done.8.refs_1_
  8.8 0.6 %collective-permute-done.9.refs_2_ = bf16[64,128]{1,0:T(8,128)(2,1)S(1)} collective-permute-done((bf16[64,128]{1,0:T(8,128)(2,1)S(1)}, bf16[64,128]{1,0:T(8,128)(2,1)S(1)}, u32[]{:S(2)}, u32[]{:S(2)}) %collective-permute-start.9) | collective-permute-done | bytes 16416 | tf_op jit(solution)/shard_map/ppermute | solution.py:287
  9.3 0.0 copy-done.1
  9.3 0.5 %shard_map.67 = bf16[224,128]{1,0:T(8,128)(2,1)S(1)} custom-call(bf16[256,256]{1,0:T(8,128)(2,1)S(1)} %copy-done.1, f32[32,1024]{1,0:T(8,128)S(1)} %copy-done, bf16[64,128]{1,0:T(8,128)(2,1)S(1)} %collective-permute-done.7.refs_0_, bf16[64,128]{1,0:T(8,128)(2,1)S(1)} %collective-permute-done.8.refs_1_, bf16[64,128]{1,0:T(8,128)(2,1)S(1)} %collective-permute-done.9.refs_2_, ...), custom_call_target="tpu_custom_call" | custom-call | tf_op jit(solution)/shard_map/pallas_call | solution.py:268
  9.8 2.1 %collective-permute-start.10 = (bf16[224,128]{1,0:T(8,128)(2,1)S(1)}, bf16[224,128]{1,0:T(8,128)(2,1)S(1)}, u32[]{:S(2)}, u32[]{:S(2)}) collective-permute-start(bf16[224,128]{1,0:T(8,128)(2,1)S(1)} %shard_map.67), channel_id=1, source_target_pairs={{0,4},{1,5},{2,6},{3,7},{4,0},{5,1},{6,2},{7,3},{8,12},{9,13},{10,... | collective-permute-start | bytes 172040 | tf_op jit(solution)/shard_map/ppermute | solution.py:287
  11.9 0.0 collective-permute-done.6.other_ref
  11.9 0.8 %shard_map.66 = (bf16[64,128]{1,0:T(8,128)(2,1)S(1)}, bf16[64,128]{1,0:T(8,128)(2,1)S(1)}, bf16[64,128]{1,0:T(8,128)(2,1)S(1)}, bf16[64,128]{1,0:T(8,128)(2,1)S(...) custom-call(bf16[256,256]{1,0:T(8,128)(2,1)S(1)} %copy-done.1, ...), custom_call_target="tpu_custom_call" | custom-call | tf_op jit(solution)/shard_map/pallas_call | solution.py:268
  12.7 6.5 %conditional.2 = (bf16[256,128]{1,0:T(8,128)(2,1)S(1)}) conditional(s32[]{:T(128)} %convert_element_type.4, bf16[256,128]{1,0:T(8,128)(2,1)S(1)} %get-tuple-element.64.gated_ref, (bf16[64,128]{1,0:T(8,128)(2,1)S(1)}, bf16[64,128]{1,0:T(8,128)(2,1)S(1)}, bf16[64,128]{1,0:T(8,128)(2,1)S(1)}, bf16[64,128]{1,0:T(8,128)(2,1)S(1)}) %tuple.18), branch_computations={%region_0.0_spmd, %region_1.0_spmd} | conditional | bytes 196736 | solution.py:344
  12.7 1.6 %collective-permute-start = (bf16[64,128]{1,0:T(8,128)(2,1)S(1)}, bf16[64,128]{1,0:T(8,128)(2,1)S(1)}, u32[]{:S(2)}, u32[]{:S(2)}) collective-permute-start(bf16[64,128]{1,0:T(8,128)(2,1)S(1)} %get-tuple-element.33), channel_id=1, source_target_pairs={{0,1},{1,0},{2,3},{3,2},{4,5},{5,4},{6,7},{7,6},{8,9},{9,8},{10,11... | collective-permute-start | bytes 49160 | tf_op jit(solution)/shard_map/cond/branch_1_fun/ppermute | solution.py:287
  14.2 1.2 %collective-permute-start.1 = (bf16[64,128]{1,0:T(8,128)(2,1)S(1)}, bf16[64,128]{1,0:T(8,128)(2,1)S(1)}, u32[]{:S(2)}, u32[]{:S(2)}) collective-permute-start(bf16[64,128]{1,0:T(8,128)(2,1)S(1)} %get-tuple-element.34), channel_id=1, source_target_pairs={{0,3},{1,2},{2,1},{3,0},{4,7},{5,6},{6,5},{7,4},{8,11},{9,10},{10,... | collective-permute-start | bytes 49160 | tf_op jit(solution)/shard_map/cond/branch_1_fun/ppermute | solution.py:287
  15.4 0.8 %collective-permute-start.2 = (bf16[64,128]{1,0:T(8,128)(2,1)S(1)}, bf16[64,128]{1,0:T(8,128)(2,1)S(1)}, u32[]{:S(2)}, u32[]{:S(2)}) collective-permute-start(bf16[64,128]{1,0:T(8,128)(2,1)S(1)} %get-tuple-element.35), channel_id=1, source_target_pairs={{0,2},{1,3},{2,0},{3,1},{4,6},{5,7},{6,4},{7,5},{8,10},{9,11},{10,... | collective-permute-start | bytes 49160 | tf_op jit(solution)/shard_map/cond/branch_1_fun/ppermute | solution.py:287
  16.2 0.2 %collective-permute-done.refs_0_ = bf16[64,128]{1,0:T(8,128)(2,1)S(1)} collective-permute-done((bf16[64,128]{1,0:T(8,128)(2,1)S(1)}, bf16[64,128]{1,0:T(8,128)(2,1)S(1)}, u32[]{:S(2)}, u32[]{:S(2)}) %collective-permute-start) | collective-permute-done | bytes 16416 | tf_op jit(solution)/shard_map/cond/branch_1_fun/ppermute | solution.py:287
  16.5 2.4 %collective-permute-done.1.refs_1_ = bf16[64,128]{1,0:T(8,128)(2,1)S(1)} collective-permute-done((bf16[64,128]{1,0:T(8,128)(2,1)S(1)}, bf16[64,128]{1,0:T(8,128)(2,1)S(1)}, u32[]{:S(2)}, u32[]{:S(2)}) %collective-permute-start.1) | collective-permute-done | bytes 16416 | tf_op jit(solution)/shard_map/cond/branch_1_fun/ppermute | solution.py:287
  18.9 0.3 %collective-permute-done.2.refs_2_ = bf16[64,128]{1,0:T(8,128)(2,1)S(1)} collective-permute-done((bf16[64,128]{1,0:T(8,128)(2,1)S(1)}, bf16[64,128]{1,0:T(8,128)(2,1)S(1)}, u32[]{:S(2)}, u32[]{:S(2)}) %collective-permute-start.2) | collective-permute-done | bytes 16416 | tf_op jit(solution)/shard_map/cond/branch_1_fun/ppermute | solution.py:287
  19.2 0.0 collective-permute-done.10
  19.2 0.7 %shard_map.68 = bf16[256,128]{1,0:T(8,128)(2,1)} custom-call(bf16[256,128]{1,0:T(8,128)(2,1)S(1)} %get-tuple-element.62.queries_ref, f32[256,128]{1,0:T(8,128)S(1)} %get-tuple-element.69.skipped_ref, bf16[256,128]{1,0:T(8,128)(2,1)S(1)} %get-tuple-element.78.convolved_ref), custom_call_target="tpu_custom_call" | custom-call | tf_op jit(solution)/shard_map/pallas_call | solution.py:268
  (4 shorter events, 0.1 us)
Async XLA Ops:
  0.0 5.7 %copy-start = (f32[32,1024]{1,0:T(8,128)S(1)}, f32[32,1024]{1,0:T(8,128)}, u32[]{:S(2)}) copy-start(f32[32,1024]{1,0:T(8,128)} %own_ref.3) | copy-start | bytes 393220
  1.0 8.3 %copy-start.1 = (bf16[256,256]{1,0:T(8,128)(2,1)S(1)}, bf16[256,256]{1,0:T(8,128)(2,1)}, u32[]{:S(2)}) copy-start(bf16[256,256]{1,0:T(8,128)(2,1)} %constant.8.clone.table_ref) | copy-start | bytes 393220
  1.0 7.7 %collective-permute-start.7 = (bf16[64,128]{1,0:T(8,128)(2,1)S(1)}, bf16[64,128]{1,0:T(8,128)(2,1)S(1)}, u32[]{:S(2)}, u32[]{:S(2)}) collective-permute-start(bf16[64,128]{1,0:T(8,128)(2,1)S(1)} %get-tuple-element.66), channel_id=1, source_target_pairs={{0,3},{1,2},{2,1},{3,0},{4,7},{5,6},{6,5},{7,4},{8,11},{9,10},{10,... | collective-permute-start | bytes 49160 | tf_op jit(solution)/shard_map/ppermute | solution.py:287
  5.0 3.7 %collective-permute-start.8 = (bf16[64,128]{1,0:T(8,128)(2,1)S(1)}, bf16[64,128]{1,0:T(8,128)(2,1)S(1)}, u32[]{:S(2)}, u32[]{:S(2)}) collective-permute-start(bf16[64,128]{1,0:T(8,128)(2,1)S(1)} %get-tuple-element.67), channel_id=1, source_target_pairs={{0,1},{1,0},{2,3},{3,2},{4,5},{5,4},{6,7},{7,6},{8,9},{9,8},{10,11... | collective-permute-start | bytes 49160 | tf_op jit(solution)/shard_map/ppermute | solution.py:287
  5.5 3.8 %collective-permute-start.9 = (bf16[64,128]{1,0:T(8,128)(2,1)S(1)}, bf16[64,128]{1,0:T(8,128)(2,1)S(1)}, u32[]{:S(2)}, u32[]{:S(2)}) collective-permute-start(bf16[64,128]{1,0:T(8,128)(2,1)S(1)} %get-tuple-element.68), channel_id=1, source_target_pairs={{0,2},{1,3},{2,0},{3,1},{4,6},{5,7},{6,4},{7,5},{8,10},{9,11},{10,... | collective-permute-start | bytes 49160 | tf_op jit(solution)/shard_map/ppermute | solution.py:287
  5.7 6.2 %collective-permute-start.6 = (bf16[224,128]{1,0:T(8,128)(2,1)S(1)}, bf16[224,128]{1,0:T(8,128)(2,1)S(1)}, u32[]{:S(2)}, u32[]{:S(2)}) collective-permute-start(bf16[224,128]{1,0:T(8,128)(2,1)S(1)} %shard_map.65), channel_id=1, source_target_pairs={{0,4},{1,5},{2,6},{3,7},{4,0},{5,1},{6,2},{7,3},{8,12},{9,13},{10,... | collective-permute-start | bytes 172040 | tf_op jit(solution)/shard_map/ppermute | solution.py:287
  9.8 9.4 %collective-permute-start.10 = (bf16[224,128]{1,0:T(8,128)(2,1)S(1)}, bf16[224,128]{1,0:T(8,128)(2,1)S(1)}, u32[]{:S(2)}, u32[]{:S(2)}) collective-permute-start(bf16[224,128]{1,0:T(8,128)(2,1)S(1)} %shard_map.67), channel_id=1, source_target_pairs={{0,4},{1,5},{2,6},{3,7},{4,0},{5,1},{6,2},{7,3},{8,12},{9,13},{10,... | collective-permute-start | bytes 172040 | tf_op jit(solution)/shard_map/ppermute | solution.py:287
  12.7 3.8 %collective-permute-start = (bf16[64,128]{1,0:T(8,128)(2,1)S(1)}, bf16[64,128]{1,0:T(8,128)(2,1)S(1)}, u32[]{:S(2)}, u32[]{:S(2)}) collective-permute-start(bf16[64,128]{1,0:T(8,128)(2,1)S(1)} %get-tuple-element.33), channel_id=1, source_target_pairs={{0,1},{1,0},{2,3},{3,2},{4,5},{5,4},{6,7},{7,6},{8,9},{9,8},{10,11... | collective-permute-start | bytes 49160 | tf_op jit(solution)/shard_map/cond/branch_1_fun/ppermute | solution.py:287
  14.2 4.6 %collective-permute-start.1 = (bf16[64,128]{1,0:T(8,128)(2,1)S(1)}, bf16[64,128]{1,0:T(8,128)(2,1)S(1)}, u32[]{:S(2)}, u32[]{:S(2)}) collective-permute-start(bf16[64,128]{1,0:T(8,128)(2,1)S(1)} %get-tuple-element.34), channel_id=1, source_target_pairs={{0,3},{1,2},{2,1},{3,0},{4,7},{5,6},{6,5},{7,4},{8,11},{9,10},{10,... | collective-permute-start | bytes 49160 | tf_op jit(solution)/shard_map/cond/branch_1_fun/ppermute | solution.py:287
  15.4 3.7 %collective-permute-start.2 = (bf16[64,128]{1,0:T(8,128)(2,1)S(1)}, bf16[64,128]{1,0:T(8,128)(2,1)S(1)}, u32[]{:S(2)}, u32[]{:S(2)}) collective-permute-start(bf16[64,128]{1,0:T(8,128)(2,1)S(1)} %get-tuple-element.35), channel_id=1, source_target_pairs={{0,2},{1,3},{2,0},{3,1},{4,6},{5,7},{6,4},{7,5},{8,10},{9,11},{10,... | collective-permute-start | bytes 49160 | tf_op jit(solution)/shard_map/cond/branch_1_fun/ppermute | solution.py:287
